TPU v7x, 32 devices: a whole 2x2x4 slice. The times are simulated.
32 devices in a mesh: clus: 8 (over y, x, core), rep: 4 (over z).
Axes of the slice: x: 2, y: 2, z: 4, core: 2. Of those that a mesh axis runs over, the one named last changes fastest.
Arguments:
- nodes: bfloat16 [65536, 2048], P(('clus', 'rep')), may hold values from -6 to 6
- weight: bfloat16 [2048, 2048], P(('clus', 'rep')), may hold values from -0.125 to 0.125
- bias: bfloat16 [2048], P(('clus', 'rep')), may hold values from -3 to 3
- neighbours: int32 [65536, 16], P(('clus', 'rep')), may hold values from 0 to 2047, as said below
- degree: int32 [65536], P(('clus', 'rep')), may hold values from 0 to 16
- counts: int32 [32], P(('clus', 'rep')), may hold values from 614 to 2048, as said below
- cotangent: bfloat16 [65536, 2048], P(('clus', 'rep')), may hold values from -6 to 6
Outputs:
- activations: bfloat16 [65536, 2048], P(('clus', 'rep'))
- nodes_grad: bfloat16 [65536, 2048], P(('clus', 'rep'))
- weight_grad: float32 [2048, 2048], P(('clus', 'rep'))
- bias_grad: float32 [2048], P(('clus', 'rep'))
Inputs may be any that keep to these rules, and one draw needn't show every extreme that they name: `counts`: one device's batch is full in every draw. `neighbours`: each entry is below its device's count.
All inputs are finite; a program needn't handle non-finite values.
Results may differ from a plain program's by a relative error of at most 0.0059.
Values may be sent and summed in bfloat16 or wider, within the bound.
No kernel may reach another device: no remote copies, remote signals or barrier semaphores. Data moves between devices by JAX's collectives and lax.ppermute only.
A program may use at most 192 MiB of HBM per device.

v0:
```python
import jax
import jax.numpy as jnp
from jax import lax
from jax.sharding import PartitionSpec as P


def body(nodes, weight, bias, neighbours, degree, counts, cotangent):
    rows = nodes.shape[0]
    fan = neighbours.shape[1]
    slots = jnp.arange(rows, dtype=jnp.int32)
    live = (slots < counts[0]).astype(jnp.float32)[:, None]
    scale = live / (degree.astype(jnp.float32)[:, None] + 1.0)

    def count_step(k, table):
        column = lax.dynamic_slice_in_dim(neighbours, k, 1, 1)
        valid = (k < degree)[:, None]
        hits = jnp.logical_and(column == slots[None, :], valid)
        return table + hits.astype(jnp.bfloat16)

    diagonal = (slots[:, None] == slots[None, :]).astype(jnp.bfloat16) * 2.0
    table = lax.fori_loop(0, fan, count_step, diagonal)
    total = jnp.dot(table, nodes, preferred_element_type=jnp.float32)
    agg = (total * scale).astype(jnp.bfloat16)
    w_piece = lax.all_gather(weight, ("clus", "rep"), axis=0, tiled=True)
    b_piece = lax.all_gather(bias, ("clus", "rep"), axis=0, tiled=True)
    acc = jnp.dot(agg, w_piece, preferred_element_type=jnp.float32)
    bias_full = b_piece.astype(jnp.float32)
    acc, bias_full = (acc, bias_full)
    pre = acc + bias_full
    sig = jax.nn.sigmoid(pre)
    activations = (live * pre * sig).astype(jnp.bfloat16)
    pre_grad = (cotangent.astype(jnp.float32) * live * sig * (1.0 + pre * (1.0 - sig))).astype(
        jnp.bfloat16
    )
    agg_grad = lax.dot_general(
        pre_grad,
        lax.all_gather(weight, ("clus", "rep"), axis=0, tiled=True),
        (((1,), (1,)), ((), ())),
        preferred_element_type=jnp.float32,
    )
    spread = agg_grad.astype(jnp.bfloat16).astype(jnp.float32) * scale
    spread_high = spread.astype(jnp.bfloat16)
    spread_low = (spread - spread_high.astype(jnp.float32)).astype(jnp.bfloat16)
    contract = (((0,), (0,)), ((), ()))
    nodes_grad = lax.dot_general(table, spread_high, contract, preferred_element_type=jnp.float32)
    nodes_grad = nodes_grad + lax.dot_general(
        table, spread_low, contract, preferred_element_type=jnp.float32
    )
    weight_term = lax.dot_general(agg, pre_grad, contract, preferred_element_type=jnp.float32)
    bias_term = jnp.sum(pre_grad.astype(jnp.float32), axis=0)
    weight_grad, bias_grad = (
        lax.psum_scatter(weight_term, ("clus", "rep"), scatter_dimension=0, tiled=True),
        lax.psum_scatter(bias_term, ("clus", "rep"), scatter_dimension=0, tiled=True),
    )
    return (activations, nodes_grad.astype(jnp.bfloat16), weight_grad, bias_grad)


def solution(mesh):
    placed = (
        P(("clus", "rep"), None),
        P(("clus", "rep"), None),
        P(("clus", "rep")),
        P(("clus", "rep"), None),
        P(("clus", "rep")),
        P(("clus", "rep")),
        P(("clus", "rep"), None),
    )
    return jax.shard_map(
        body,
        mesh=mesh,
        in_specs=placed,
        out_specs=(
            P(("clus", "rep"), None),
            P(("clus", "rep"), None),
            P(("clus", "rep"), None),
            P(("clus", "rep")),
        ),
        check_vma=False,
    )
```

profile of v0, /device:TPU:0, one launch (start us, length us, event | category | flops | bytes accessed | tf_op | source)
XLA Modules:
  0.0 680.1 jit_solution(8160456520577094073)
XLA Ops:
  12.3 162.4 %while.14 = (s32[]{:T(128)}, bf16[2048,2048]{1,0:T(8,128)(2,1)}, s32[2048,16]{0,1:T(8,128)}, s32[2048]{0:T(1024)S(1)}, s32[]{:T(128)}) while((s32[]{:T(128)}, bf16[2048,2048]{1,0:T(8,128)(2,1)}, s32[2048,16]{0,1:T(8,128)}, s32[2048]{0:T(1024)S(1)}, s32[]{:T(128)}) %tuple.44), condition=%wide.region_1.0_spmd.clone, body=%wide.region_0.0_spmd.clone.sunk | while | flops 29362176 | bytes 16814156 | solution.py:21
  13.1 9.3 %fusion.24 = bf16[2048,2048]{1,0:T(8,128)(2,1)} fusion(bf16[2048,2048]{1,0:T(8,128)(2,1)} %get-tuple-element.151, s32[2048]{0:T(1024)S(1)} %bitcast.16, pred[2048]{0:T(1024)(128)(4,1)S(1)} %broadcast_compare_fusion.2), kind=kLoop, calls=%fused_computation.4.clone.1 | loop fusion | flops 29360128 | bytes 16787456 | tf_op jit(solution)/shard_map/while/body/eval_jaxpr/add | solution.py:18
  23.3 9.3 %fusion.24 = bf16[2048,2048]{1,0:T(8,128)(2,1)} fusion(bf16[2048,2048]{1,0:T(8,128)(2,1)} %get-tuple-element.151, s32[2048]{0:T(1024)S(1)} %bitcast.16, pred[2048]{0:T(1024)(128)(4,1)S(1)} %broadcast_compare_fusion.2), kind=kLoop, calls=%fused_computation.4.clone.1 | loop fusion | flops 29360128 | bytes 16787456 | tf_op jit(solution)/shard_map/while/body/eval_jaxpr/add | solution.py:18
  33.4 9.3 %fusion.24 = bf16[2048,2048]{1,0:T(8,128)(2,1)} fusion(bf16[2048,2048]{1,0:T(8,128)(2,1)} %get-tuple-element.151, s32[2048]{0:T(1024)S(1)} %bitcast.16, pred[2048]{0:T(1024)(128)(4,1)S(1)} %broadcast_compare_fusion.2), kind=kLoop, calls=%fused_computation.4.clone.1 | loop fusion | flops 29360128 | bytes 16787456 | tf_op jit(solution)/shard_map/while/body/eval_jaxpr/add | solution.py:18
  43.6 9.3 %fusion.24 = bf16[2048,2048]{1,0:T(8,128)(2,1)} fusion(bf16[2048,2048]{1,0:T(8,128)(2,1)} %get-tuple-element.151, s32[2048]{0:T(1024)S(1)} %bitcast.16, pred[2048]{0:T(1024)(128)(4,1)S(1)} %broadcast_compare_fusion.2), kind=kLoop, calls=%fused_computation.4.clone.1 | loop fusion | flops 29360128 | bytes 16787456 | tf_op jit(solution)/shard_map/while/body/eval_jaxpr/add | solution.py:18
  53.7 9.3 %fusion.24 = bf16[2048,2048]{1,0:T(8,128)(2,1)} fusion(bf16[2048,2048]{1,0:T(8,128)(2,1)} %get-tuple-element.151, s32[2048]{0:T(1024)S(1)} %bitcast.16, pred[2048]{0:T(1024)(128)(4,1)S(1)} %broadcast_compare_fusion.2), kind=kLoop, calls=%fused_computation.4.clone.1 | loop fusion | flops 29360128 | bytes 16787456 | tf_op jit(solution)/shard_map/while/body/eval_jaxpr/add | solution.py:18
  63.9 9.3 %fusion.24 = bf16[2048,2048]{1,0:T(8,128)(2,1)} fusion(bf16[2048,2048]{1,0:T(8,128)(2,1)} %get-tuple-element.151, s32[2048]{0:T(1024)S(1)} %bitcast.16, pred[2048]{0:T(1024)(128)(4,1)S(1)} %broadcast_compare_fusion.2), kind=kLoop, calls=%fused_computation.4.clone.1 | loop fusion | flops 29360128 | bytes 16787456 | tf_op jit(solution)/shard_map/while/body/eval_jaxpr/add | solution.py:18
  74.1 9.3 %fusion.24 = bf16[2048,2048]{1,0:T(8,128)(2,1)} fusion(bf16[2048,2048]{1,0:T(8,128)(2,1)} %get-tuple-element.151, s32[2048]{0:T(1024)S(1)} %bitcast.16, pred[2048]{0:T(1024)(128)(4,1)S(1)} %broadcast_compare_fusion.2), kind=kLoop, calls=%fused_computation.4.clone.1 | loop fusion | flops 29360128 | bytes 16787456 | tf_op jit(solution)/shard_map/while/body/eval_jaxpr/add | solution.py:18
  84.2 9.4 %fusion.24 = bf16[2048,2048]{1,0:T(8,128)(2,1)} fusion(bf16[2048,2048]{1,0:T(8,128)(2,1)} %get-tuple-element.151, s32[2048]{0:T(1024)S(1)} %bitcast.16, pred[2048]{0:T(1024)(128)(4,1)S(1)} %broadcast_compare_fusion.2), kind=kLoop, calls=%fused_computation.4.clone.1 | loop fusion | flops 29360128 | bytes 16787456 | tf_op jit(solution)/shard_map/while/body/eval_jaxpr/add | solution.py:18
  94.4 9.3 %fusion.24 = bf16[2048,2048]{1,0:T(8,128)(2,1)} fusion(bf16[2048,2048]{1,0:T(8,128)(2,1)} %get-tuple-element.151, s32[2048]{0:T(1024)S(1)} %bitcast.16, pred[2048]{0:T(1024)(128)(4,1)S(1)} %broadcast_compare_fusion.2), kind=kLoop, calls=%fused_computation.4.clone.1 | loop fusion | flops 29360128 | bytes 16787456 | tf_op jit(solution)/shard_map/while/body/eval_jaxpr/add | solution.py:18
  104.5 9.3 %fusion.24 = bf16[2048,2048]{1,0:T(8,128)(2,1)} fusion(bf16[2048,2048]{1,0:T(8,128)(2,1)} %get-tuple-element.151, s32[2048]{0:T(1024)S(1)} %bitcast.16, pred[2048]{0:T(1024)(128)(4,1)S(1)} %broadcast_compare_fusion.2), kind=kLoop, calls=%fused_computation.4.clone.1 | loop fusion | flops 29360128 | bytes 16787456 | tf_op jit(solution)/shard_map/while/body/eval_jaxpr/add | solution.py:18
  114.7 9.3 %fusion.24 = bf16[2048,2048]{1,0:T(8,128)(2,1)} fusion(bf16[2048,2048]{1,0:T(8,128)(2,1)} %get-tuple-element.151, s32[2048]{0:T(1024)S(1)} %bitcast.16, pred[2048]{0:T(1024)(128)(4,1)S(1)} %broadcast_compare_fusion.2), kind=kLoop, calls=%fused_computation.4.clone.1 | loop fusion | flops 29360128 | bytes 16787456 | tf_op jit(solution)/shard_map/while/body/eval_jaxpr/add | solution.py:18
  135.0 9.3 %fusion.24 = bf16[2048,2048]{1,0:T(8,128)(2,1)} fusion(bf16[2048,2048]{1,0:T(8,128)(2,1)} %get-tuple-element.151, s32[2048]{0:T(1024)S(1)} %bitcast.16, pred[2048]{0:T(1024)(128)(4,1)S(1)} %broadcast_compare_fusion.2), kind=kLoop, calls=%fused_computation.4.clone.1 | loop fusion | flops 29360128 | bytes 16787456 | tf_op jit(solution)/shard_map/while/body/eval_jaxpr/add | solution.py:18
  145.1 9.3 %fusion.24 = bf16[2048,2048]{1,0:T(8,128)(2,1)} fusion(bf16[2048,2048]{1,0:T(8,128)(2,1)} %get-tuple-element.151, s32[2048]{0:T(1024)S(1)} %bitcast.16, pred[2048]{0:T(1024)(128)(4,1)S(1)} %broadcast_compare_fusion.2), kind=kLoop, calls=%fused_computation.4.clone.1 | loop fusion | flops 29360128 | bytes 16787456 | tf_op jit(solution)/shard_map/while/body/eval_jaxpr/add | solution.py:18
  155.2 9.3 %fusion.24 = bf16[2048,2048]{1,0:T(8,128)(2,1)} fusion(bf16[2048,2048]{1,0:T(8,128)(2,1)} %get-tuple-element.151, s32[2048]{0:T(1024)S(1)} %bitcast.16, pred[2048]{0:T(1024)(128)(4,1)S(1)} %broadcast_compare_fusion.2), kind=kLoop, calls=%fused_computation.4.clone.1 | loop fusion | flops 29360128 | bytes 16787456 | tf_op jit(solution)/shard_map/while/body/eval_jaxpr/add | solution.py:18
  175.6 42.3 %all-reduce = bf16[2048]{0:T(1024)(128)(2,1)S(1)} all-reduce(bf16[2048]{0:T(1024)(128)(2,1)S(1)} %dynamic-update-slice), channel_id=1, replica_groups=mesh['clus'=8,'rep'=4] {'clus','rep'}, use_global_device_ids=true, to_apply=%add | all-reduce | flops 2048 | bytes 8192
  217.9 23.5 %multiply_convert_fusion.2 = bf16[2048,2048]{1,0:T(8,128)(2,1)} fusion(bf16[2048,2048]{1,0:T(8,128)(2,1)} %get-tuple-element.98, bf16[2048,2048]{1,0:T(8,128)(2,1)} %param.9, f32[2048]{0:T(1024)S(1)} %add_divide_fusion.1), kind=kOutput, calls=%fused_computation.15 | convolution fusion | flops 17188257792 | bytes 25174016 | tf_op jit(solution)/shard_map/dot_general | solution.py:22
  241.4 30.8 %convert_reduce_fusion = (f32[2048]{0:T(1024)S(1)}, bf16[2048,2048]{1,0:T(8,128)(2,1)S(1)}, bf16[2048,2048]{1,0:T(8,128)(2,1)}) fusion(f32[2048]{0:T(1024)S(1)} %convert_element_type.57, f32[2048]{0:T(1024)S(1)} %fusion.11, bf16[2048,2048]{1,0:T(8,128)(2,1)} %param.15, bf16[2048,2048]{1,0:T(8,128)(2,1)} %multiply_convert_fusion.2, ...), kind=kOutput, calls=%fused_computation.7 | convolution fusion | flops 17251170304 | bytes 41967616 | tf_op jit(solution)/shard_map/dot_general | solution.py:26
  275.4 32.3 %fusion.12 = f32[2048,2048]{1,0:T(8,128)} fusion(bf16[2048,2048]{1,0:T(8,128)(2,1)} %multiply_convert_fusion.2, bf16[2048,2048]{1,0:T(8,128)(2,1)S(1)} %get-tuple-element.118), kind=kOutput, calls=%fused_computation.25 | convolution fusion | flops 17179869184 | bytes 33554432 | tf_op jit(solution)/shard_map/dot_general | solution.py:49
  307.7 44.5 %all-reduce.1 = f32[2048]{0:T(1024)S(1)} all-reduce(f32[2048]{0:T(1024)S(1)} %get-tuple-element.117), channel_id=3, replica_groups=mesh['clus'=8,'rep'=4] {'clus','rep'}, use_global_device_ids=true, to_apply=%region_4.0.clone | all-reduce | flops 2048 | bytes 16384
  352.8 22.4 %convolution_convert_fusion = bf16[2048,2048]{1,0:T(8,128)(2,1)S(1)} fusion(bf16[2048,2048]{1,0:T(8,128)(2,1)} %copy-done.2, bf16[2048,2048]{1,0:T(8,128)(2,1)} %all-gather.2.cloned.1.call-done), kind=kOutput, calls=%fused_computation.21 | convolution fusion | flops 17184063488 | bytes 25165824 | tf_op jit(solution)/shard_map/dot_general | solution.py:35
  378.4 23.3 %fusion.7 = f32[2048,2048]{1,0:T(8,128)} fusion(bf16[2048,2048]{1,0:T(8,128)(2,1)} %get-tuple-element.98, bf16[2048,2048]{1,0:T(8,128)(2,1)S(1)} %convolution_convert_fusion, f32[2048]{0:T(1024)S(1)} %add_divide_fusion.1), kind=kOutput, calls=%fused_computation.18 | convolution fusion | flops 17192452096 | bytes 33562624 | tf_op jit(solution)/shard_map/dot_general | solution.py:45
  401.7 27.7 %add_convert_fusion = bf16[2048,2048]{1,0:T(8,128)(2,1)} fusion(f32[2048,2048]{1,0:T(8,128)} %fusion.7, bf16[2048,2048]{1,0:T(8,128)(2,1)} %get-tuple-element.98, bf16[2048,2048]{1,0:T(8,128)(2,1)} %copy-done.3, f32[2048]{0:T(1024)S(1)} %add_divide_fusion.1), kind=kOutput, calls=%fused_computation.8 | convolution fusion | flops 17213423616 | bytes 41951232 | tf_op jit(solution)/shard_map/dot_general | solution.py:46
  429.4 243.6 %reduce-scatter.2.cloned.1.call-done = f32[64,2048]{1,0:T(8,128)} async-done(((f32[2048,2048]{1,0:T(8,128)}), f32[64,2048]{1,0:T(8,128)}) %reduce-scatter.2.cloned.1.call-update) | async-done | bytes 524304 | tf_op jit(solution)/shard_map/reduce_scatter | solution.py:52
  (54 shorter events, 44.6 us)
Async XLA Ops:
  7.2 5.1 copy-start
  7.2 234.2 %all-gather.2.cloned.1.call-start = ((), (), s32[]{:S(2)}) async-start(), calls=%async_computation.1 | async-start | bytes 8650752 | tf_op jit(solution)/shard_map/all_gather | solution.py:24
  7.9 665.1 %reduce-scatter.2.cloned.1.call-start = ((), (), s32[]{:S(2)}) async-start(), calls=%async_computation.2 | async-start | bytes 17301504 | tf_op jit(solution)/shard_map/reduce_scatter | solution.py:52
  12.3 163.1 %copy-start.1 = (bf16[64]{0:T(256)(128)(2,1)S(1)}, bf16[64]{0:T(256)(128)(2,1)}, u32[]{:S(2)}) copy-start(bf16[64]{0:T(256)(128)(2,1)} %param.11) | copy-start | bytes 388
  272.2 3.2 copy-start.2
  375.2 3.2 copy-start.3
Sparse Core Ops, SparseCore 0:
  10.9 80.0 all-gather.1
  307.8 365.1 reduce-scatter.1
where the time goes:
time: 679 us; the launch traced here: 680 us
  waiting for transfers between devices  244 us (36%)
  matrix products  160 us (24%)
  other arithmetic  153 us (23%)
  blocking collectives  86.8 us (13%)
  local copies, waits for them, and re-layouts  20.8 us (3%)
  between operations  15 us (2%)
    reduce_scatter x1, waiting for transfers between devices, body(): lax.psum_scatter(weight_term, ('clus', 'rep'), scatter_dimension=0, tiled...  244 us
    add x16, other arithmetic, count_step(): return table + hits.astype(jnp.bfloat16)  149 us
    unnamed x2, blocking collectives  86.8 us
    dot_general x1, matrix products, body(): lax.dot_general(agg, pre_grad, contract, preferred_element_type=jnp.float32)  32.3 us
    dot_general x1, matrix products, body(): acc = jnp.dot(agg, w_piece, preferred_element_type=jnp.float32)  30.8 us
    dot_general x1, matrix products, body(): lax.dot_general(table, spread_low, contract, preferred_element_type=jnp.f...  27.7 us
    dot_general x1, matrix products, body(): total = jnp.dot(table, nodes, preferred_element_type=jnp.float32)  23.5 us
    dot_general x1, matrix products, body(): lax.dot_general(table, spread_high, contract, preferred_element_type=jnp....  23.3 us
  transfers between devices with their start and end apart: 2, of which 1 were waited for; matrix products, arithmetic and copies ran while one was open for 39% of the time, Pallas kernels for 0%

commit v1 on v0

v1 whole, which is shorter than its diff:
```python
import functools

import jax
import jax.numpy as jnp
from jax import lax
from jax.experimental import pallas as pl
from jax.experimental.pallas import tpu as pltpu
from jax.sharding import PartitionSpec as P

AXES = ("clus", "rep")
MIB = 2**20
F32 = jnp.float32
BF16 = jnp.bfloat16
Z1, Z2, CORE, X, Y = 1, 2, 4, 8, 16
ANY = pl.BlockSpec(memory_space=pl.ANY)
SMEM = pl.BlockSpec(memory_space=pltpu.SMEM)


def params(mib=48):
    return pltpu.CompilerParams(vmem_limit_bytes=mib * MIB)


def cost(flops, nbytes):
    return pl.CostEstimate(flops=flops, bytes_accessed=nbytes, transcendentals=0)


def column(row):
    return jnp.transpose(jnp.broadcast_to(row, (8, row.shape[1])))[:, :1]


def scale_row(start, degree, count):
    slots = start + lax.broadcasted_iota(jnp.int32, degree.shape, 1)
    live = (slots < count).astype(F32)
    return live / (degree.astype(F32) + 1.0)


def table_agg_kernel(count, nb, deg, nodes, table, agg):
    step = pl.program_id(0)
    n = nodes.shape[0]
    fan, tile = nb.shape
    degree = deg[...]
    start = step * tile
    chunk = 256
    used = lax.broadcasted_iota(jnp.int32, (fan, tile), 0) < degree
    slots = jnp.where(used, nb[...], -1)
    targets = lax.broadcasted_iota(jnp.int32, (chunk, tile), 0).astype(F32).astype(BF16)
    own = start + lax.broadcasted_iota(jnp.int32, (1, tile), 1)

    def local(rows, base):
        off = rows - base
        off = jnp.where(jnp.logical_and(off >= 0, off < chunk), off, -1)
        return off.astype(F32).astype(BF16)

    def build(c, carry):
        base = c * chunk
        here = local(slots, base)
        mine = local(own, base)
        one = jnp.ones((), BF16)
        zero = jnp.zeros((), BF16)
        acc = jnp.where(targets == mine, one + one, zero)
        for k in range(fan):
            acc = acc + jnp.where(targets == here[k : k + 1, :], one, zero)
        table[pl.ds(pl.multiple_of(base, chunk), chunk), :] = acc
        return carry

    lax.fori_loop(0, n // chunk, build, 0)
    total = lax.dot_general(table[...], nodes[...], (((0,), (0,)), ((), ())), preferred_element_type=F32)
    agg[...] = (total * column(scale_row(start, degree, count[0]))).astype(BF16)


def table_agg(count, nb, deg, nodes):
    n, d = nodes.shape
    fan = nb.shape[0]
    tile = 256
    return pl.pallas_call(
        table_agg_kernel,
        grid=(n // tile,),
        in_specs=[
            SMEM,
            pl.BlockSpec((fan, tile), lambda t: (0, t)),
            pl.BlockSpec((1, tile), lambda t: (0, t)),
            pl.BlockSpec((n, d), lambda t: (0, 0)),
        ],
        out_specs=[pl.BlockSpec((n, tile), lambda t: (0, t)), pl.BlockSpec((tile, d), lambda t: (t, 0))],
        out_shape=[jax.ShapeDtypeStruct((n, n), BF16), jax.ShapeDtypeStruct((n, d), BF16)],
        compiler_params=params(),
        cost_estimate=cost(3 * n * n * d, 3 * n * n * 2),
        name="table_agg",
    )(count, nb, deg, nodes)


def forward_kernel(count, agg, weight, bias, cot, act, grad, bias_sum):
    step = pl.program_id(0)
    tile = agg.shape[0]
    pre = jnp.dot(agg[...], weight[...], preferred_element_type=F32) + bias[...]
    slots = step * tile + lax.broadcasted_iota(jnp.int32, (tile, 1), 0)
    live = (slots < count[0]).astype(F32)
    sig = jax.nn.sigmoid(pre)
    act[...] = (live * pre * sig).astype(BF16)
    out = (cot[...].astype(F32) * live * sig * (1.0 + pre * (1.0 - sig))).astype(BF16)
    grad[...] = out
    part = jnp.sum(out.astype(F32), axis=0, keepdims=True)

    @pl.when(step == 0)
    def _():
        bias_sum[...] = part

    @pl.when(step > 0)
    def _():
        bias_sum[...] += part


def forward(count, agg, weight, bias, cot):
    n, d = agg.shape
    m = weight.shape[1]
    tile = 256
    row = pl.BlockSpec((tile, m), lambda t: (t, 0))
    return pl.pallas_call(
        forward_kernel,
        grid=(n // tile,),
        in_specs=[
            SMEM,
            pl.BlockSpec((tile, d), lambda t: (t, 0)),
            pl.BlockSpec((d, m), lambda t: (0, 0)),
            pl.BlockSpec((1, m), lambda t: (0, 0)),
            row,
        ],
        out_specs=[row, row, pl.BlockSpec((1, m), lambda t: (0, 0))],
        out_shape=[
            jax.ShapeDtypeStruct((n, m), BF16),
            jax.ShapeDtypeStruct((n, m), BF16),
            jax.ShapeDtypeStruct((1, m), F32),
        ],
        compiler_params=params(),
        cost_estimate=cost(2 * n * d * m, 5 * n * m * 2),
        name="forward",
    )(count, agg, weight, bias, cot)


def spread_rows(me, out, value):
    rows = value.shape[0] // 4
    z = lax.rem(me, 4)
    for q in range(4):
        place = pl.multiple_of(lax.bitwise_xor(z, q) * rows, rows)
        out[pl.ds(place, rows), :] = value[q * rows : (q + 1) * rows, :]


TN = (((0,), (0,)), ((), ()))


def wgrad_send_kernel(me, agg, grad, out):
    value = lax.dot_general(agg[...], grad[...], TN, preferred_element_type=F32)
    spread_rows(me[0], out.at[0], value.astype(BF16))


def wgrad_send(me, agg, grad):
    n, d = agg.shape
    m = grad.shape[1]
    tile = d // 8
    return pl.pallas_call(
        wgrad_send_kernel,
        grid_spec=pltpu.PrefetchScalarGridSpec(
            num_scalar_prefetch=1,
            grid=(4,),
            in_specs=[
                pl.BlockSpec((n, tile), lambda t, me: (0, (me[0] // 4) ^ (2 * t + 1))),
                pl.BlockSpec((n, m), lambda t, me: (0, 0)),
            ],
            out_specs=pl.BlockSpec((1, tile, m), lambda t, me: (t, 0, 0)),
        ),
        out_shape=jax.ShapeDtypeStruct((4, tile, m), BF16),
        compiler_params=params(),
        cost_estimate=cost(n * d * m, 2 * n * m * 2),
        name="wgrad_send",
    )(me, agg, grad)


def wgrad_keep_kernel(me, agg, grad, got, send_p, keep_p, send_q, keep_q, acc):
    t = pl.program_id(0)
    half = got.shape[2] // 2
    value = lax.dot_general(agg[...], grad[...], TN, preferred_element_type=F32)
    spread_rows(me[0], acc, value)
    for step in range(4):
        ry, rx = step // 2, step % 2

        @pl.when(t == step)
        def _():
            p = acc[:, :half] + got[0, :, :half].astype(F32)
            q = acc[:, half:] + got[0, :, half:].astype(F32)
            if ry:
                send_p[rx, :, :] = p.astype(BF16)
            else:
                keep_p[rx, :, :] = p
            if rx:
                send_q[ry, :, :] = q.astype(BF16)
            else:
                keep_q[ry, :, :] = q


def wgrad_keep(me, agg, grad, got):
    n, d = agg.shape
    m = grad.shape[1]
    tile = d // 8
    whole = pl.BlockSpec((2, tile, m // 2), lambda t, me: (0, 0, 0))
    low = jax.ShapeDtypeStruct((2, tile, m // 2), BF16)
    wide = jax.ShapeDtypeStruct((2, tile, m // 2), F32)
    return pl.pallas_call(
        wgrad_keep_kernel,
        grid_spec=pltpu.PrefetchScalarGridSpec(
            num_scalar_prefetch=1,
            grid=(4,),
            in_specs=[
                pl.BlockSpec((n, tile), lambda t, me: (0, (me[0] // 4) ^ (2 * t))),
                pl.BlockSpec((n, m), lambda t, me: (0, 0)),
                pl.BlockSpec((1, tile, m), lambda t, me: (t, 0, 0)),
            ],
            out_specs=[whole] * 4,
            scratch_shapes=[pltpu.VMEM((tile, m), F32)],
        ),
        out_shape=[low, wide, low, wide],
        compiler_params=params(),
        cost_estimate=cost(n * d * m, 3 * n * m * 2),
        name="wgrad_keep",
    )(me, agg, grad, got)


def agg_grad_kernel(first, count, deg, grad, weight, out):
    tile = grad.shape[0]
    value = lax.dot_general(grad[...], weight[...], (((1,), (1,)), ((), ())), preferred_element_type=F32)
    start = (pl.program_id(0) + first) * tile
    out[...] = (value * column(scale_row(start, deg[...], count[0]))).astype(BF16)


def agg_grad(count, deg, grad, weight, first, steps):
    m = grad.shape[1]
    d = weight.shape[0]
    tile = 256
    return pl.pallas_call(
        functools.partial(agg_grad_kernel, first),
        grid=(steps,),
        in_specs=[
            SMEM,
            pl.BlockSpec((1, tile), lambda t: (0, t + first)),
            pl.BlockSpec((tile, m), lambda t: (t + first, 0)),
            pl.BlockSpec((d, m), lambda t: (0, 0)),
        ],
        out_specs=pl.BlockSpec((tile, d), lambda t: (t, 0)),
        out_shape=jax.ShapeDtypeStruct((steps * tile, d), BF16),
        compiler_params=params(),
        cost_estimate=cost(2 * steps * tile * d * m, (d + 2 * steps * tile) * m * 2),
        name="agg_grad",
    )(count, deg, grad, weight)


def nodes_grad_kernel(table, low, high, *rest):
    out = rest[-1]
    half = low.shape[0]
    value = jnp.dot(table[:, :half], low[...], preferred_element_type=F32)
    value = value + jnp.dot(table[:, half:], high[...], preferred_element_type=F32)
    out[...] = value.astype(BF16)


def nodes_grad(table, low, high, first, steps, into=None):
    n = table.shape[0]
    d = low.shape[1]
    tile = 256
    whole = pl.BlockSpec(low.shape, lambda t: (0, 0))
    extra = [] if into is None else [into]
    return pl.pallas_call(
        nodes_grad_kernel,
        grid=(steps,),
        in_specs=[pl.BlockSpec((tile, n), lambda t: (t + first, 0)), whole, whole] + [ANY] * len(extra),
        out_specs=pl.BlockSpec((tile, d), lambda t: (t + first, 0)),
        out_shape=jax.ShapeDtypeStruct((n, d), BF16),
        input_output_aliases={3: 0} if extra else {},
        compiler_params=params(),
        cost_estimate=cost(2 * steps * tile * d * n, (n + 2 * steps * tile) * d * 2),
        name="nodes_grad",
    )(table, low, high, *extra)


def swap(value, bit):
    return lax.ppermute(value, AXES, [(i, i ^ bit) for i in range(32)])


def place_kernel(codes, me, *refs):
    pieces, out, sem = refs[:-2], refs[-2], refs[-1]
    copies = []
    for (order, col), piece in zip(codes, pieces):
        rows = piece.shape[0] // len(order)
        for i, code in enumerate(order):
            at = pl.multiple_of(lax.bitwise_xor(me[0], code) * rows, rows)
            copies.append(
                pltpu.make_async_copy(
                    piece.at[pl.ds(i * rows, rows), :],
                    out.at[pl.ds(at, rows), pl.ds(col, piece.shape[1])],
                    sem.at[len(copies)],
                )
            )
    for c in copies:
        c.start()
    for c in copies:
        c.wait()


def place(me, pieces, codes, shape):
    total = sum(len(order) for order, _ in codes)
    return pl.pallas_call(
        functools.partial(place_kernel, codes),
        in_specs=[SMEM] + [ANY] * len(pieces),
        out_specs=ANY,
        out_shape=jax.ShapeDtypeStruct(shape, pieces[0].dtype),
        scratch_shapes=[pltpu.SemaphoreType.DMA((total,))],
        compiler_params=params(8),
        cost_estimate=cost(0, 4 * shape[0] * shape[1]),
        name="place",
    )(me, *pieces)


def gather_z(block):
    one, two = swap(block, Z1), swap(block, Z2)
    return jnp.concatenate([block, one, two, swap(two, Z1)], axis=0)


def gather(block, bit):
    return jnp.concatenate([block, swap(block, bit)], axis=0)


def codes_of(*bits):
    order = [0]
    for group in bits:
        order = [code ^ g for g in group for code in order]
    return order


ZS = (0, Z1, Z2, Z1 ^ Z2)


def gather_weight(me, weight):
    half = weight.shape[1] // 2
    p = gather_z(gather(gather(weight[:, :half], X), Y))
    q = gather(gather(gather_z(weight[:, half:]), X), Y)
    order_p = codes_of((0, X), (0, Y), ZS)
    order_q = codes_of(ZS, (0, X), (0, Y))
    codes = (
        (order_p, 0),
        ([c ^ CORE for c in order_p], 0),
        (order_q, half),
        ([c ^ CORE for c in order_q], half),
    )
    rows = 32 * weight.shape[0]
    return place(me, (p, swap(p, CORE), q, swap(q, CORE)), codes, (rows, 2 * half))


def gather_bias(me, bias):
    block = bias[None, :]
    for bit in (CORE, X, Y, Z2, Z1):
        block = gather(block, bit)
    order = jnp.array(codes_of((0, CORE), (0, X), (0, Y), (0, Z2), (0, Z1)), jnp.int32)
    inverse = jnp.argsort(order) if False else order
    del inverse
    position = [0] * 32
    for i, code in enumerate(codes_of((0, CORE), (0, X), (0, Y), (0, Z2), (0, Z1))):
        position[code] = i
    wanted = jnp.bitwise_xor(jnp.arange(32, dtype=jnp.int32), me[0])
    return block[jnp.array(position, jnp.int32)[wanted]].reshape(1, -1)


def scatter_weight(send_p, keep_p, send_q, keep_q, rows):
    got_p, got_q = swap(send_p, Y), swap(send_q, X)
    next_p = (keep_p[1] + got_p[1].astype(F32)).astype(BF16)
    next_q = (keep_q[1] + got_q[1].astype(F32)).astype(BF16)
    got2_p, got2_q = swap(next_p, X), swap(next_q, Y)
    p = keep_p[0] + got_p[0].astype(F32) + got2_p.astype(F32)
    q = keep_q[0] + got_q[0].astype(F32) + got2_q.astype(F32)

    def piece(i):
        return jnp.concatenate([p[i * rows : (i + 1) * rows], q[i * rows : (i + 1) * rows]], axis=1)

    far = swap(piece(3).astype(BF16), Z1)
    near = swap(piece(1).astype(BF16), Z1)
    mid = swap((piece(2) + far.astype(F32)).astype(BF16), Z2)
    return piece(0) + near.astype(F32) + mid.astype(F32)


def sum_bias(me, part, rows):
    for bit in (CORE, X, Y, Z2, Z1):
        part = part + swap(part, bit)
    return lax.dynamic_slice_in_dim(part[0], me[0] * rows, rows, 0)


def fast(nodes, weight, bias, neighbours, degree, counts, cotangent):
    me = (lax.axis_index("clus") * 4 + lax.axis_index("rep")).astype(jnp.int32)[None]
    rows = weight.shape[0]
    nb = neighbours.T
    deg = degree[None, :]
    full = gather_weight(me, weight)
    bias_full = gather_bias(me, bias).astype(F32)
    table, agg = table_agg(counts, nb, deg, nodes)
    act, grad, bias_part = forward(counts, agg, full, bias_full, cotangent)
    terms = wgrad_send(me, agg, grad)
    got = swap(terms, CORE)
    steps = nodes.shape[0] // 512
    low = agg_grad(counts, deg, grad, full, 0, steps)
    parts = wgrad_keep(me, agg, grad, got)
    high = agg_grad(counts, deg, grad, full, steps, steps)
    weight_grad = scatter_weight(*parts, rows)
    bias_grad = sum_bias(me, bias_part, rows)
    first = nodes_grad(table, low, high, 0, steps)
    out = nodes_grad(table, low, high, steps, steps, first)
    return act, out, weight_grad, bias_grad


def general(nodes, weight, bias, neighbours, degree, counts, cotangent):
    nb = neighbours.T
    deg = degree[None, :]
    full = lax.all_gather(weight, AXES, axis=0, tiled=True)
    bias_full = lax.all_gather(bias, AXES, axis=0, tiled=True).astype(F32)[None, :]
    table, agg = table_agg(counts, nb, deg, nodes)
    act, grad, bias_part = forward(counts, agg, full, bias_full, cotangent)
    term = lax.dot_general(agg, grad, TN, preferred_element_type=F32)
    weight_grad = lax.psum_scatter(term, AXES, scatter_dimension=0, tiled=True)
    bias_grad = lax.psum_scatter(bias_part[0], AXES, scatter_dimension=0, tiled=True)
    steps = nodes.shape[0] // 512
    low = agg_grad(counts, deg, grad, full, 0, steps)
    high = agg_grad(counts, deg, grad, full, steps, steps)
    first = nodes_grad(table, low, high, 0, steps)
    out = nodes_grad(table, low, high, steps, steps, first)
    return act, out, weight_grad, bias_grad


def solution(mesh):
    both = P(AXES, None)
    one = P(AXES)
    cube = (mesh.shape["clus"], mesh.shape["rep"]) == (8, 4)
    return jax.shard_map(
        fast if cube else general,
        mesh=mesh,
        in_specs=(both, both, one, both, one, one, both),
        out_specs=(both, both, both, one),
        check_vma=False,
    )
```

time: 679 us -> 286 us (0.42)
  waiting for transfers between devices: 244 us -> 70.4 us
  matrix products: 160 us -> 0 us
  Pallas kernels: 0 us -> 156 us
  other arithmetic: 153 us -> 2.5 us
  blocking collectives: 86.8 us -> 0 us
  starting transfers between devices: 0.08 us -> 42.4 us
  between operations: 15 us -> 1.57 us
  local copies, waits for them, and re-layouts: 20.8 us -> 12.8 us
    reduce_scatter x1 -> x0, waiting for transfers between devices: 244 us -> none  [body(): lax.psum_scatter(weight_term, ('clus', 'rep'), scatter_dimension=0, tiled...]
    dot_general x6 -> x0, matrix products: 160 us -> none  [the longest x1 32.3 us: body(): lax.dot_general(agg, pre_grad, contract, preferred_element_type=jnp.float32)]
    pallas_call x0 -> x9, Pallas kernels: none -> 156 us  [the longest x1 38.7 us: table_agg(): pl.pallas_call(table_agg_kernel, grid=(n // tile,), in_specs=[SMEM, pl.Bl...]
    add x16 -> x5, other arithmetic: 149 us -> 0.91 us  [the longest x1 0.87 us: scatter_weight(): return piece(0) + near.astype(F32) + mid.astype(F32)]
    unnamed x2 -> x0, blocking collectives: 86.8 us -> none
    ppermute x0 -> x30, waiting for transfers between devices: none -> 70.4 us  [swap(): return lax.ppermute(value, AXES, [(i, i ^ bit) for i in range(32)])]
    ppermute x0 -> x30, starting transfers between devices: none -> 42.4 us  [swap(): return lax.ppermute(value, AXES, [(i, i ^ bit) for i in range(32)])]
    dynamic_slice x16 -> x0, local copies, waits for them, and re-layouts: 13.6 us -> none  [count_step(): column = lax.dynamic_slice_in_dim(neighbours, k, 1, 1)]
  transfers between devices with their start and end apart: 2 -> 30, of which waited for: 1 -> 15; matrix products, arithmetic and copies ran while one was open for 39% -> 3% of each run, Pallas kernels for 0% -> 37%
where the time goes in v1:
time: 286 us; the launch traced here: 285 us
  Pallas kernels  156 us (55%)
  waiting for transfers between devices  70.4 us (25%)
  starting transfers between devices  42.4 us (15%)
  local copies, waits for them, and re-layouts  12.8 us (4%)
    ppermute x30, waiting for transfers between devices, swap(): return lax.ppermute(value, AXES, [(i, i ^ bit) for i in range(32)])  70.4 us
    ppermute x30, starting transfers between devices, swap(): return lax.ppermute(value, AXES, [(i, i ^ bit) for i in range(32)])  42.4 us
    pallas_call x1, Pallas kernels, table_agg(): pl.pallas_call(table_agg_kernel, grid=(n // tile,), in_specs=[SMEM, pl.Bl...  38.7 us
    pallas_call x1, Pallas kernels, forward(): pl.pallas_call(forward_kernel, grid=(n // tile,), in_specs=[SMEM, pl.Bloc...  30.8 us
    pallas_call x2, Pallas kernels, agg_grad(): pl.pallas_call(functools.partial(agg_grad_kernel, first), grid=(steps,),...  26.5 us
    pallas_call x2, Pallas kernels, nodes_grad(): pl.pallas_call(nodes_grad_kernel, grid=(steps,), in_specs=[pl.BlockSpec((...  25.7 us
    pallas_call x1, Pallas kernels, wgrad_keep(): pl.pallas_call(wgrad_keep_kernel, grid_spec=pltpu.PrefetchScalarGridSpec(...  15.8 us
    pallas_call x1, Pallas kernels, wgrad_send(): pl.pallas_call(wgrad_send_kernel, grid_spec=pltpu.PrefetchScalarGridSpec(...  14.3 us
  transfers between devices with their start and end apart: 30, of which 15 were waited for; matrix products, arithmetic and copies ran while one was open for 3% of the time, Pallas kernels for 37%

profile of v1, /device:TPU:0, one launch (start us, length us, event | category | flops | bytes accessed | tf_op | source)
XLA Modules:
  0.0 285.3 jit_solution(17701229715585539816)
XLA Ops:
  2.3 4.0 %collective-permute-start.7 = (bf16[64,1024]{1,0:T(8,128)(2,1)S(1)}, bf16[64,1024]{1,0:T(8,128)(2,1)S(1)}, u32[]{:S(2)}, u32[]{:S(2)}) collective-permute-start(bf16[64,1024]{1,0:T(8,128)(2,1)S(1)} %get-tuple-element.39), channel_id=1, source_target_pairs={{0,2},{1,3},{2,0},{3,1},{4,6},{5,7},{6,4},{7,5},{8,10},{9,11},{10,... | collective-permute-start | bytes 393224 | tf_op jit(solution)/shard_map/ppermute | solution.py:283
  7.9 4.8 %collective-permute-done.7 = bf16[64,1024]{1,0:T(8,128)(2,1)S(1)} collective-permute-done((bf16[64,1024]{1,0:T(8,128)(2,1)S(1)}, bf16[64,1024]{1,0:T(8,128)(2,1)S(1)}, u32[]{:S(2)}, u32[]{:S(2)}) %collective-permute-start.7) | collective-permute-done | bytes 131104 | tf_op jit(solution)/shard_map/ppermute | solution.py:283
  14.9 2.9 %collective-permute-done.8 = bf16[64,1024]{1,0:T(8,128)(2,1)S(1)} collective-permute-done((bf16[64,1024]{1,0:T(8,128)(2,1)S(1)}, bf16[64,1024]{1,0:T(8,128)(2,1)S(1)}, u32[]{:S(2)}, u32[]{:S(2)}) %collective-permute-start.8) | collective-permute-done | bytes 131104 | tf_op jit(solution)/shard_map/ppermute | solution.py:283
  23.1 2.8 collective-permute-done.1
  25.9 3.8 %collective-permute-start.3 = (bf16[256,1024]{1,0:T(8,128)(2,1)S(1)}, bf16[256,1024]{1,0:T(8,128)(2,1)S(1)}, u32[]{:S(2)}, u32[]{:S(2)}) collective-permute-start(bf16[256,1024]{1,0:T(8,128)(2,1)S(1)} %pad_maximum_fusion), channel_id=1, source_target_pairs={{0,2},{1,3},{2,0},{3,1},{4,6},{5,7},{6,4},{7,5},{8,10},{9,11},{10,... | collective-permute-start | bytes 1572872 | tf_op jit(solution)/shard_map/ppermute | solution.py:283
  34.4 17.0 %collective-permute-done.3 = bf16[256,1024]{1,0:T(8,128)(2,1)S(1)} collective-permute-done((bf16[256,1024]{1,0:T(8,128)(2,1)S(1)}, bf16[256,1024]{1,0:T(8,128)(2,1)S(1)}, u32[]{:S(2)}, u32[]{:S(2)}) %collective-permute-start.3) | collective-permute-done | bytes 524320 | tf_op jit(solution)/shard_map/ppermute | solution.py:283
  52.4 4.3 %collective-permute-done.2 = bf16[256,1024]{1,0:T(8,128)(2,1)S(1)} collective-permute-done((bf16[256,1024]{1,0:T(8,128)(2,1)S(1)}, bf16[256,1024]{1,0:T(8,128)(2,1)S(1)}, u32[]{:S(2)}, u32[]{:S(2)}) %collective-permute-start.2) | collective-permute-done | bytes 524320 | tf_op jit(solution)/shard_map/ppermute | solution.py:283
  56.8 9.5 %collective-permute-done.4 = bf16[256,1024]{1,0:T(8,128)(2,1)S(1)} collective-permute-done((bf16[256,1024]{1,0:T(8,128)(2,1)S(1)}, bf16[256,1024]{1,0:T(8,128)(2,1)S(1)}, u32[]{:S(2)}, u32[]{:S(2)}) %collective-permute-start.4) | collective-permute-done | bytes 524320 | tf_op jit(solution)/shard_map/ppermute | solution.py:283
  67.9 38.7 %table_agg.1 = (bf16[2048,2048]{1,0:T(8,128)(2,1)}, bf16[2048,2048]{1,0:T(8,128)(2,1)}) custom-call(s32[1]{0:T(128)S(6)} %copy.28.count, s32[16,2048]{1,0:T(8,128)S(1)} %bitcast.22, s32[1,2048]{1,0:T(1,128)S(1)} %bitcast.23, bf16[2048,2048]{1,0:T(8,128)(2,1)} %nodes.1), custom_call_target="tpu_custom_call" | custom-call | flops 25769803776 | bytes 25165824 | tf_op jit(solution)/shard_map/table_agg/pallas_call | solution.py:75
  114.0 2.9 %collective-permute-start.15 = (bf16[8,64]{1,0:T(8,128)(2,1)S(1)}, bf16[8,64]{1,0:T(8,128)(2,1)S(1)}, u32[]{:S(2)}, u32[]{:S(2)}) collective-permute-start(bf16[8,64]{1,0:T(8,128)(2,1)S(1)} %pad_maximum_fusion.5), channel_id=1, source_target_pairs={{0,2},{1,3},{2,0},{3,1},{4,6},{5,7},{6,4},{7,5},{8,10},{9,11},{10,... | collective-permute-start | bytes 3080 | tf_op jit(solution)/shard_map/ppermute | solution.py:283
  118.5 2.4 collective-permute-start.16
  123.3 3.8 %place.1.weight = bf16[2048,2048]{1,0:T(8,128)(2,1)S(1)} custom-call(s32[1]{0:T(128)} %bitcast.2.me, bf16[1024,1024]{1,0:T(8,128)(2,1)S(1)} %constant_dynamic-update-slice_fusion.refs_0_, bf16[1024,1024]{1,0:T(8,128)(2,1)} %collective-permute-done.5.refs_1_, bf16[1024,1024]{1,0:T(8,128)(2,1)} %constant_dynamic-update-slice_fusion.11.refs_2_, ...), custom_call_target="tpu_custom_call" | custom-call | bytes 16777216 | tf_op jit(solution)/shard_map/place/pallas_call | solution.py:308
  127.2 3.2 %copy-done = bf16[2048,2048]{1,0:T(8,128)(2,1)} copy-done((bf16[2048,2048]{1,0:T(8,128)(2,1)}, bf16[2048,2048]{1,0:T(8,128)(2,1)S(1)}, u32[]{:S(2)}) %copy-start) | copy-done | bytes 8388632
  130.4 30.8 %forward.1 = (bf16[2048,2048]{1,0:T(8,128)(2,1)}, bf16[2048,2048]{1,0:T(8,128)(2,1)}, f32[1,2048]{1,0:T(1,128)S(1)}) custom-call(s32[1]{0:T(128)S(6)} %copy.28.count, bf16[2048,2048]{1,0:T(8,128)(2,1)} %get-tuple-element.13.agg, bf16[2048,2048]{1,0:T(8,128)(2,1)} %copy-done, f32[1,2048]{1,0:T(1,128)S(1)} %reshape.63.bias, bf16[2048,2048]{1,0:T(8,128)(2,1)} %cot.1), custom_call_target="tpu_custom_call" | custom-call | flops 17179869184 | bytes 41943040 | tf_op jit(solution)/shard_map/forward/pallas_call | solution.py:118
  161.2 14.3 %wgrad_send.1 = bf16[4,256,2048]{2,1,0:T(8,128)(2,1)} custom-call(s32[1]{0:T(128)} %bitcast.2.me, bf16[2048,2048]{1,0:T(8,128)(2,1)} %get-tuple-element.13.agg, bf16[2048,2048]{1,0:T(8,128)(2,1)} %get-tuple-element.16.grad), custom_call_target="tpu_custom_call" | custom-call | flops 8589934592 | bytes 16777216 | tf_op jit(solution)/shard_map/wgrad_send/pallas_call | solution.py:160
  176.0 5.4 %collective-permute-done.25 = f32[1,2048]{1,0:T(1,128)S(1)} collective-permute-done((f32[1,2048]{1,0:T(1,128)S(1)}, f32[1,2048]{1,0:T(1,128)S(1)}, u32[]{:S(2)}, u32[]{:S(2)}) %collective-permute-start.25) | collective-permute-done | bytes 8224 | tf_op jit(solution)/shard_map/ppermute | solution.py:283
  183.0 15.8 %wgrad_keep.1 = (bf16[2,256,1024]{2,1,0:T(8,128)(2,1)S(1)}, f32[2,256,1024]{2,1,0:T(8,128)S(1)}, bf16[2,256,1024]{2,1,0:T(8,128)(2,1)S(1)}, f32[2,256,1024]{2,1,0:T(8,128)}) custom-call(s32[1]{0:T(128)} %bitcast.2.me, bf16[2048,2048]{1,0:T(8,128)(2,1)} %get-tuple-element.13.agg, bf16[2048,2048]{1,0:T(8,128)(2,1)} %get-tuple-element.16.grad, ...), custom_call_target="tpu_custom_call" | custom-call | flops 8589934592 | bytes 25165824 | tf_op jit(solution)/shard_map/wgrad_keep/pallas_call | solution.py:207
  199.4 13.2 %agg_grad.3.high = bf16[1024,2048]{1,0:T(8,128)(2,1)S(1)} custom-call(s32[1]{0:T(128)S(6)} %copy.28.count, s32[1,2048]{1,0:T(1,128)S(1)} %bitcast.24, bf16[2048,2048]{1,0:T(8,128)(2,1)} %get-tuple-element.16.grad, bf16[2048,2048]{1,0:T(8,128)(2,1)} %copy-done), custom_call_target="tpu_custom_call" | custom-call | flops 8589934592 | bytes 16777216 | tf_op jit(solution)/shard_map/agg_grad/pallas_call | solution.py:238
  217.7 13.2 %agg_grad.2.low = bf16[1024,2048]{1,0:T(8,128)(2,1)S(1)} custom-call(s32[1]{0:T(128)S(6)} %copy.28.count, s32[1,2048]{1,0:T(1,128)S(1)} %bitcast.25, bf16[2048,2048]{1,0:T(8,128)(2,1)} %get-tuple-element.16.grad, bf16[2048,2048]{1,0:T(8,128)(2,1)} %copy-done), custom_call_target="tpu_custom_call" | custom-call | flops 8589934592 | bytes 16777216 | tf_op jit(solution)/shard_map/agg_grad/pallas_call | solution.py:238
  231.0 3.0 %collective-permute-start.28 = (f32[1,2048]{1,0:T(1,128)S(1)}, f32[1,2048]{1,0:T(1,128)S(1)}, u32[]{:S(2)}, u32[]{:S(2)}) collective-permute-start(f32[1,2048]{1,0:T(1,128)S(1)} %add.92), channel_id=1, source_target_pairs={{0,2},{1,3},{2,0},{3,1},{4,6},{5,7},{6,4},{7,5},{8,10},{9,11},{10,... | collective-permute-start | bytes 24584 | tf_op jit(solution)/shard_map/ppermute | solution.py:283
  234.8 7.6 %collective-permute-done.20 = bf16[2,256,1024]{2,1,0:T(8,128)(2,1)S(1)} collective-permute-done((bf16[2,256,1024]{2,1,0:T(8,128)(2,1)S(1)}, bf16[2,256,1024]{2,1,0:T(8,128)(2,1)S(1)}, u32[]{:S(2)}, u32[]{:S(2)}) %collective-permute-start.20) | collective-permute-done | bytes 1048608 | tf_op jit(solution)/shard_map/ppermute | solution.py:283
  243.1 12.9 %nodes_grad.2.rest_0_ = bf16[2048,2048]{1,0:T(8,128)(2,1)} custom-call(bf16[2048,2048]{1,0:T(8,128)(2,1)} %get-tuple-element.15.table, bf16[1024,2048]{1,0:T(8,128)(2,1)S(1)} %agg_grad.2.low, bf16[1024,2048]{1,0:T(8,128)(2,1)} %copy-done.1), custom_call_target="tpu_custom_call" | custom-call | flops 8589934592 | bytes 16777216 | tf_op jit(solution)/shard_map/nodes_grad/pallas_call | solution.py:269
  260.9 8.3 %collective-permute-done.23 = bf16[64,2048]{1,0:T(8,128)(2,1)S(1)} collective-permute-done((bf16[64,2048]{1,0:T(8,128)(2,1)S(1)}, bf16[64,2048]{1,0:T(8,128)(2,1)S(1)}, u32[]{:S(2)}, u32[]{:S(2)}) %collective-permute-start.23) | collective-permute-done | bytes 262176 | tf_op jit(solution)/shard_map/ppermute | solution.py:283
  271.0 12.9 %nodes_grad.3 = bf16[2048,2048]{1,0:T(8,128)(2,1)} custom-call(bf16[2048,2048]{1,0:T(8,128)(2,1)} %get-tuple-element.15.table, bf16[1024,2048]{1,0:T(8,128)(2,1)S(1)} %agg_grad.2.low, bf16[1024,2048]{1,0:T(8,128)(2,1)} %copy-done.1, bf16[2048,2048]{1,0:T(8,128)(2,1)} %nodes_grad.2.rest_0_), custom_call_target="tpu_custom_call", output_to_operand_aliasing={{}: (3, {})} | custom-call | flops 8589934592 | bytes 16777216 | tf_op jit(solution)/shard_map/nodes_grad/pallas_call | solution.py:269
  (100 shorter events, 46.1 us)
Async XLA Ops:
  2.3 10.4 %collective-permute-start.7 = (bf16[64,1024]{1,0:T(8,128)(2,1)S(1)}, bf16[64,1024]{1,0:T(8,128)(2,1)S(1)}, u32[]{:S(2)}, u32[]{:S(2)}) collective-permute-start(bf16[64,1024]{1,0:T(8,128)(2,1)S(1)} %get-tuple-element.39), channel_id=1, source_target_pairs={{0,2},{1,3},{2,0},{3,1},{4,6},{5,7},{6,4},{7,5},{8,10},{9,11},{10,... | collective-permute-start | bytes 393224 | tf_op jit(solution)/shard_map/ppermute | solution.py:283
  6.4 8.5 %collective-permute-start.6 = (bf16[64,1024]{1,0:T(8,128)(2,1)S(1)}, bf16[64,1024]{1,0:T(8,128)(2,1)S(1)}, u32[]{:S(2)}, u32[]{:S(2)}) collective-permute-start(bf16[64,1024]{1,0:T(8,128)(2,1)S(1)} %get-tuple-element.39), channel_id=1, source_target_pairs={{0,1},{1,0},{2,3},{3,2},{4,5},{5,4},{6,7},{7,6},{8,9},{9,8},{10,11... | collective-permute-start | bytes 393224 | tf_op jit(solution)/shard_map/ppermute | solution.py:283
  13.4 6.0 %collective-permute-start = (bf16[64,1024]{1,0:T(8,128)(2,1)S(1)}, bf16[64,1024]{1,0:T(8,128)(2,1)S(1)}, u32[]{:S(2)}, u32[]{:S(2)}) collective-permute-start(bf16[64,1024]{1,0:T(8,128)(2,1)S(1)} %get-tuple-element.40), channel_id=1, source_target_pairs={{0,8},{1,9},{2,10},{3,11},{4,12},{5,13},{6,14},{7,15},{8,0},{9,1},... | collective-permute-start | bytes 393224 | tf_op jit(solution)/shard_map/ppermute | solution.py:283
  17.8 12.0 %collective-permute-start.9 = (bf16[256,1024]{1,0:T(8,128)(2,1)S(1)}, bf16[256,1024]{1,0:T(8,128)(2,1)S(1)}, u32[]{:S(2)}, u32[]{:S(2)}) collective-permute-start(bf16[256,1024]{1,0:T(8,128)(2,1)S(1)} %pad_maximum_fusion.1), channel_id=1, source_target_pairs={{0,8},{1,9},{2,10},{3,11},{4,12},{5,13},{6,14},{7,15},{8,0},{9,1},... | collective-permute-start | bytes 1572872 | tf_op jit(solution)/shard_map/ppermute | solution.py:283
  19.4 6.4 %collective-permute-start.1 = (bf16[128,1024]{1,0:T(8,128)(2,1)S(1)}, bf16[128,1024]{1,0:T(8,128)(2,1)S(1)}, u32[]{:S(2)}, u32[]{:S(2)}) collective-permute-start(bf16[128,1024]{1,0:T(8,128)(2,1)S(1)} %pad_maximum_fusion.2), channel_id=1, source_target_pairs={{0,16},{1,17},{2,18},{3,19},{4,20},{5,21},{6,22},{7,23},{8,24},{9,... | collective-permute-start | bytes 786440 | tf_op jit(solution)/shard_map/ppermute | solution.py:283
  25.9 25.5 %collective-permute-start.3 = (bf16[256,1024]{1,0:T(8,128)(2,1)S(1)}, bf16[256,1024]{1,0:T(8,128)(2,1)S(1)}, u32[]{:S(2)}, u32[]{:S(2)}) collective-permute-start(bf16[256,1024]{1,0:T(8,128)(2,1)S(1)} %pad_maximum_fusion), channel_id=1, source_target_pairs={{0,2},{1,3},{2,0},{3,1},{4,6},{5,7},{6,4},{7,5},{8,10},{9,11},{10,... | collective-permute-start | bytes 1572872 | tf_op jit(solution)/shard_map/ppermute | solution.py:283
  30.7 35.7 %collective-permute-start.10 = (bf16[512,1024]{1,0:T(8,128)(2,1)S(1)}, bf16[512,1024]{1,0:T(8,128)(2,1)S(1)}, u32[]{:S(2)}, u32[]{:S(2)}) collective-permute-start(bf16[512,1024]{1,0:T(8,128)(2,1)S(1)} %get-tuple-element.34), channel_id=1, source_target_pairs={{0,16},{1,17},{2,18},{3,19},{4,20},{5,21},{6,22},{7,23},{8,24},{9,... | collective-permute-start | bytes 3145736 | tf_op jit(solution)/shard_map/ppermute | solution.py:283
  32.2 24.4 %collective-permute-start.2 = (bf16[256,1024]{1,0:T(8,128)(2,1)S(1)}, bf16[256,1024]{1,0:T(8,128)(2,1)S(1)}, u32[]{:S(2)}, u32[]{:S(2)}) collective-permute-start(bf16[256,1024]{1,0:T(8,128)(2,1)S(1)} %pad_maximum_fusion), channel_id=1, source_target_pairs={{0,1},{1,0},{2,3},{3,2},{4,5},{5,4},{6,7},{7,6},{8,9},{9,8},{10,11... | collective-permute-start | bytes 1572872 | tf_op jit(solution)/shard_map/ppermute | solution.py:283
  51.4 14.9 %collective-permute-start.4 = (bf16[256,1024]{1,0:T(8,128)(2,1)S(1)}, bf16[256,1024]{1,0:T(8,128)(2,1)S(1)}, u32[]{:S(2)}, u32[]{:S(2)}) collective-permute-start(bf16[256,1024]{1,0:T(8,128)(2,1)S(1)} %collective-permute-done.3), channel_id=1, source_target_pairs={{0,1},{1,0},{2,3},{3,2},{4,5},{5,4},{6,7},{7,6},{8,9},{9,8},{10,11... | collective-permute-start | bytes 1572872 | tf_op jit(solution)/shard_map/ppermute | solution.py:283
  51.7 55.0 %collective-permute-start.12 = (bf16[1,64]{1,0:T(2,128)(2,1)S(1)}, bf16[1,64]{1,0:T(2,128)(2,1)S(1)}, u32[]{:S(2)}, u32[]{:S(2)}) collective-permute-start(bf16[1,64]{1,0:T(2,128)(2,1)S(1)} %bitcast.26), channel_id=1, source_target_pairs={{0,4},{1,5},{2,6},{3,7},{4,0},{5,1},{6,2},{7,3},{8,12},{9,13},{10,... | collective-permute-start | bytes 392 | tf_op jit(solution)/shard_map/ppermute | solution.py:283
  66.3 57.0 %collective-permute-start.5 = (bf16[1024,1024]{1,0:T(8,128)(2,1)S(1)}, bf16[1024,1024]{1,0:T(8,128)(2,1)}, u32[]{:S(2)}, u32[]{:S(2)}) collective-permute-start(bf16[1024,1024]{1,0:T(8,128)(2,1)S(1)} %constant_dynamic-update-slice_fusion.refs_0_), channel_id=1, source_target_pairs={{0,4},{1,5},{2,6},{3,7},{4,0},{5,1},{6,2},{7,3},{8,12},{9,13},{10,... | collective-permute-start | bytes 6291464 | tf_op jit(solution)/shard_map/ppermute | solution.py:283
  67.4 55.9 %collective-permute-start.11 = (bf16[1024,1024]{1,0:T(8,128)(2,1)}, bf16[1024,1024]{1,0:T(8,128)(2,1)}, u32[]{:S(2)}, u32[]{:S(2)}) collective-permute-start(bf16[1024,1024]{1,0:T(8,128)(2,1)} %constant_dynamic-update-slice_fusion.11.refs_2_), channel_id=1, source_target_pairs={{0,4},{1,5},{2,6},{3,7},{4,0},{5,1},{6,2},{7,3},{8,12},{9,13},{10,... | collective-permute-start | bytes 6291464 | tf_op jit(solution)/shard_map/ppermute | solution.py:283
  175.5 7.5 %collective-permute-start.17 = (bf16[4,256,2048]{2,1,0:T(8,128)(2,1)}, bf16[4,256,2048]{2,1,0:T(8,128)(2,1)}, u32[]{:S(2)}, u32[]{:S(2)}) collective-permute-start(bf16[4,256,2048]{2,1,0:T(8,128)(2,1)} %wgrad_send.1), channel_id=1, source_target_pairs={{0,4},{1,5},{2,6},{3,7},{4,0},{5,1},{6,2},{7,3},{8,12},{9,13},{10,... | collective-permute-start | bytes 12582920 | tf_op jit(solution)/shard_map/ppermute | solution.py:283
  181.4 33.2 %collective-permute-start.26 = (f32[1,2048]{1,0:T(1,128)S(1)}, f32[1,2048]{1,0:T(1,128)S(1)}, u32[]{:S(2)}, u32[]{:S(2)}) collective-permute-start(f32[1,2048]{1,0:T(1,128)S(1)} %add.90), channel_id=1, source_target_pairs={{0,8},{1,9},{2,10},{3,11},{4,12},{5,13},{6,14},{7,15},{8,0},{9,1},... | collective-permute-start | bytes 24584 | tf_op jit(solution)/shard_map/ppermute | solution.py:283
  198.9 35.1 %collective-permute-start.18 = (bf16[2,256,1024]{2,1,0:T(8,128)(2,1)S(1)}, bf16[2,256,1024]{2,1,0:T(8,128)(2,1)S(1)}, u32[]{:S(2)}, u32[]{:S(2)}) collective-permute-start(bf16[2,256,1024]{2,1,0:T(8,128)(2,1)S(1)} %get-tuple-element.18), channel_id=1, source_target_pairs={{0,16},{1,17},{2,18},{3,19},{4,20},{5,21},{6,22},{7,23},{8,24},{9,... | collective-permute-start | bytes 3145736 | tf_op jit(solution)/shard_map/ppermute | solution.py:283
  214.7 16.2 %collective-permute-start.27 = (f32[1,2048]{1,0:T(1,128)S(1)}, f32[1,2048]{1,0:T(1,128)S(1)}, u32[]{:S(2)}, u32[]{:S(2)}) collective-permute-start(f32[1,2048]{1,0:T(1,128)S(1)} %add.91), channel_id=1, source_target_pairs={{0,16},{1,17},{2,18},{3,19},{4,20},{5,21},{6,22},{7,23},{8,24},{9,... | collective-permute-start | bytes 24584 | tf_op jit(solution)/shard_map/ppermute | solution.py:283
  216.3 26.1 %collective-permute-start.20 = (bf16[2,256,1024]{2,1,0:T(8,128)(2,1)S(1)}, bf16[2,256,1024]{2,1,0:T(8,128)(2,1)S(1)}, u32[]{:S(2)}, u32[]{:S(2)}) collective-permute-start(bf16[2,256,1024]{2,1,0:T(8,128)(2,1)S(1)} %get-tuple-element.20), channel_id=1, source_target_pairs={{0,8},{1,9},{2,10},{3,11},{4,12},{5,13},{6,14},{7,15},{8,0},{9,1},... | collective-permute-start | bytes 3145736 | tf_op jit(solution)/shard_map/ppermute | solution.py:283
  231.0 25.0 %collective-permute-start.28 = (f32[1,2048]{1,0:T(1,128)S(1)}, f32[1,2048]{1,0:T(1,128)S(1)}, u32[]{:S(2)}, u32[]{:S(2)}) collective-permute-start(f32[1,2048]{1,0:T(1,128)S(1)} %add.92), channel_id=1, source_target_pairs={{0,2},{1,3},{2,0},{3,1},{4,6},{5,7},{6,4},{7,5},{8,10},{9,11},{10,... | collective-permute-start | bytes 24584 | tf_op jit(solution)/shard_map/ppermute | solution.py:283
  234.1 24.0 %collective-permute-start.19 = (bf16[256,1024]{1,0:T(8,128)(2,1)S(1)}, bf16[256,1024]{1,0:T(8,128)(2,1)S(1)}, u32[]{:S(2)}, u32[]{:S(2)}) collective-permute-start(bf16[256,1024]{1,0:T(8,128)(2,1)S(1)} %fusion), channel_id=1, source_target_pairs={{0,8},{1,9},{2,10},{3,11},{4,12},{5,13},{6,14},{7,15},{8,0},{9,1},... | collective-permute-start | bytes 1572872 | tf_op jit(solution)/shard_map/ppermute | solution.py:283
  242.5 15.8 %collective-permute-start.21 = (bf16[256,1024]{1,0:T(8,128)(2,1)S(1)}, bf16[256,1024]{1,0:T(8,128)(2,1)S(1)}, u32[]{:S(2)}, u32[]{:S(2)}) collective-permute-start(bf16[256,1024]{1,0:T(8,128)(2,1)S(1)} %fusion.1), channel_id=1, source_target_pairs={{0,16},{1,17},{2,18},{3,19},{4,20},{5,21},{6,22},{7,23},{8,24},{9,... | collective-permute-start | bytes 1572872 | tf_op jit(solution)/shard_map/ppermute | solution.py:283
  256.0 27.9 %collective-permute-start.29 = (f32[1,2048]{1,0:T(1,128)S(1)}, f32[1,2048]{1,0:T(1,128)S(1)}, u32[]{:S(2)}, u32[]{:S(2)}) collective-permute-start(f32[1,2048]{1,0:T(1,128)S(1)} %add.93), channel_id=1, source_target_pairs={{0,1},{1,0},{2,3},{3,2},{4,5},{5,4},{6,7},{7,6},{8,9},{9,8},{10,11... | collective-permute-start | bytes 24584 | tf_op jit(solution)/shard_map/ppermute | solution.py:283
  258.7 10.6 %collective-permute-start.23 = (bf16[64,2048]{1,0:T(8,128)(2,1)S(1)}, bf16[64,2048]{1,0:T(8,128)(2,1)S(1)}, u32[]{:S(2)}, u32[]{:S(2)}) collective-permute-start(bf16[64,2048]{1,0:T(8,128)(2,1)S(1)} %pad_maximum_fusion.4), channel_id=1, source_target_pairs={{0,1},{1,0},{2,3},{3,2},{4,5},{5,4},{6,7},{7,6},{8,9},{9,8},{10,11... | collective-permute-start | bytes 786440 | tf_op jit(solution)/shard_map/ppermute | solution.py:283
  258.8 25.7 %collective-permute-start.22 = (bf16[64,2048]{1,0:T(8,128)(2,1)S(1)}, bf16[64,2048]{1,0:T(8,128)(2,1)S(1)}, u32[]{:S(2)}, u32[]{:S(2)}) collective-permute-start(bf16[64,2048]{1,0:T(8,128)(2,1)S(1)} %pad_maximum_fusion.3), channel_id=1, source_target_pairs={{0,1},{1,0},{2,3},{3,2},{4,5},{5,4},{6,7},{7,6},{8,9},{9,8},{10,11... | collective-permute-start | bytes 786440 | tf_op jit(solution)/shard_map/ppermute | solution.py:283
  269.3 15.1 %collective-permute-start.24 = (bf16[64,2048]{1,0:T(8,128)(2,1)S(1)}, bf16[64,2048]{1,0:T(8,128)(2,1)S(1)}, u32[]{:S(2)}, u32[]{:S(2)}) collective-permute-start(bf16[64,2048]{1,0:T(8,128)(2,1)S(1)} %fusion.3), channel_id=1, source_target_pairs={{0,2},{1,3},{2,0},{3,1},{4,6},{5,7},{6,4},{7,5},{8,10},{9,11},{10,... | collective-permute-start | bytes 786440 | tf_op jit(solution)/shard_map/ppermute | solution.py:283
  (13 other events, 142.7 us)

commit v2 on v0

v2 whole, which is shorter than its diff:
```python
import functools

import jax
import jax.numpy as jnp
from jax import lax
from jax.experimental import pallas as pl
from jax.experimental.pallas import tpu as pltpu
from jax.sharding import PartitionSpec as P

AXES = ("clus", "rep")
MIB = 2**20
F32 = jnp.float32
BF16 = jnp.bfloat16
Z1, Z2, CORE, X, Y = 1, 2, 4, 8, 16
ANY = pl.BlockSpec(memory_space=pl.ANY)
SMEM = pl.BlockSpec(memory_space=pltpu.SMEM)
TN = (((0,), (0,)), ((), ()))
NT = (((1,), (1,)), ((), ()))
NN = (((1,), (0,)), ((), ()))
VMEM = pl.BlockSpec(memory_space=pltpu.VMEM)
HBM = pl.BlockSpec(memory_space=pltpu.HBM)
EXTRA = 128


def params(mib=12):
    return pltpu.CompilerParams(vmem_limit_bytes=int(mib * MIB))


def cost(flops, nbytes):
    return pl.CostEstimate(flops=flops, bytes_accessed=nbytes, transcendentals=0)


def column(row):
    return jnp.transpose(jnp.broadcast_to(row, (8, row.shape[1])))[:, :1]


def scale_row(start, degree, count):
    slots = start + lax.broadcasted_iota(jnp.int32, degree.shape, 1)
    live = (slots < count).astype(F32)
    return live / (degree.astype(F32) + 1.0)


def table_kernel(first, ctl, nb, deg, *rest):
    table, ctl_out = rest[-2:]
    hand_on(ctl, ctl_out)
    n = table.shape[0]
    fan, tile = nb.shape
    start = (pl.program_id(0) + first) * tile
    chunk = 256
    used = lax.broadcasted_iota(jnp.int32, (fan, tile), 0) < deg[...]
    slots = jnp.where(used, nb[...], -1)
    targets = lax.broadcasted_iota(jnp.int32, (chunk, tile), 0).astype(F32).astype(BF16)
    own = start + lax.broadcasted_iota(jnp.int32, (1, tile), 1)
    one = jnp.ones((), BF16)
    zero = jnp.zeros((), BF16)

    def local(rows, base):
        off = rows - base
        off = jnp.where(jnp.logical_and(off >= 0, off < chunk), off, -1)
        return off.astype(F32).astype(BF16)

    def build(c, carry):
        base = c * chunk
        here = local(slots, base)
        acc = jnp.where(targets == local(own, base), one + one, zero)
        for k in range(fan):
            acc = acc + jnp.where(targets == here[k : k + 1, :], one, zero)
        table[pl.ds(pl.multiple_of(base, chunk), chunk), :] = acc
        return carry

    lax.fori_loop(0, n // chunk, build, 0)


def neighbour_table(ctl, nb, deg, first, steps, into=None):
    fan, n = nb.shape
    tile = n // 4
    extra = [] if into is None else [into]
    return pl.pallas_call(
        functools.partial(table_kernel, first),
        grid=(steps,),
        in_specs=[
            SMEM,
            pl.BlockSpec((fan, tile), lambda t: (0, t + first)),
            pl.BlockSpec((1, tile), lambda t: (0, t + first)),
        ]
        + [ANY] * len(extra),
        out_specs=[pl.BlockSpec((n, tile), lambda t: (0, t + first)), SMEM],
        out_shape=[jax.ShapeDtypeStruct((n, n), BF16), CTL],
        input_output_aliases={3: 0} if extra else {},
        compiler_params=params(6),
        cost_estimate=cost(n * n * tile * steps, n * tile * steps * 2),
        name="table",
    )(ctl, nb, deg, *extra)


TILE = 256


def columns_of(ref, t):
    return ref[:, pl.ds(pl.multiple_of(t * TILE, TILE), TILE)]


def scaled(ctl, deg, t, value):
    at = pl.multiple_of(t * TILE, TILE)
    return (value * column(scale_row(at, deg[:, pl.ds(at, TILE)], ctl[1]))).astype(BF16)


CTL = jax.ShapeDtypeStruct((2,), jnp.int32)


def hand_on(ctl, ctl_out):
    ctl_out[0] = ctl[0]
    ctl_out[1] = ctl[1]


def rows_spec(width, first=0):
    return pl.BlockSpec((TILE, width), lambda t: (t + first, 0))


def aggregate_kernel(first, ctl, deg, table, nodes, *rest):
    out, ctl_out = rest[-2:]
    hand_on(ctl, ctl_out)
    t = pl.program_id(0) + first
    value = lax.dot_general(columns_of(table, t), nodes[...], TN, preferred_element_type=F32)
    out[...] = scaled(ctl, deg, t, value)


def aggregate(ctl, deg, table, nodes, first, steps, into=None):
    n, d = nodes.shape
    extra = [] if into is None else [into]
    return pl.pallas_call(
        functools.partial(aggregate_kernel, first),
        grid=(steps,),
        in_specs=[SMEM, VMEM, VMEM, VMEM] + [ANY] * len(extra),
        out_specs=[rows_spec(d, first), SMEM],
        out_shape=[jax.ShapeDtypeStruct((n, d), BF16), CTL],
        input_output_aliases={4: 0} if extra else {},
        compiler_params=params(3),
        cost_estimate=cost(2 * steps * TILE * d * n, (n + 2 * steps * TILE) * d * 2),
        name="aggregate",
    )(ctl, deg, table, nodes, *extra)


def forward_kernel(ctl, agg, weight, bias, cot_all, act, grad, bias_sum, ctl_out, cot_v, cot_sem):
    hand_on(ctl, ctl_out)
    t = pl.program_id(0)
    half = weight.shape[1] // 2

    def fetch(i):
        slot = lax.rem(i, 2)
        rows = pl.ds(pl.multiple_of(i * TILE, TILE), TILE)
        return pltpu.make_async_copy(cot_all.at[rows, :], cot_v.at[slot], cot_sem.at[slot])

    @pl.when(t == 0)
    def _():
        bias_sum[...] = jnp.zeros_like(bias_sum)
        fetch(t).start()

    fetch(t).wait()

    @pl.when(t + 1 < pl.num_programs(0))
    def _():
        fetch(t + 1).start()

    cot = cot_v.at[lax.rem(t, 2)]

    slots = t * TILE + lax.broadcasted_iota(jnp.int32, (TILE, half), 0)
    live = (slots < ctl[1]).astype(F32).astype(BF16)
    for side in range(2):
        at = slice(side * half, (side + 1) * half)
        pre = jnp.dot(agg[...], weight[:, at], preferred_element_type=F32) + bias[:, at]
        sig = jax.nn.sigmoid(pre)
        silu = pre * sig
        act[:, at] = silu.astype(BF16) * live
        slope = (cot[:, at] * live).astype(F32) * (sig + silu * (1.0 - sig))
        grad[:, at] = slope.astype(BF16)
        bias_sum[:, at] += jnp.sum(slope, axis=0, keepdims=True)


def forward(ctl, agg, weight, bias, cot):
    n, d = agg.shape
    m = weight.shape[1]
    return pl.pallas_call(
        forward_kernel,
        grid=(n // TILE,),
        in_specs=[SMEM, rows_spec(d), VMEM, VMEM, HBM],
        out_specs=[rows_spec(m), rows_spec(m), VMEM, SMEM],
        out_shape=[
            jax.ShapeDtypeStruct((n, m), BF16),
            jax.ShapeDtypeStruct((n, m), BF16),
            jax.ShapeDtypeStruct((1, m), F32),
            CTL,
        ],
        scratch_shapes=[pltpu.VMEM((2, TILE, m), BF16), pltpu.SemaphoreType.DMA((2,))],
        compiler_params=params(14),
        cost_estimate=cost(2 * n * d * m, 5 * n * m * 2),
        name="forward",
    )(ctl, agg, weight, bias, cot)


def place_kernel(codes, ctl, *refs):
    pieces, refs = refs[: len(codes)], refs[len(codes) :]
    weight, bias, ctl_out, heads, weight_sem, head_sem = refs[-6:]
    hand_on(ctl, ctl_out)
    m = weight.shape[1]
    copies, head_copies, pairs = [], [], []
    for (order, col), piece in zip(codes, pieces):
        rows = piece.shape[0] // len(order)
        wide = min(piece.shape[1], m - col)
        for i, code in enumerate(order):
            owner = lax.bitwise_xor(ctl[0], code)
            copies.append(
                pltpu.make_async_copy(
                    piece.at[pl.ds(i * rows, rows), pl.ds(0, wide)],
                    weight.at[pl.ds(pl.multiple_of(owner * rows, rows), rows), pl.ds(col, wide)],
                    weight_sem.at[len(copies)],
                )
            )
            if wide < piece.shape[1]:
                head = piece.at[pl.ds(i * rows, 16), pl.ds(wide, EXTRA)]
                k = len(head_copies)
                head_copies.append(pltpu.make_async_copy(head, heads.at[k], head_sem.at[k]))
                if code & 1 == 0:
                    pairs.append((k, order.index(code ^ 1) - i + k, owner // 2))
    for c in copies + head_copies:
        c.start()
    bias[...] = refs[1][...] if len(refs) == 8 else jnp.zeros_like(bias)
    for c in head_copies:
        c.wait()
    for one, two, pair in pairs:
        both = heads[one, :1, :].astype(F32) + heads[two, :1, :].astype(F32)
        bias[:, pl.ds(pl.multiple_of(pair * EXTRA, EXTRA), EXTRA)] = both
    for c in copies:
        c.wait()


def place(ctl, pieces, codes, shape, into=()):
    total = sum(len(order) for order, _ in codes)
    first = 1 + len(pieces)
    return pl.pallas_call(
        functools.partial(place_kernel, codes),
        in_specs=[SMEM] + [ANY] * len(pieces) + ([ANY, VMEM] if into else []),
        out_specs=[ANY, VMEM, SMEM],
        out_shape=[jax.ShapeDtypeStruct(shape, BF16), jax.ShapeDtypeStruct((1, shape[1]), F32), CTL],
        input_output_aliases={first: 0} if into else {},
        scratch_shapes=[
            pltpu.VMEM((total // 2, 16, EXTRA), BF16),
            pltpu.SemaphoreType.DMA((total,)),
            pltpu.SemaphoreType.DMA((total // 2,)),
        ],
        compiler_params=params(1),
        cost_estimate=cost(0, 2 * shape[0] * shape[1]),
        name="place",
    )(ctl, *pieces, *into)


def terms_of(me, tile, value, bias_sum, out):
    m = value.shape[1]
    rows = value.shape[0] // 4
    z = lax.rem(me, 4)
    out[:, m:] = jnp.zeros((value.shape[0], EXTRA), BF16)
    head = lax.broadcasted_iota(jnp.int32, (16, EXTRA), 0) == 0
    for q in range(4):
        at = pl.multiple_of(lax.bitwise_xor(z, q) * rows, rows)
        out[pl.ds(at, rows), :m] = value[q * rows : (q + 1) * rows, :].astype(BF16)
        pair = bias_sum[:, pl.ds(pl.multiple_of(tile * TILE + q // 2 * EXTRA, EXTRA), EXTRA)]
        out[pl.ds(at, 16), m:] = jnp.where(head, pair, 0.0).astype(BF16)


def wgrad_kernel(other, ctl, agg, grad, bias_sum, out, ctl_out):
    hand_on(ctl, ctl_out)
    tile = lax.bitwise_xor(ctl[0] // 4, 2 * pl.program_id(0) + other)
    value = lax.dot_general(columns_of(agg, tile), grad[...], TN, preferred_element_type=F32)
    terms_of(ctl[0], tile, value, bias_sum, out.at[0])


def wgrad(ctl, agg, grad, bias_sum, other):
    n, d = agg.shape
    m = grad.shape[1]
    return pl.pallas_call(
        functools.partial(wgrad_kernel, other),
        grid=(4,),
        in_specs=[SMEM, VMEM, VMEM, VMEM],
        out_specs=[pl.BlockSpec((1, TILE, m + EXTRA), lambda t: (t, 0, 0)), SMEM],
        out_shape=[jax.ShapeDtypeStruct((4, TILE, m + EXTRA), BF16), CTL],
        compiler_params=params(5),
        cost_estimate=cost(n * d * m, 2 * n * m * 2),
        name="wgrad",
    )(ctl, agg, grad, bias_sum)


def agg_grad_kernel(ctl, deg, grad, weight, out, ctl_out):
    hand_on(ctl, ctl_out)
    value = lax.dot_general(grad[...], weight[...], NT, preferred_element_type=F32)
    out[...] = scaled(ctl, deg, pl.program_id(0), value)


def agg_grad(ctl, deg, grad, weight):
    n, m = grad.shape
    d = weight.shape[0]
    return pl.pallas_call(
        agg_grad_kernel,
        grid=(n // TILE,),
        in_specs=[SMEM, VMEM, rows_spec(m), VMEM],
        out_specs=[rows_spec(d), SMEM],
        out_shape=[jax.ShapeDtypeStruct((n, d), BF16), CTL],
        compiler_params=params(3),
        cost_estimate=cost(2 * n * d * m, 3 * n * m * 2),
        name="agg_grad",
    )(ctl, deg, grad, weight)


def nodes_grad_kernel(ctl, table, spread, *rest):
    out, ctl_out = rest[-2:]
    hand_on(ctl, ctl_out)
    out[...] = jnp.dot(table[...], spread[...], preferred_element_type=F32).astype(BF16)


def nodes_grad(ctl, table, spread, first, steps, into=None):
    n, d = spread.shape
    extra = [] if into is None else [into]
    return pl.pallas_call(
        nodes_grad_kernel,
        grid=(steps,),
        in_specs=[SMEM, rows_spec(n, first), VMEM] + [ANY] * len(extra),
        out_specs=[rows_spec(d, first), SMEM],
        out_shape=[jax.ShapeDtypeStruct((n, d), BF16), CTL],
        input_output_aliases={3: 0} if extra else {},
        compiler_params=params(4),
        cost_estimate=cost(2 * steps * TILE * d * n, (n + 2 * steps * TILE) * d * 2),
        name="nodes_grad",
    )(ctl, table, spread, *extra)


def swap(value, bit):
    return lax.ppermute(value, AXES, [(i, i ^ bit) for i in range(32)])


def after(value, *others):
    return lax.optimization_barrier((value, *others))[0]


def codes_of(*bits):
    order = [0]
    for group in bits:
        order = [code ^ g for g in group for code in order]
    return order


def with_bias(odd, weight, bias):
    rows = bias.shape[0]
    lanes = jnp.concatenate([bias, bias])
    mine = (jnp.arange(EXTRA) >= rows) == odd
    head = jnp.where(mine, lanes, 0).astype(BF16)[None, :]
    tail = jnp.where(jnp.arange(rows)[:, None] == 0, head, 0).astype(BF16)
    return jnp.concatenate([weight, tail], axis=1)


def cat(*parts):
    return jnp.concatenate(parts, axis=0)


def fast(nodes, weight, bias, neighbours, degree, counts, cotangent):
    me = (lax.axis_index("clus") * 4 + lax.axis_index("rep")).astype(jnp.int32)[None]
    ctl = cat(me, counts)
    rows, m = weight.shape
    half = m // 2
    nb = neighbours.T
    deg = degree[None, :]
    steps = nodes.shape[0] // TILE

    odd = me % 2 == 1
    own = with_bias(odd, weight, bias)
    one, two = swap(own, Z1), swap(own, Z2)
    table, ctl = neighbour_table(after(ctl, own), nb, deg, 0, 3)
    one, two = after(one, ctl), after(two, ctl)
    three = swap(two, Z1)
    table, ctl = neighbour_table(after(ctl, two), nb, deg, 3, 1, table)
    three = after(three, ctl)
    p = cat(own[:, :half], one[:, :half], two[:, :half], three[:, :half])
    q = cat(own[:, half:], one[:, half:], two[:, half:], three[:, half:])
    px, qy = swap(p, X), swap(q, Y)
    agg, ctl = aggregate(after(ctl, p, q), deg, table, nodes, 0, 3)
    px, qy = after(px, ctl), after(qy, ctl)
    p, q = cat(p, px), cat(q, qy)
    py, qx = swap(p, Y), swap(q, X)
    p_other, q_other = swap(p, CORE), swap(q, CORE)
    agg, ctl = aggregate(after(ctl, p, q), deg, table, nodes, 3, steps - 3, agg)
    zs = (0, Z1, Z2, Z1 ^ Z2)
    near_p, near_q = codes_of(zs, (0, X)), codes_of(zs, (0, Y))

    def ends(flip_p, flip_q):
        order_p, order_q = [c ^ flip_p for c in near_p], [c ^ flip_q for c in near_q]
        return (order_p, 0), (order_q, half), ([c ^ CORE for c in order_p], 0), ([c ^ CORE for c in order_q], half)

    *full, ctl = place(ctl, (p, q, p_other, q_other), ends(0, 0), (32 * rows, m))
    py, qx = after(py, ctl), after(qx, ctl)
    pieces = (py, qx, swap(py, CORE), swap(qx, CORE))
    full, bias_full, ctl = place(ctl, pieces, ends(Y, X), (32 * rows, m), full)
    act, grad, bias_sum, ctl = forward(ctl, agg, full, bias_full, cotangent)

    terms, ctl = wgrad(ctl, agg, grad, bias_sum, 1)
    got = swap(terms, CORE)
    mine, ctl = wgrad(ctl, agg, grad, bias_sum, 0)
    got = after(got, ctl).reshape(2, 2, 4 * rows, m + EXTRA)
    mine = mine.reshape(2, 2, 4 * rows, m + EXTRA)

    def total(*parts):
        return functools.reduce(jnp.add, [part.astype(F32) for part in parts])

    send_p = total(mine[1, :, :, :half], got[1, :, :, :half]).astype(BF16)
    send_q = total(mine[:, 1, :, half:], got[:, 1, :, half:]).astype(BF16)
    got_p, got_q = swap(send_p, Y), swap(send_q, X)
    spread, ctl = agg_grad(after(ctl, send_p, send_q), deg, grad, full)
    got_p, got_q = after(got_p, ctl), after(got_q, ctl)
    next_p = total(mine[0, 1, :, :half], got[0, 1, :, :half], got_p[1]).astype(BF16)
    next_q = total(mine[1, 0, :, half:], got[1, 0, :, half:], got_q[1]).astype(BF16)
    got2_p, got2_q = swap(next_p, X), swap(next_q, Y)
    out, ctl = nodes_grad(after(ctl, next_p, next_q), table, spread, 0, 3)
    got2_p, got2_q = after(got2_p, ctl), after(got2_q, ctl)

    def piece(i):
        at = slice(i * rows, (i + 1) * rows)
        p = total(mine[0, 0, at, :half], got[0, 0, at, :half], got_p[0, at], got2_p[at])
        q = total(mine[0, 0, at, half:], got[0, 0, at, half:], got_q[0, at], got2_q[at])
        return jnp.concatenate([p, q], axis=1)

    third, first = piece(3).astype(BF16), piece(1).astype(BF16)
    far, near = swap(third, Z1), swap(first, Z1)
    out, ctl = nodes_grad(after(ctl, third, first), table, spread, 3, 2, out)
    second = (piece(2) + after(far, ctl).astype(F32)).astype(BF16)
    mid = swap(second, Z2)
    out, ctl = nodes_grad(after(ctl, second), table, spread, 5, steps - 5, out)
    near, mid = after(near, ctl), after(mid, ctl)
    last = piece(0) + near.astype(F32) + mid.astype(F32)
    bias_grad = jnp.where(odd, last[0, m + rows :], last[0, m : m + rows])
    return act, out, last[:, :m], bias_grad


def general(nodes, weight, bias, neighbours, degree, counts, cotangent):
    ctl = cat(jnp.zeros_like(counts), counts)
    nb = neighbours.T
    deg = degree[None, :]
    steps = nodes.shape[0] // TILE
    full = lax.all_gather(weight, AXES, axis=0, tiled=True)
    bias_full = lax.all_gather(bias, AXES, axis=0, tiled=True).astype(F32)[None, :]
    table, _ = neighbour_table(ctl, nb, deg, 0, 4)
    agg, _ = aggregate(ctl, deg, table, nodes, 0, steps)
    act, grad, bias_sum, _ = forward(ctl, agg, full, bias_full, cotangent)
    term = lax.dot_general(agg, grad, TN, preferred_element_type=F32)
    weight_grad = lax.psum_scatter(term, AXES, scatter_dimension=0, tiled=True)
    bias_grad = lax.psum_scatter(bias_sum[0], AXES, scatter_dimension=0, tiled=True)
    spread, _ = agg_grad(ctl, deg, grad, full)
    out, _ = nodes_grad(ctl, table, spread, 0, steps)
    return act, out, weight_grad, bias_grad


def solution(mesh):
    both = P(AXES, None)
    one = P(AXES)
    cube = (mesh.shape["clus"], mesh.shape["rep"]) == (8, 4)
    return jax.shard_map(
        fast if cube else general,
        mesh=mesh,
        in_specs=(both, both, one, both, one, one, both),
        out_specs=(both, both, both, one),
        check_vma=False,
    )
```

time: 679 us -> 205 us (0.30)
  waiting for transfers between devices: 244 us -> 30.9 us
  matrix products: 160 us -> 0 us
  other arithmetic: 153 us -> 11.3 us
  Pallas kernels: 0 us -> 135 us
  blocking collectives: 86.8 us -> 0 us
  starting transfers between devices: 0.08 us -> 17.7 us
  between operations: 15 us -> 1.64 us
  local copies, waits for them, and re-layouts: 20.8 us -> 8.4 us
    reduce_scatter x1 -> x0, waiting for transfers between devices: 244 us -> none  [body(): lax.psum_scatter(weight_term, ('clus', 'rep'), scatter_dimension=0, tiled...]
    dot_general x6 -> x0, matrix products: 160 us -> none  [the longest x1 32.3 us: body(): lax.dot_general(agg, pre_grad, contract, preferred_element_type=jnp.float32)]
    add x16 -> x3, other arithmetic: 149 us -> 2.87 us  [the longest x2 2.8 us: total(): return functools.reduce(jnp.add, [part.astype(F32) for part in parts])]
    pallas_call x0 -> x13, Pallas kernels: none -> 135 us  [the longest x1 27.2 us: forward(): pl.pallas_call(forward_kernel, grid=(n // TILE,), in_specs=[SMEM, rows_sp...]
    unnamed x2 -> x0, blocking collectives: 86.8 us -> none
    ppermute x0 -> x19, waiting for transfers between devices: none -> 30.9 us  [swap(): return lax.ppermute(value, AXES, [(i, i ^ bit) for i in range(32)])]
    ppermute x0 -> x19, starting transfers between devices: none -> 17.7 us  [swap(): return lax.ppermute(value, AXES, [(i, i ^ bit) for i in range(32)])]
    dynamic_slice x16 -> x0, local copies, waits for them, and re-layouts: 13.6 us -> none  [count_step(): column = lax.dynamic_slice_in_dim(neighbours, k, 1, 1)]
  transfers between devices with their start and end apart: 2 -> 19, of which waited for: 1 -> 10; matrix products, arithmetic and copies ran while one was open for 39% -> 2% of each run, Pallas kernels for 0% -> 46%
where the time goes in v2:
time: 205 us
  Pallas kernels  135 us (66%)
  waiting for transfers between devices  30.9 us (15%)
  starting transfers between devices  17.7 us (9%)
  other arithmetic  11.3 us (6%)
  local copies, waits for them, and re-layouts  8.4 us (4%)
    ppermute x19, waiting for transfers between devices, swap(): return lax.ppermute(value, AXES, [(i, i ^ bit) for i in range(32)])  30.9 us
    pallas_call x1, Pallas kernels, forward(): pl.pallas_call(forward_kernel, grid=(n // TILE,), in_specs=[SMEM, rows_sp...  27.2 us
    pallas_call x3, Pallas kernels, nodes_grad(): pl.pallas_call(nodes_grad_kernel, grid=(steps,), in_specs=[SMEM, rows_spe...  23.4 us
    pallas_call x2, Pallas kernels, wgrad(): pl.pallas_call(functools.partial(wgrad_kernel, other), grid=(4,), in_spec...  21 us
    pallas_call x2, Pallas kernels, aggregate(): pl.pallas_call(functools.partial(aggregate_kernel, first), grid=(steps,),...  20.9 us
    pallas_call x1, Pallas kernels, agg_grad(): pl.pallas_call(agg_grad_kernel, grid=(n // TILE,), in_specs=[SMEM, VMEM,...  19.9 us
    ppermute x19, starting transfers between devices, swap(): return lax.ppermute(value, AXES, [(i, i ^ bit) for i in range(32)])  17.7 us
    pallas_call x2, Pallas kernels, neighbour_table(): pl.pallas_call(functools.partial(table_kernel, first), grid=(steps,), in_...  17.6 us
  transfers between devices with their start and end apart: 19, of which 10 were waited for; matrix products, arithmetic and copies ran while one was open for 2% of the time, Pallas kernels for 46%

profile of v2, /device:TPU:0, one launch (start us, length us, event | category | flops | bytes accessed | tf_op | source)
XLA Modules:
  0.0 205.0 jit_solution(13133685916588909041)
XLA Ops:
  2.5 3.1 %collective-permute-start.1 = (bf16[64,2176]{1,0:T(8,128)(2,1)S(1)}, bf16[64,2176]{1,0:T(8,128)(2,1)S(1)}, u32[]{:S(2)}, u32[]{:S(2)}) collective-permute-start(bf16[64,2176]{1,0:T(8,128)(2,1)S(1)} %pad_maximum_fusion.2), channel_id=1, source_target_pairs={{0,1},{1,0},{2,3},{3,2},{4,5},{5,4},{6,7},{7,6},{8,9},{9,8},{10,11... | collective-permute-start | bytes 835592 | tf_op jit(solution)/shard_map/ppermute | solution.py:336
  5.6 2.6 %collective-permute-start = (bf16[64,2176]{1,0:T(8,128)(2,1)S(1)}, bf16[64,2176]{1,0:T(8,128)(2,1)S(1)}, u32[]{:S(2)}, u32[]{:S(2)}) collective-permute-start(bf16[64,2176]{1,0:T(8,128)(2,1)S(1)} %pad_maximum_fusion.2), channel_id=1, source_target_pairs={{0,2},{1,3},{2,0},{3,1},{4,6},{5,7},{6,4},{7,5},{8,10},{9,11},{10,... | collective-permute-start | bytes 835592 | tf_op jit(solution)/shard_map/ppermute | solution.py:336
  10.5 12.8 %table.2 = (bf16[2048,2048]{1,0:T(8,128)(2,1)S(1)}, s32[2]{0:T(128)S(1)}) custom-call(s32[2]{0:T(128)S(1)} %pad_add_fusion.ctl, s32[16,2048]{1,0:T(8,128)S(1)} %bitcast.68, s32[1,2048]{1,0:T(1,128)S(1)} %bitcast.70), custom_call_target="tpu_custom_call" | custom-call | flops 6442450944 | bytes 6291456 | tf_op jit(solution)/shard_map/table/pallas_call | solution.py:78
  24.2 4.8 %table.3 = (bf16[2048,2048]{1,0:T(8,128)(2,1)S(1)}, s32[2]{0:T(128)S(1)}) custom-call(s32[2]{0:T(128)S(1)} %get-tuple-element.60.ctl, s32[16,2048]{1,0:T(8,128)S(1)} %bitcast.69, s32[1,2048]{1,0:T(1,128)S(1)} %bitcast.71, bf16[2048,2048]{1,0:T(8,128)(2,1)S(1)} %get-tuple-element.61.rest_0_), custom_call_target="tpu_custom_call", output_to_operand_aliasing={{0}: (3, {})} | custom-call | flops 2147483648 | bytes 2097152 | tf_op jit(solution)/shard_map/table/pallas_call | solution.py:78
  29.1 2.2 %collective-permute-done.2 = bf16[64,2176]{1,0:T(8,128)(2,1)S(1)} collective-permute-done((bf16[64,2176]{1,0:T(8,128)(2,1)S(1)}, bf16[64,2176]{1,0:T(8,128)(2,1)S(1)}, u32[]{:S(2)}, u32[]{:S(2)}) %collective-permute-start.2) | collective-permute-done | bytes 278560 | tf_op jit(solution)/shard_map/ppermute | solution.py:336
  34.6 8.0 %aggregate.2 = (bf16[2048,2048]{1,0:T(8,128)(2,1)S(1)}, s32[2]{0:T(128)S(1)}) custom-call(s32[2]{0:T(128)S(1)} %get-tuple-element.65.ctl, s32[1,2048]{1,0:T(1,128)S(1)} %bitcast.72, bf16[2048,2048]{1,0:T(8,128)(2,1)S(1)} %get-tuple-element.66.table, bf16[2048,2048]{1,0:T(8,128)(2,1)S(1)} %copy-done.4), custom_call_target="tpu_custom_call" | custom-call | flops 6442450944 | bytes 14680064 | tf_op jit(solution)/shard_map/aggregate/pallas_call | solution.py:131
  42.6 3.8 %collective-permute-done.4 = bf16[256,1152]{1,0:T(8,128)(2,1)S(1)} collective-permute-done((bf16[256,1152]{1,0:T(8,128)(2,1)S(1)}, bf16[256,1152]{1,0:T(8,128)(2,1)S(1)}, u32[]{:S(2)}, u32[]{:S(2)}) %collective-permute-start.4) | collective-permute-done | bytes 589856 | tf_op jit(solution)/shard_map/ppermute | solution.py:336
  49.0 12.9 %aggregate.3 = (bf16[2048,2048]{1,0:T(8,128)(2,1)S(1)}, s32[2]{0:T(128)S(1)}) custom-call(s32[2]{0:T(128)S(1)} %get-tuple-element.70.ctl, s32[1,2048]{1,0:T(1,128)S(1)} %bitcast.73, bf16[2048,2048]{1,0:T(8,128)(2,1)S(1)} %get-tuple-element.66.table, bf16[2048,2048]{1,0:T(8,128)(2,1)S(1)} %copy-done.4, ...), custom_call_target="tpu_custom_call", output_to_operand_aliasing={{0}: (4, {})} | custom-call | flops 10737418240 | bytes 18874368 | tf_op jit(solution)/shard_map/aggregate/pallas_call | solution.py:131
  61.9 3.4 %copy-done.5 = bf16[2048,2048]{1,0:T(8,128)(2,1)} copy-done((bf16[2048,2048]{1,0:T(8,128)(2,1)}, bf16[2048,2048]{1,0:T(8,128)(2,1)S(1)}, u32[]{:S(2)}) %copy-start.5) | copy-done | bytes 8388632
  65.3 2.5 %place.2 = (bf16[2048,2048]{1,0:T(8,128)(2,1)S(1)}, f32[1,2048]{1,0:T(1,128)S(1)}, s32[2]{0:T(128)S(1)}) custom-call(s32[2]{0:T(128)S(1)} %get-tuple-element.72.ctl, bf16[512,1024]{1,0:T(8,128)(2,1)S(1)} %constant_dynamic-update-slice_fusion.refs_0_, bf16[512,1152]{1,0:T(8,128)(2,1)S(1)} %constant_dynamic-update-slice_fusion.5.refs_1_, ...), custom_call_target="tpu_custom_call" | custom-call | bytes 8388608 | tf_op jit(solution)/shard_map/place/pallas_call | solution.py:240
  67.8 7.1 %collective-permute-done.8.refs_1_ = bf16[512,1152]{1,0:T(8,128)(2,1)S(1)} collective-permute-done((bf16[512,1152]{1,0:T(8,128)(2,1)S(1)}, bf16[512,1152]{1,0:T(8,128)(2,1)S(1)}, u32[]{:S(2)}, u32[]{:S(2)}) %collective-permute-start.8) | collective-permute-done | bytes 1179680 | tf_op jit(solution)/shard_map/ppermute | solution.py:336
  75.5 3.8 %collective-permute-done.9.refs_2_ = bf16[512,1024]{1,0:T(8,128)(2,1)S(1)} collective-permute-done((bf16[512,1024]{1,0:T(8,128)(2,1)S(1)}, bf16[512,1024]{1,0:T(8,128)(2,1)S(1)}, u32[]{:S(2)}, u32[]{:S(2)}) %collective-permute-start.9) | collective-permute-done | bytes 1048608 | tf_op jit(solution)/shard_map/ppermute | solution.py:336
  79.3 2.5 %place.3 = (bf16[2048,2048]{1,0:T(8,128)(2,1)S(1)}, f32[1,2048]{1,0:T(1,128)S(1)}, s32[2]{0:T(128)S(1)}) custom-call(s32[2]{0:T(128)S(1)} %get-tuple-element.73.ctl, bf16[512,1024]{1,0:T(8,128)(2,1)S(1)} %collective-permute-done.7.refs_0_, bf16[512,1152]{1,0:T(8,128)(2,1)S(1)} %collective-permute-done.8.refs_1_, ...), custom_call_target="tpu_custom_call", output_to_operand_aliasing={{0}: (5, {})} | custom-call | bytes 8388608 | tf_op jit(solution)/shard_map/place/pallas_call | solution.py:240
  84.0 27.2 %forward.1 = (bf16[2048,2048]{1,0:T(8,128)(2,1)}, bf16[2048,2048]{1,0:T(8,128)(2,1)S(1)}, f32[1,2048]{1,0:T(1,128)S(1)}, s32[2]{0:T(128)S(1)}) custom-call(s32[2]{0:T(128)S(1)} %get-tuple-element.78.ctl, bf16[2048,2048]{1,0:T(8,128)(2,1)S(1)} %copy-done.6, bf16[2048,2048]{1,0:T(8,128)(2,1)S(1)} %get-tuple-element.80.weight, ...), custom_call_target="tpu_custom_call" | custom-call | flops 17179869184 | bytes 41943040 | tf_op jit(solution)/shard_map/forward/pallas_call | solution.py:183
  111.2 10.5 %wgrad.2 = (bf16[4,256,2176]{2,1,0:T(8,128)(2,1)S(1)}, s32[2]{0:T(128)S(1)}) custom-call(s32[2]{0:T(128)S(1)} %get-tuple-element.83.ctl, bf16[2048,2048]{1,0:T(8,128)(2,1)S(1)} %bitcast.78, bf16[2048,2048]{1,0:T(8,128)(2,1)S(1)} %get-tuple-element.84.grad, f32[1,2048]{1,0:T(1,128)S(1)} %get-tuple-element.85.bias_sum), custom_call_target="tpu_custom_call" | custom-call | flops 8589934592 | bytes 16777216 | tf_op jit(solution)/shard_map/wgrad/pallas_call | solution.py:280
  121.8 10.5 %wgrad.3 = (bf16[4,256,2176]{2,1,0:T(8,128)(2,1)S(1)}, s32[2]{0:T(128)S(1)}) custom-call(s32[2]{0:T(128)S(1)} %get-tuple-element.86.ctl, bf16[2048,2048]{1,0:T(8,128)(2,1)S(1)} %bitcast.78, bf16[2048,2048]{1,0:T(8,128)(2,1)S(1)} %get-tuple-element.84.grad, f32[1,2048]{1,0:T(1,128)S(1)} %get-tuple-element.85.bias_sum), custom_call_target="tpu_custom_call" | custom-call | flops 8589934592 | bytes 16777216 | tf_op jit(solution)/shard_map/wgrad/pallas_call | solution.py:280
  137.6 19.9 %agg_grad.1 = (bf16[2048,2048]{1,0:T(8,128)(2,1)S(1)}, s32[2]{0:T(128)S(1)}) custom-call(s32[2]{0:T(128)S(1)} %get-tuple-element.91.ctl, s32[1,2048]{1,0:T(1,128)S(1)} %bitcast.74, bf16[2048,2048]{1,0:T(8,128)(2,1)S(1)} %get-tuple-element.84.grad, bf16[2048,2048]{1,0:T(8,128)(2,1)S(1)} %get-tuple-element.80.weight), custom_call_target="tpu_custom_call" | custom-call | flops 17179869184 | bytes 25165824 | tf_op jit(solution)/shard_map/agg_grad/pallas_call | solution.py:301
  157.5 3.5 %collective-permute-done.12 = bf16[2,256,1024]{2,1,0:T(8,128)(2,1)S(1)} collective-permute-done((bf16[2,256,1024]{2,1,0:T(8,128)(2,1)S(1)}, bf16[2,256,1024]{2,1,0:T(8,128)(2,1)S(1)}, u32[]{:S(2)}, u32[]{:S(2)}) %collective-permute-start.12) | collective-permute-done | bytes 1048608 | tf_op jit(solution)/shard_map/ppermute | solution.py:336
  162.9 2.6 %collective-permute-done.13 = bf16[2,256,1152]{2,1,0:T(8,128)(2,1)S(1)} collective-permute-done((bf16[2,256,1152]{2,1,0:T(8,128)(2,1)S(1)}, bf16[2,256,1152]{2,1,0:T(8,128)(2,1)S(1)}, u32[]{:S(2)}, u32[]{:S(2)}) %collective-permute-start.13) | collective-permute-done | bytes 1179680 | tf_op jit(solution)/shard_map/ppermute | solution.py:336
  166.9 8.6 %nodes_grad.3 = (bf16[2048,2048]{1,0:T(8,128)(2,1)}, s32[2]{0:T(128)S(1)}) custom-call(s32[2]{0:T(128)S(1)} %get-tuple-element.95.ctl, bf16[2048,2048]{1,0:T(8,128)(2,1)S(1)} %get-tuple-element.66.table, bf16[2048,2048]{1,0:T(8,128)(2,1)S(1)} %get-tuple-element.96.spread), custom_call_target="tpu_custom_call" | custom-call | flops 6442450944 | bytes 14680064 | tf_op jit(solution)/shard_map/nodes_grad/pallas_call | solution.py:322
  177.7 3.2 %collective-permute-done.15 = bf16[256,1152]{1,0:T(8,128)(2,1)S(1)} collective-permute-done((bf16[256,1152]{1,0:T(8,128)(2,1)S(1)}, bf16[256,1152]{1,0:T(8,128)(2,1)S(1)}, u32[]{:S(2)}, u32[]{:S(2)}) %collective-permute-start.15) | collective-permute-done | bytes 589856 | tf_op jit(solution)/shard_map/ppermute | solution.py:336
  184.5 6.2 %nodes_grad.4 = (bf16[2048,2048]{1,0:T(8,128)(2,1)}, s32[2]{0:T(128)S(1)}) custom-call(s32[2]{0:T(128)S(1)} %get-tuple-element.100.ctl, bf16[2048,2048]{1,0:T(8,128)(2,1)S(1)} %get-tuple-element.66.table, bf16[2048,2048]{1,0:T(8,128)(2,1)S(1)} %get-tuple-element.96.spread, bf16[2048,2048]{1,0:T(8,128)(2,1)} %get-tuple-element.101.rest_0_), custom_call_target="tpu_custom_call", output_to_operand_aliasing={{0}: (3, {})} | custom-call | flops 4294967296 | bytes 12582912 | tf_op jit(solution)/shard_map/nodes_grad/pallas_call | solution.py:322
  192.3 8.6 %nodes_grad.5 = (bf16[2048,2048]{1,0:T(8,128)(2,1)}, s32[2]{0:T(128)}) custom-call(s32[2]{0:T(128)S(1)} %get-tuple-element.104.ctl, bf16[2048,2048]{1,0:T(8,128)(2,1)S(1)} %get-tuple-element.66.table, bf16[2048,2048]{1,0:T(8,128)(2,1)S(1)} %get-tuple-element.96.spread, bf16[2048,2048]{1,0:T(8,128)(2,1)} %get-tuple-element.105.rest_0_), custom_call_target="tpu_custom_call", output_to_operand_aliasing={{0}: (3, {})} | custom-call | flops 6442450944 | bytes 14680064 | tf_op jit(solution)/shard_map/nodes_grad/pallas_call | solution.py:322
  200.9 2.6 %collective-permute-done.18 = bf16[64,2176]{1,0:T(8,128)(2,1)S(1)} collective-permute-done((bf16[64,2176]{1,0:T(8,128)(2,1)S(1)}, bf16[64,2176]{1,0:T(8,128)(2,1)S(1)}, u32[]{:S(2)}, u32[]{:S(2)}) %collective-permute-start.18) | collective-permute-done | bytes 278560 | tf_op jit(solution)/shard_map/ppermute | solution.py:336
  (82 shorter events, 30.3 us)
Async XLA Ops:
  2.5 21.4 %collective-permute-start.1 = (bf16[64,2176]{1,0:T(8,128)(2,1)S(1)}, bf16[64,2176]{1,0:T(8,128)(2,1)S(1)}, u32[]{:S(2)}, u32[]{:S(2)}) collective-permute-start(bf16[64,2176]{1,0:T(8,128)(2,1)S(1)} %pad_maximum_fusion.2), channel_id=1, source_target_pairs={{0,1},{1,0},{2,3},{3,2},{4,5},{5,4},{6,7},{7,6},{8,9},{9,8},{10,11... | collective-permute-start | bytes 835592 | tf_op jit(solution)/shard_map/ppermute | solution.py:336
  5.6 17.8 %collective-permute-start = (bf16[64,2176]{1,0:T(8,128)(2,1)S(1)}, bf16[64,2176]{1,0:T(8,128)(2,1)S(1)}, u32[]{:S(2)}, u32[]{:S(2)}) collective-permute-start(bf16[64,2176]{1,0:T(8,128)(2,1)S(1)} %pad_maximum_fusion.2), channel_id=1, source_target_pairs={{0,2},{1,3},{2,0},{3,1},{4,6},{5,7},{6,4},{7,5},{8,10},{9,11},{10,... | collective-permute-start | bytes 835592 | tf_op jit(solution)/shard_map/ppermute | solution.py:336
  10.5 12.8 %copy-start.7 = (bf16[64,2048]{1,0:T(8,128)(2,1)S(1)}, bf16[64,2048]{1,0:T(8,128)(2,1)}, u32[]{:S(2)}) copy-start(bf16[64,2048]{1,0:T(8,128)(2,1)} %param.8) | copy-start | bytes 786436
  23.4 7.9 %collective-permute-start.2 = (bf16[64,2176]{1,0:T(8,128)(2,1)S(1)}, bf16[64,2176]{1,0:T(8,128)(2,1)S(1)}, u32[]{:S(2)}, u32[]{:S(2)}) collective-permute-start(bf16[64,2176]{1,0:T(8,128)(2,1)S(1)} %collective-permute-done), channel_id=1, source_target_pairs={{0,1},{1,0},{2,3},{3,2},{4,5},{5,4},{6,7},{7,6},{8,9},{9,8},{10,11... | collective-permute-start | bytes 835592 | tf_op jit(solution)/shard_map/ppermute | solution.py:336
  24.2 10.4 %copy-start.4 = (bf16[2048,2048]{1,0:T(8,128)(2,1)S(1)}, bf16[2048,2048]{1,0:T(8,128)(2,1)}, u32[]{:S(2)}) copy-start(bf16[2048,2048]{1,0:T(8,128)(2,1)} %nodes.3) | copy-start | bytes 25165828
  31.4 15.7 %collective-permute-start.3 = (bf16[256,1024]{1,0:T(8,128)(2,1)S(1)}, bf16[256,1024]{1,0:T(8,128)(2,1)S(1)}, u32[]{:S(2)}, u32[]{:S(2)}) collective-permute-start(bf16[256,1024]{1,0:T(8,128)(2,1)S(1)} %pad_maximum_fusion.1), channel_id=1, source_target_pairs={{0,8},{1,9},{2,10},{3,11},{4,12},{5,13},{6,14},{7,15},{8,0},{9,1},... | collective-permute-start | bytes 1572872 | tf_op jit(solution)/shard_map/ppermute | solution.py:336
  33.0 13.4 %collective-permute-start.4 = (bf16[256,1152]{1,0:T(8,128)(2,1)S(1)}, bf16[256,1152]{1,0:T(8,128)(2,1)S(1)}, u32[]{:S(2)}, u32[]{:S(2)}) collective-permute-start(bf16[256,1152]{1,0:T(8,128)(2,1)S(1)} %pad_maximum_fusion), channel_id=1, source_target_pairs={{0,16},{1,17},{2,18},{3,19},{4,20},{5,21},{6,22},{7,23},{8,24},{9,... | collective-permute-start | bytes 1769480 | tf_op jit(solution)/shard_map/ppermute | solution.py:336
  46.5 18.8 %collective-permute-start.6 = (bf16[512,1152]{1,0:T(8,128)(2,1)S(1)}, bf16[512,1152]{1,0:T(8,128)(2,1)S(1)}, u32[]{:S(2)}, u32[]{:S(2)}) collective-permute-start(bf16[512,1152]{1,0:T(8,128)(2,1)S(1)} %constant_dynamic-update-slice_fusion.5.refs_1_), channel_id=1, source_target_pairs={{0,4},{1,5},{2,6},{3,7},{4,0},{5,1},{6,2},{7,3},{8,12},{9,13},{10,... | collective-permute-start | bytes 3538952 | tf_op jit(solution)/shard_map/ppermute | solution.py:336
  46.6 28.4 %collective-permute-start.8 = (bf16[512,1152]{1,0:T(8,128)(2,1)S(1)}, bf16[512,1152]{1,0:T(8,128)(2,1)S(1)}, u32[]{:S(2)}, u32[]{:S(2)}) collective-permute-start(bf16[512,1152]{1,0:T(8,128)(2,1)S(1)} %constant_dynamic-update-slice_fusion.5.refs_1_), channel_id=1, source_target_pairs={{0,8},{1,9},{2,10},{3,11},{4,12},{5,13},{6,14},{7,15},{8,0},{9,1},... | collective-permute-start | bytes 3538952 | tf_op jit(solution)/shard_map/ppermute | solution.py:336
  47.2 18.1 %collective-permute-start.5 = (bf16[512,1024]{1,0:T(8,128)(2,1)S(1)}, bf16[512,1024]{1,0:T(8,128)(2,1)S(1)}, u32[]{:S(2)}, u32[]{:S(2)}) collective-permute-start(bf16[512,1024]{1,0:T(8,128)(2,1)S(1)} %constant_dynamic-update-slice_fusion.refs_0_), channel_id=1, source_target_pairs={{0,4},{1,5},{2,6},{3,7},{4,0},{5,1},{6,2},{7,3},{8,12},{9,13},{10,... | collective-permute-start | bytes 3145736 | tf_op jit(solution)/shard_map/ppermute | solution.py:336
  47.4 27.5 %collective-permute-start.7 = (bf16[512,1024]{1,0:T(8,128)(2,1)S(1)}, bf16[512,1024]{1,0:T(8,128)(2,1)S(1)}, u32[]{:S(2)}, u32[]{:S(2)}) collective-permute-start(bf16[512,1024]{1,0:T(8,128)(2,1)S(1)} %constant_dynamic-update-slice_fusion.refs_0_), channel_id=1, source_target_pairs={{0,16},{1,17},{2,18},{3,19},{4,20},{5,21},{6,22},{7,23},{8,24},{9,... | collective-permute-start | bytes 3145736 | tf_op jit(solution)/shard_map/ppermute | solution.py:336
  65.3 16.6 %slice-start = ((s8[8388608]{0:T(1024)(128)(4,1)}), s8[4194304]{0:T(1024)(128)(4,1)S(1)}, s32[]{:S(2)}) async-start(s8[8388608]{0:T(1024)(128)(4,1)} %bitcast.75), calls=%async_computation | async-start | bytes 8388608
  74.9 4.4 %collective-permute-start.10 = (bf16[512,1152]{1,0:T(8,128)(2,1)S(1)}, bf16[512,1152]{1,0:T(8,128)(2,1)S(1)}, u32[]{:S(2)}, u32[]{:S(2)}) collective-permute-start(bf16[512,1152]{1,0:T(8,128)(2,1)S(1)} %collective-permute-done.8.refs_1_), channel_id=1, source_target_pairs={{0,4},{1,5},{2,6},{3,7},{4,0},{5,1},{6,2},{7,3},{8,12},{9,13},{10,... | collective-permute-start | bytes 3538952 | tf_op jit(solution)/shard_map/ppermute | solution.py:336
  75.0 4.3 %collective-permute-start.9 = (bf16[512,1024]{1,0:T(8,128)(2,1)S(1)}, bf16[512,1024]{1,0:T(8,128)(2,1)S(1)}, u32[]{:S(2)}, u32[]{:S(2)}) collective-permute-start(bf16[512,1024]{1,0:T(8,128)(2,1)S(1)} %collective-permute-done.7.refs_0_), channel_id=1, source_target_pairs={{0,4},{1,5},{2,6},{3,7},{4,0},{5,1},{6,2},{7,3},{8,12},{9,13},{10,... | collective-permute-start | bytes 3145736 | tf_op jit(solution)/shard_map/ppermute | solution.py:336
  79.3 31.9 %slice-start.2 = ((s8[8388608]{0:T(1024)(128)(4,1)}), s8[4194304]{0:T(1024)(128)(4,1)S(1)}, s32[]{:S(2)}) async-start(s8[8388608]{0:T(1024)(128)(4,1)} %bitcast.77), calls=%async_computation.2 | async-start | bytes 8388608
  84.0 27.2 %slice-start.3 = ((s8[8388608]{0:T(1024)(128)(4,1)}), s8[4194304]{0:T(1024)(128)(4,1)S(1)}, s32[]{:S(2)}) async-start(s8[8388608]{0:T(1024)(128)(4,1)} %bitcast.77), calls=%async_computation.3 | async-start | bytes 8388608
  121.7 10.7 %collective-permute-start.11 = (bf16[4,256,2176]{2,1,0:T(8,128)(2,1)S(1)}, bf16[4,256,2176]{2,1,0:T(8,128)(2,1)}, u32[]{:S(2)}, u32[]{:S(2)}) collective-permute-start(bf16[4,256,2176]{2,1,0:T(8,128)(2,1)S(1)} %get-tuple-element.89), channel_id=1, source_target_pairs={{0,4},{1,5},{2,6},{3,7},{4,0},{5,1},{6,2},{7,3},{8,12},{9,13},{10,... | collective-permute-start | bytes 13369352 | tf_op jit(solution)/shard_map/ppermute | solution.py:336
  135.5 25.5 %collective-permute-start.12 = (bf16[2,256,1024]{2,1,0:T(8,128)(2,1)S(1)}, bf16[2,256,1024]{2,1,0:T(8,128)(2,1)S(1)}, u32[]{:S(2)}, u32[]{:S(2)}) collective-permute-start(bf16[2,256,1024]{2,1,0:T(8,128)(2,1)S(1)} %fusion.2), channel_id=1, source_target_pairs={{0,16},{1,17},{2,18},{3,19},{4,20},{5,21},{6,22},{7,23},{8,24},{9,... | collective-permute-start | bytes 3145736 | tf_op jit(solution)/shard_map/ppermute | solution.py:336
  137.1 28.4 %collective-permute-start.13 = (bf16[2,256,1152]{2,1,0:T(8,128)(2,1)S(1)}, bf16[2,256,1152]{2,1,0:T(8,128)(2,1)S(1)}, u32[]{:S(2)}, u32[]{:S(2)}) collective-permute-start(bf16[2,256,1152]{2,1,0:T(8,128)(2,1)S(1)} %fusion), channel_id=1, source_target_pairs={{0,8},{1,9},{2,10},{3,11},{4,12},{5,13},{6,14},{7,15},{8,0},{9,1},... | collective-permute-start | bytes 3538952 | tf_op jit(solution)/shard_map/ppermute | solution.py:336
  162.3 14.0 %collective-permute-start.14 = (bf16[256,1024]{1,0:T(8,128)(2,1)S(1)}, bf16[256,1024]{1,0:T(8,128)(2,1)S(1)}, u32[]{:S(2)}, u32[]{:S(2)}) collective-permute-start(bf16[256,1024]{1,0:T(8,128)(2,1)S(1)} %fusion.3), channel_id=1, source_target_pairs={{0,8},{1,9},{2,10},{3,11},{4,12},{5,13},{6,14},{7,15},{8,0},{9,1},... | collective-permute-start | bytes 1572872 | tf_op jit(solution)/shard_map/ppermute | solution.py:336
  166.8 14.0 %collective-permute-start.15 = (bf16[256,1152]{1,0:T(8,128)(2,1)S(1)}, bf16[256,1152]{1,0:T(8,128)(2,1)S(1)}, u32[]{:S(2)}, u32[]{:S(2)}) collective-permute-start(bf16[256,1152]{1,0:T(8,128)(2,1)S(1)} %fusion.1), channel_id=1, source_target_pairs={{0,16},{1,17},{2,18},{3,19},{4,20},{5,21},{6,22},{7,23},{8,24},{9,... | collective-permute-start | bytes 1769480 | tf_op jit(solution)/shard_map/ppermute | solution.py:336
  182.3 9.6 %collective-permute-start.16 = (bf16[64,2176]{1,0:T(8,128)(2,1)S(1)}, bf16[64,2176]{1,0:T(8,128)(2,1)S(1)}, u32[]{:S(2)}, u32[]{:S(2)}) collective-permute-start(bf16[64,2176]{1,0:T(8,128)(2,1)S(1)} %pad_maximum_fusion.3), channel_id=1, source_target_pairs={{0,1},{1,0},{2,3},{3,2},{4,5},{5,4},{6,7},{7,6},{8,9},{9,8},{10,11... | collective-permute-start | bytes 835592 | tf_op jit(solution)/shard_map/ppermute | solution.py:336
  182.9 18.0 %collective-permute-start.17 = (bf16[64,2176]{1,0:T(8,128)(2,1)S(1)}, bf16[64,2176]{1,0:T(8,128)(2,1)S(1)}, u32[]{:S(2)}, u32[]{:S(2)}) collective-permute-start(bf16[64,2176]{1,0:T(8,128)(2,1)S(1)} %pad_maximum_fusion.4), channel_id=1, source_target_pairs={{0,1},{1,0},{2,3},{3,2},{4,5},{5,4},{6,7},{7,6},{8,9},{9,8},{10,11... | collective-permute-start | bytes 835592 | tf_op jit(solution)/shard_map/ppermute | solution.py:336
  192.0 11.6 %collective-permute-start.18 = (bf16[64,2176]{1,0:T(8,128)(2,1)S(1)}, bf16[64,2176]{1,0:T(8,128)(2,1)S(1)}, u32[]{:S(2)}, u32[]{:S(2)}) collective-permute-start(bf16[64,2176]{1,0:T(8,128)(2,1)S(1)} %fusion.4), channel_id=1, source_target_pairs={{0,2},{1,3},{2,0},{3,1},{4,6},{5,7},{6,4},{7,5},{8,10},{9,11},{10,... | collective-permute-start | bytes 835592 | tf_op jit(solution)/shard_map/ppermute | solution.py:336
  (7 other events, 14.0 us)

commit v3 on v2

--- a/solution.py
+++ b/solution.py
@@ -85,7 +85,7 @@
         ]
         + [ANY] * len(extra),
         out_specs=[pl.BlockSpec((n, tile), lambda t: (0, t + first)), SMEM],
-        out_shape=[jax.ShapeDtypeStruct((n, n), BF16), CTL],
+        out_shape=[pltpu.HBM((n, n), BF16), CTL],
         input_output_aliases={3: 0} if extra else {},
         compiler_params=params(6),
         cost_estimate=cost(n * n * tile * steps, n * tile * steps * 2),
@@ -96,10 +96,6 @@
 TILE = 256
 
 
-def columns_of(ref, t):
-    return ref[:, pl.ds(pl.multiple_of(t * TILE, TILE), TILE)]
-
-
 def scaled(ctl, deg, t, value):
     at = pl.multiple_of(t * TILE, TILE)
     return (value * column(scale_row(at, deg[:, pl.ds(at, TILE)], ctl[1]))).astype(BF16)
@@ -118,10 +114,10 @@
 
 
 def aggregate_kernel(first, ctl, deg, table, nodes, *rest):
-    out, ctl_out = rest[-2:]
+    out, ctl_out, _ = rest[-3:]
     hand_on(ctl, ctl_out)
     t = pl.program_id(0) + first
-    value = lax.dot_general(columns_of(table, t), nodes[...], TN, preferred_element_type=F32)
+    value = lax.dot_general(table[...], nodes[...], TN, preferred_element_type=F32)
     out[...] = scaled(ctl, deg, t, value)
 
 
@@ -131,44 +127,75 @@
     return pl.pallas_call(
         functools.partial(aggregate_kernel, first),
         grid=(steps,),
-        in_specs=[SMEM, VMEM, VMEM, VMEM] + [ANY] * len(extra),
-        out_specs=[rows_spec(d, first), SMEM],
-        out_shape=[jax.ShapeDtypeStruct((n, d), BF16), CTL],
-        input_output_aliases={4: 0} if extra else {},
-        compiler_params=params(3),
+        in_specs=[SMEM, VMEM, pl.BlockSpec((n, TILE), lambda t: (0, t + first)), VMEM] + [ANY] * len(extra),
+        out_specs=[rows_spec(d, first), SMEM, ANY],
+        out_shape=[pltpu.HBM((n, d), BF16), CTL, pltpu.HBM((n, n), BF16)],
+        input_output_aliases={2: 2, 4: 0} if extra else {2: 2},
+        compiler_params=params(6.5),
         cost_estimate=cost(2 * steps * TILE * d * n, (n + 2 * steps * TILE) * d * 2),
         name="aggregate",
     )(ctl, deg, table, nodes, *extra)
 
 
-def forward_kernel(ctl, agg, weight, bias, cot_all, act, grad, bias_sum, ctl_out, cot_v, cot_sem):
+def halves(ctl, width, far):
+    y, x = ctl[0] // 16, lax.rem(ctl[0] // 8, 2)
+    if far:
+        y, x = 1 - y, 1 - x
+    two, four = width // 2, width // 4
+    return [(y * two, two)], [(x * four, four), (two + x * four, four)]
+
+
+def half_product(agg, weight, where, at):
+    parts = []
+    for start, length in where:
+        rows = pl.ds(pl.multiple_of(start, length), length)
+        parts.append(jnp.dot(agg[:, rows], weight[rows, at], preferred_element_type=F32))
+    return functools.reduce(jnp.add, parts)
+
+
+def near_kernel(ctl, agg, weight, part, ctl_out, _):
+    hand_on(ctl, ctl_out)
+    d, m = weight.shape
+    for side, where in enumerate(halves(ctl, d, False)):
+        at = slice(side * m // 2, (side + 1) * m // 2)
+        part[:, at] = half_product(agg, weight, where, at).astype(BF16)
+
+
+def near_product(ctl, agg, weight):
+    n, d = agg.shape
+    m = weight.shape[1]
+    return pl.pallas_call(
+        near_kernel,
+        grid=(n // TILE,),
+        in_specs=[SMEM, rows_spec(d), VMEM],
+        out_specs=[rows_spec(m), SMEM, ANY],
+        out_shape=[pltpu.HBM((n, m), BF16), CTL, pltpu.HBM((n, d), BF16)],
+        input_output_aliases={1: 2},
+        compiler_params=params(8),
+        cost_estimate=cost(n * d * m, 8 * n * m),
+        name="near",
+    )(ctl, agg, weight)
+
+
+def forward_kernel(split, ctl, agg, weight, bias, cot, *refs):
+    act, grad, bias_sum, ctl_out, _ = refs[-5:]
     hand_on(ctl, ctl_out)
     t = pl.program_id(0)
-    half = weight.shape[1] // 2
-
-    def fetch(i):
-        slot = lax.rem(i, 2)
-        rows = pl.ds(pl.multiple_of(i * TILE, TILE), TILE)
-        return pltpu.make_async_copy(cot_all.at[rows, :], cot_v.at[slot], cot_sem.at[slot])
+    d, m = weight.shape
+    half = m // 2
 
     @pl.when(t == 0)
     def _():
         bias_sum[...] = jnp.zeros_like(bias_sum)
-        fetch(t).start()
-
-    fetch(t).wait()
-
-    @pl.when(t + 1 < pl.num_programs(0))
-    def _():
-        fetch(t + 1).start()
-
-    cot = cot_v.at[lax.rem(t, 2)]
 
     slots = t * TILE + lax.broadcasted_iota(jnp.int32, (TILE, half), 0)
     live = (slots < ctl[1]).astype(F32).astype(BF16)
-    for side in range(2):
+    for side, where in enumerate(halves(ctl, d, True)):
         at = slice(side * half, (side + 1) * half)
-        pre = jnp.dot(agg[...], weight[:, at], preferred_element_type=F32) + bias[:, at]
+        if split:
+            pre = half_product(agg, weight, where, at) + refs[0][:, at].astype(F32) + bias[:, at]
+        else:
+            pre = jnp.dot(agg[...], weight[:, at], preferred_element_type=F32) + bias[:, at]
         sig = jax.nn.sigmoid(pre)
         silu = pre * sig
         act[:, at] = silu.astype(BF16) * live
@@ -177,25 +204,26 @@
         bias_sum[:, at] += jnp.sum(slope, axis=0, keepdims=True)
 
 
-def forward(ctl, agg, weight, bias, cot):
+def forward(ctl, agg, weight, bias, cot, *part):
     n, d = agg.shape
     m = weight.shape[1]
     return pl.pallas_call(
-        forward_kernel,
+        functools.partial(forward_kernel, bool(part)),
         grid=(n // TILE,),
-        in_specs=[SMEM, rows_spec(d), VMEM, VMEM, HBM],
-        out_specs=[rows_spec(m), rows_spec(m), VMEM, SMEM],
+        in_specs=[SMEM, rows_spec(d), VMEM, VMEM, rows_spec(m)] + [rows_spec(m)] * len(part),
+        out_specs=[rows_spec(m), rows_spec(m), VMEM, SMEM, ANY],
         out_shape=[
-            jax.ShapeDtypeStruct((n, m), BF16),
+            pltpu.HBM((n, m), BF16),
             jax.ShapeDtypeStruct((n, m), BF16),
             jax.ShapeDtypeStruct((1, m), F32),
             CTL,
+            pltpu.HBM((n, d), BF16),
         ],
-        scratch_shapes=[pltpu.VMEM((2, TILE, m), BF16), pltpu.SemaphoreType.DMA((2,))],
+        input_output_aliases={1: 4, 5: 0} if part else {1: 4},
         compiler_params=params(14),
         cost_estimate=cost(2 * n * d * m, 5 * n * m * 2),
         name="forward",
-    )(ctl, agg, weight, bias, cot)
+    )(ctl, agg, weight, bias, cot, *part)
 
 
 def place_kernel(codes, ctl, *refs):
@@ -248,7 +276,7 @@
             pltpu.SemaphoreType.DMA((total,)),
             pltpu.SemaphoreType.DMA((total // 2,)),
         ],
-        compiler_params=params(1),
+        compiler_params=params(2),
         cost_estimate=cost(0, 2 * shape[0] * shape[1]),
         name="place",
     )(ctl, *pieces, *into)
@@ -267,10 +295,10 @@
         out[pl.ds(at, 16), m:] = jnp.where(head, pair, 0.0).astype(BF16)
 
 
-def wgrad_kernel(other, ctl, agg, grad, bias_sum, out, ctl_out):
+def wgrad_kernel(other, ctl, agg, grad, bias_sum, out, ctl_out, _):
     hand_on(ctl, ctl_out)
     tile = lax.bitwise_xor(ctl[0] // 4, 2 * pl.program_id(0) + other)
-    value = lax.dot_general(columns_of(agg, tile), grad[...], TN, preferred_element_type=F32)
+    value = lax.dot_general(agg[...], grad[...], TN, preferred_element_type=F32)
     terms_of(ctl[0], tile, value, bias_sum, out.at[0])
 
 
@@ -279,11 +307,19 @@
     m = grad.shape[1]
     return pl.pallas_call(
         functools.partial(wgrad_kernel, other),
-        grid=(4,),
-        in_specs=[SMEM, VMEM, VMEM, VMEM],
-        out_specs=[pl.BlockSpec((1, TILE, m + EXTRA), lambda t: (t, 0, 0)), SMEM],
-        out_shape=[jax.ShapeDtypeStruct((4, TILE, m + EXTRA), BF16), CTL],
-        compiler_params=params(5),
+        grid_spec=pltpu.PrefetchScalarGridSpec(
+            num_scalar_prefetch=1,
+            grid=(4,),
+            in_specs=[
+                pl.BlockSpec((n, TILE), lambda t, ctl: (0, (ctl[0] // 4) ^ (2 * t + other))),
+                VMEM,
+                VMEM,
+            ],
+            out_specs=[pl.BlockSpec((1, TILE, m + EXTRA), lambda t, ctl: (t, 0, 0)), SMEM, ANY],
+        ),
+        out_shape=[jax.ShapeDtypeStruct((4, TILE, m + EXTRA), BF16), CTL, pltpu.HBM((n, d), BF16)],
+        input_output_aliases={1: 2},
+        compiler_params=params(8),
         cost_estimate=cost(n * d * m, 2 * n * m * 2),
         name="wgrad",
     )(ctl, agg, grad, bias_sum)
@@ -304,7 +340,7 @@
         in_specs=[SMEM, VMEM, rows_spec(m), VMEM],
         out_specs=[rows_spec(d), SMEM],
         out_shape=[jax.ShapeDtypeStruct((n, d), BF16), CTL],
-        compiler_params=params(3),
+        compiler_params=params(5),
         cost_estimate=cost(2 * n * d * m, 3 * n * m * 2),
         name="agg_grad",
     )(ctl, deg, grad, weight)
@@ -326,7 +362,7 @@
         out_specs=[rows_spec(d, first), SMEM],
         out_shape=[jax.ShapeDtypeStruct((n, d), BF16), CTL],
         input_output_aliases={3: 0} if extra else {},
-        compiler_params=params(4),
+        compiler_params=params(5),
         cost_estimate=cost(2 * steps * TILE * d * n, (n + 2 * steps * TILE) * d * 2),
         name="nodes_grad",
     )(ctl, table, spread, *extra)
@@ -380,12 +416,12 @@
     p = cat(own[:, :half], one[:, :half], two[:, :half], three[:, :half])
     q = cat(own[:, half:], one[:, half:], two[:, half:], three[:, half:])
     px, qy = swap(p, X), swap(q, Y)
-    agg, ctl = aggregate(after(ctl, p, q), deg, table, nodes, 0, 3)
+    agg, ctl, table = aggregate(after(ctl, p, q), deg, table, nodes, 0, 3)
     px, qy = after(px, ctl), after(qy, ctl)
     p, q = cat(p, px), cat(q, qy)
     py, qx = swap(p, Y), swap(q, X)
     p_other, q_other = swap(p, CORE), swap(q, CORE)
-    agg, ctl = aggregate(after(ctl, p, q), deg, table, nodes, 3, steps - 3, agg)
+    agg, ctl, table = aggregate(after(ctl, p, q), deg, table, nodes, 3, steps - 3, agg)
     zs = (0, Z1, Z2, Z1 ^ Z2)
     near_p, near_q = codes_of(zs, (0, X)), codes_of(zs, (0, Y))
 
@@ -394,14 +430,15 @@
         return (order_p, 0), (order_q, half), ([c ^ CORE for c in order_p], 0), ([c ^ CORE for c in order_q], half)
 
     *full, ctl = place(ctl, (p, q, p_other, q_other), ends(0, 0), (32 * rows, m))
+    part, ctl, agg = near_product(ctl, agg, full[0])
     py, qx = after(py, ctl), after(qx, ctl)
     pieces = (py, qx, swap(py, CORE), swap(qx, CORE))
     full, bias_full, ctl = place(ctl, pieces, ends(Y, X), (32 * rows, m), full)
-    act, grad, bias_sum, ctl = forward(ctl, agg, full, bias_full, cotangent)
-
-    terms, ctl = wgrad(ctl, agg, grad, bias_sum, 1)
+    act, grad, bias_sum, ctl, agg = forward(ctl, agg, full, bias_full, cotangent, part)
+
+    terms, ctl, agg = wgrad(ctl, agg, grad, bias_sum, 1)
     got = swap(terms, CORE)
-    mine, ctl = wgrad(ctl, agg, grad, bias_sum, 0)
+    mine, ctl, _ = wgrad(ctl, agg, grad, bias_sum, 0)
     got = after(got, ctl).reshape(2, 2, 4 * rows, m + EXTRA)
     mine = mine.reshape(2, 2, 4 * rows, m + EXTRA)
 
@@ -445,8 +482,8 @@
     full = lax.all_gather(weight, AXES, axis=0, tiled=True)
     bias_full = lax.all_gather(bias, AXES, axis=0, tiled=True).astype(F32)[None, :]
     table, _ = neighbour_table(ctl, nb, deg, 0, 4)
-    agg, _ = aggregate(ctl, deg, table, nodes, 0, steps)
-    act, grad, bias_sum, _ = forward(ctl, agg, full, bias_full, cotangent)
+    agg, _, table = aggregate(ctl, deg, table, nodes, 0, steps)
+    act, grad, bias_sum, _, agg = forward(ctl, agg, full, bias_full, cotangent)
     term = lax.dot_general(agg, grad, TN, preferred_element_type=F32)
     weight_grad = lax.psum_scatter(term, AXES, scatter_dimension=0, tiled=True)
     bias_grad = lax.psum_scatter(bias_sum[0], AXES, scatter_dimension=0, tiled=True)

time: 205 us -> 198 us (0.966)
  Pallas kernels: 135 us -> 148 us
  waiting for transfers between devices: 30.9 us -> 19.6 us
  other arithmetic: 11.3 us -> 4.34 us
  local copies, waits for them, and re-layouts: 8.4 us -> 2.96 us
  starting transfers between devices: 17.7 us -> 20.8 us
    ppermute x19, waiting for transfers between devices: 30.9 us -> 19.6 us  [swap(): return lax.ppermute(value, AXES, [(i, i ^ bit) for i in range(32)])]
    pallas_call x3 -> x4, Pallas kernels: 48.2 us -> 56.2 us  [the longest x2 23 us: wgrad(): pl.pallas_call(functools.partial(wgrad_kernel, other), grid_spec=pltpu.Pr...]
    unnamed x31 -> x27, local copies, waits for them, and re-layouts: 7.47 us -> 2.03 us
    pallas_call x2, Pallas kernels: 20.9 us -> 24.2 us  [aggregate(): pl.pallas_call(functools.partial(aggregate_kernel, first), grid=(steps,),...]
    ppermute x19, starting transfers between devices: 17.7 us -> 20.8 us  [swap(): return lax.ppermute(value, AXES, [(i, i ^ bit) for i in range(32)])]
    add x2, other arithmetic: 2.8 us -> 0.55 us  [total(): return functools.reduce(jnp.add, [part.astype(F32) for part in parts])]
  transfers between devices with their start and end apart: 19 -> 19, of which waited for: 10 -> 8; matrix products, arithmetic and copies ran while one was open for 2% -> 1% of each run, Pallas kernels for 46% -> 58%
where the time goes in v3:
time: 198 us; the launch traced here: 197 us
  Pallas kernels  148 us (75%)
  starting transfers between devices  20.8 us (11%)
  waiting for transfers between devices  19.6 us (10%)
  other arithmetic  4.34 us (2%)
  local copies, waits for them, and re-layouts  2.96 us (1%)
    pallas_call x2, Pallas kernels, aggregate(): pl.pallas_call(functools.partial(aggregate_kernel, first), grid=(steps,),...  24.2 us
    pallas_call x3, Pallas kernels, nodes_grad(): pl.pallas_call(nodes_grad_kernel, grid=(steps,), in_specs=[SMEM, rows_spe...  23.7 us
    pallas_call x2, Pallas kernels, wgrad(): pl.pallas_call(functools.partial(wgrad_kernel, other), grid_spec=pltpu.Pr...  23 us
    ppermute x19, starting transfers between devices, swap(): return lax.ppermute(value, AXES, [(i, i ^ bit) for i in range(32)])  20.8 us
    pallas_call x1, Pallas kernels, agg_grad(): pl.pallas_call(agg_grad_kernel, grid=(n // TILE,), in_specs=[SMEM, VMEM,...  19.8 us
    ppermute x19, waiting for transfers between devices, swap(): return lax.ppermute(value, AXES, [(i, i ^ bit) for i in range(32)])  19.6 us
    pallas_call x1, Pallas kernels, forward(): pl.pallas_call(functools.partial(forward_kernel, bool(part)), grid=(n //...  19.4 us
    pallas_call x2, Pallas kernels, neighbour_table(): pl.pallas_call(functools.partial(table_kernel, first), grid=(steps,), in_...  18.5 us
  transfers between devices with their start and end apart: 19, of which 8 were waited for; matrix products, arithmetic and copies ran while one was open for 1% of the time, Pallas kernels for 58%

profile of v3, /device:TPU:0, one launch (start us, length us, event | category | flops | bytes accessed | tf_op | source)
XLA Modules:
  0.0 197.0 jit_solution(17697168582352347930)
XLA Ops:
  2.5 3.1 %collective-permute-start.1 = (bf16[64,2176]{1,0:T(8,128)(2,1)S(1)}, bf16[64,2176]{1,0:T(8,128)(2,1)S(1)}, u32[]{:S(2)}, u32[]{:S(2)}) collective-permute-start(bf16[64,2176]{1,0:T(8,128)(2,1)S(1)} %pad_maximum_fusion.2), channel_id=1, source_target_pairs={{0,1},{1,0},{2,3},{3,2},{4,5},{5,4},{6,7},{7,6},{8,9},{9,8},{10,11... | collective-permute-start | bytes 835592 | tf_op jit(solution)/shard_map/ppermute | solution.py:372
  5.6 2.6 %collective-permute-start = (bf16[64,2176]{1,0:T(8,128)(2,1)S(1)}, bf16[64,2176]{1,0:T(8,128)(2,1)S(1)}, u32[]{:S(2)}, u32[]{:S(2)}) collective-permute-start(bf16[64,2176]{1,0:T(8,128)(2,1)S(1)} %pad_maximum_fusion.2), channel_id=1, source_target_pairs={{0,2},{1,3},{2,0},{3,1},{4,6},{5,7},{6,4},{7,5},{8,10},{9,11},{10,... | collective-permute-start | bytes 835592 | tf_op jit(solution)/shard_map/ppermute | solution.py:372
  10.5 13.0 %table.2 = (bf16[2048,2048]{1,0:T(8,128)(2,1)}, s32[2]{0:T(128)S(1)}) custom-call(s32[2]{0:T(128)S(1)} %pad_add_fusion.ctl, s32[16,2048]{1,0:T(8,128)S(1)} %bitcast.70, s32[1,2048]{1,0:T(1,128)S(1)} %bitcast.72), custom_call_target="tpu_custom_call" | custom-call | flops 6442450944 | bytes 6291456 | tf_op jit(solution)/shard_map/table/pallas_call | solution.py:78
  24.4 5.6 %table.3 = (bf16[2048,2048]{1,0:T(8,128)(2,1)}, s32[2]{0:T(128)S(1)}) custom-call(s32[2]{0:T(128)S(1)} %get-tuple-element.67.ctl, s32[16,2048]{1,0:T(8,128)S(1)} %bitcast.71, s32[1,2048]{1,0:T(1,128)S(1)} %bitcast.73, bf16[2048,2048]{1,0:T(8,128)(2,1)} %get-tuple-element.68.rest_0_), custom_call_target="tpu_custom_call", output_to_operand_aliasing={{0}: (3, {})} | custom-call | flops 2147483648 | bytes 2097152 | tf_op jit(solution)/shard_map/table/pallas_call | solution.py:78
  33.2 1.6 collective-permute-start.4
  34.8 9.6 %aggregate.2 = (bf16[2048,2048]{1,0:T(8,128)(2,1)}, s32[2]{0:T(128)S(1)}, bf16[2048,2048]{1,0:T(8,128)(2,1)}) custom-call(s32[2]{0:T(128)S(1)} %get-tuple-element.72.ctl, s32[1,2048]{1,0:T(1,128)S(1)} %bitcast.74, bf16[2048,2048]{1,0:T(8,128)(2,1)} %get-tuple-element.73.table, bf16[2048,2048]{1,0:T(8,128)(2,1)S(1)} %copy-done.4), custom_call_target="tpu_custom_call", output_to_operand_aliasing={{2}: (2, {})} | custom-call | flops 6442450944 | bytes 14680064 | tf_op jit(solution)/shard_map/aggregate/pallas_call | solution.py:127
  44.4 2.2 %collective-permute-done.4 = bf16[256,1152]{1,0:T(8,128)(2,1)S(1)} collective-permute-done((bf16[256,1152]{1,0:T(8,128)(2,1)S(1)}, bf16[256,1152]{1,0:T(8,128)(2,1)S(1)}, u32[]{:S(2)}, u32[]{:S(2)}) %collective-permute-start.4) | collective-permute-done | bytes 589856 | tf_op jit(solution)/shard_map/ppermute | solution.py:372
  49.4 14.6 %aggregate.3 = (bf16[2048,2048]{1,0:T(8,128)(2,1)}, s32[2]{0:T(128)S(1)}, bf16[2048,2048]{1,0:T(8,128)(2,1)}) custom-call(s32[2]{0:T(128)S(1)} %get-tuple-element.77.ctl, s32[1,2048]{1,0:T(1,128)S(1)} %bitcast.75, bf16[2048,2048]{1,0:T(8,128)(2,1)} %get-tuple-element.78.table, ...), custom_call_target="tpu_custom_call", output_to_operand_aliasing={{2}: (2, {}), {0}: (4, {})} | custom-call | flops 10737418240 | bytes 18874368 | tf_op jit(solution)/shard_map/aggregate/pallas_call | solution.py:127
  64.0 2.5 %place.2 = (bf16[2048,2048]{1,0:T(8,128)(2,1)S(1)}, f32[1,2048]{1,0:T(1,128)S(1)}, s32[2]{0:T(128)S(1)}) custom-call(s32[2]{0:T(128)S(1)} %get-tuple-element.80.ctl, bf16[512,1024]{1,0:T(8,128)(2,1)S(1)} %constant_dynamic-update-slice_fusion.refs_0_, bf16[512,1152]{1,0:T(8,128)(2,1)S(1)} %constant_dynamic-update-slice_fusion.5.refs_1_, ...), custom_call_target="tpu_custom_call" | custom-call | bytes 8388608 | tf_op jit(solution)/shard_map/place/pallas_call | solution.py:268
  66.6 13.9 %near.1 = (bf16[2048,2048]{1,0:T(8,128)(2,1)}, s32[2]{0:T(128)S(1)}, bf16[2048,2048]{1,0:T(8,128)(2,1)}) custom-call(s32[2]{0:T(128)S(1)} %get-tuple-element.81.ctl, bf16[2048,2048]{1,0:T(8,128)(2,1)} %get-tuple-element.82.agg, bf16[2048,2048]{1,0:T(8,128)(2,1)S(1)} %get-tuple-element.83.weight.refs_4_), custom_call_target="tpu_custom_call", output_to_operand_aliasing={{2}: (1, {})} | custom-call | flops 8589934592 | bytes 33554432 | tf_op jit(solution)/shard_map/near/pallas_call | solution.py:167
  81.0 3.8 %collective-permute-done.9.refs_2_ = bf16[512,1024]{1,0:T(8,128)(2,1)S(1)} collective-permute-done((bf16[512,1024]{1,0:T(8,128)(2,1)S(1)}, bf16[512,1024]{1,0:T(8,128)(2,1)S(1)}, u32[]{:S(2)}, u32[]{:S(2)}) %collective-permute-start.9) | collective-permute-done | bytes 1048608 | tf_op jit(solution)/shard_map/ppermute | solution.py:372
  84.8 2.5 %place.3 = (bf16[2048,2048]{1,0:T(8,128)(2,1)S(1)}, f32[1,2048]{1,0:T(1,128)S(1)}, s32[2]{0:T(128)S(1)}) custom-call(s32[2]{0:T(128)S(1)} %get-tuple-element.84.ctl, bf16[512,1024]{1,0:T(8,128)(2,1)S(1)} %collective-permute-done.7.refs_0_, bf16[512,1152]{1,0:T(8,128)(2,1)S(1)} %collective-permute-done.8.refs_1_, ...), custom_call_target="tpu_custom_call", output_to_operand_aliasing={{0}: (5, {})} | custom-call | bytes 8388608 | tf_op jit(solution)/shard_map/place/pallas_call | solution.py:268
  87.4 19.4 %forward.1 = (bf16[2048,2048]{1,0:T(8,128)(2,1)}, bf16[2048,2048]{1,0:T(8,128)(2,1)S(1)}, f32[1,2048]{1,0:T(1,128)S(1)}, s32[2]{0:T(128)S(1)}, bf16[2048,2048]{1,0:T(8,128)(2,1)}) custom-call(s32[2]{0:T(128)S(1)} %get-tuple-element.88.ctl, bf16[2048,2048]{1,0:T(8,128)(2,1)} %get-tuple-element.89.agg, ...), custom_call_target="tpu_custom_call", output_to_operand_aliasing={{4}: (1, {}), {0}: (5, {})} | custom-call | flops 17179869184 | bytes 41943040 | tf_op jit(solution)/shard_map/forward/pallas_call | solution.py:210
  106.8 11.4 %wgrad.2 = (bf16[4,256,2176]{2,1,0:T(8,128)(2,1)S(1)}, s32[2]{0:T(128)S(1)}, bf16[2048,2048]{1,0:T(8,128)(2,1)}) custom-call(s32[2]{0:T(128)S(1)} %get-tuple-element.94.ctl, bf16[2048,2048]{1,0:T(8,128)(2,1)} %get-tuple-element.95.agg, bf16[2048,2048]{1,0:T(8,128)(2,1)S(1)} %get-tuple-element.96.grad, ...), custom_call_target="tpu_custom_call", output_to_operand_aliasing={{2}: (1, {})} | custom-call | flops 8589934592 | bytes 16777216 | tf_op jit(solution)/shard_map/wgrad/pallas_call | solution.py:308
  118.4 11.6 %wgrad.3 = (bf16[4,256,2176]{2,1,0:T(8,128)(2,1)S(1)}, s32[2]{0:T(128)S(1)}, bf16[2048,2048]{1,0:T(8,128)(2,1)}) custom-call(s32[2]{0:T(128)S(1)} %get-tuple-element.98.ctl, bf16[2048,2048]{1,0:T(8,128)(2,1)} %get-tuple-element.99.agg, bf16[2048,2048]{1,0:T(8,128)(2,1)S(1)} %get-tuple-element.96.grad, ...), custom_call_target="tpu_custom_call", output_to_operand_aliasing={{2}: (1, {})} | custom-call | flops 8589934592 | bytes 16777216 | tf_op jit(solution)/shard_map/wgrad/pallas_call | solution.py:308
  132.7 19.8 %agg_grad.1 = (bf16[2048,2048]{1,0:T(8,128)(2,1)S(1)}, s32[2]{0:T(128)S(1)}) custom-call(s32[2]{0:T(128)S(1)} %get-tuple-element.104.ctl, s32[1,2048]{1,0:T(1,128)S(1)} %bitcast.76, bf16[2048,2048]{1,0:T(8,128)(2,1)S(1)} %get-tuple-element.96.grad, bf16[2048,2048]{1,0:T(8,128)(2,1)S(1)} %get-tuple-element.90.weight), custom_call_target="tpu_custom_call" | custom-call | flops 17179869184 | bytes 25165824 | tf_op jit(solution)/shard_map/agg_grad/pallas_call | solution.py:337
  152.5 3.6 %collective-permute-done.12 = bf16[2,256,1024]{2,1,0:T(8,128)(2,1)S(1)} collective-permute-done((bf16[2,256,1024]{2,1,0:T(8,128)(2,1)S(1)}, bf16[2,256,1024]{2,1,0:T(8,128)(2,1)S(1)}, u32[]{:S(2)}, u32[]{:S(2)}) %collective-permute-start.12) | collective-permute-done | bytes 1048608 | tf_op jit(solution)/shard_map/ppermute | solution.py:372
  157.9 1.9 collective-permute-done.13
  160.0 1.8 collective-permute-start.15
  161.8 8.7 %nodes_grad.3 = (bf16[2048,2048]{1,0:T(8,128)(2,1)}, s32[2]{0:T(128)S(1)}) custom-call(s32[2]{0:T(128)S(1)} %get-tuple-element.108.ctl, bf16[2048,2048]{1,0:T(8,128)(2,1)S(1)} %bitcast.63, bf16[2048,2048]{1,0:T(8,128)(2,1)S(1)} %get-tuple-element.110.spread), custom_call_target="tpu_custom_call" | custom-call | flops 6442450944 | bytes 14680064 | tf_op jit(solution)/shard_map/nodes_grad/pallas_call | solution.py:358
  170.8 3.1 %collective-permute-done.15 = bf16[256,1152]{1,0:T(8,128)(2,1)S(1)} collective-permute-done((bf16[256,1152]{1,0:T(8,128)(2,1)S(1)}, bf16[256,1152]{1,0:T(8,128)(2,1)S(1)}, u32[]{:S(2)}, u32[]{:S(2)}) %collective-permute-start.15) | collective-permute-done | bytes 589856 | tf_op jit(solution)/shard_map/ppermute | solution.py:372
  176.4 6.3 %nodes_grad.4 = (bf16[2048,2048]{1,0:T(8,128)(2,1)}, s32[2]{0:T(128)S(1)}) custom-call(s32[2]{0:T(128)S(1)} %get-tuple-element.114.ctl, bf16[2048,2048]{1,0:T(8,128)(2,1)S(1)} %bitcast.63, bf16[2048,2048]{1,0:T(8,128)(2,1)S(1)} %get-tuple-element.110.spread, bf16[2048,2048]{1,0:T(8,128)(2,1)} %get-tuple-element.115.rest_0_), custom_call_target="tpu_custom_call", output_to_operand_aliasing={{0}: (3, {})} | custom-call | flops 4294967296 | bytes 12582912 | tf_op jit(solution)/shard_map/nodes_grad/pallas_call | solution.py:358
  184.1 8.7 %nodes_grad.5 = (bf16[2048,2048]{1,0:T(8,128)(2,1)}, s32[2]{0:T(128)}) custom-call(s32[2]{0:T(128)S(1)} %get-tuple-element.118.ctl, bf16[2048,2048]{1,0:T(8,128)(2,1)S(1)} %bitcast.63, bf16[2048,2048]{1,0:T(8,128)(2,1)S(1)} %get-tuple-element.110.spread, bf16[2048,2048]{1,0:T(8,128)(2,1)} %get-tuple-element.119.rest_0_), custom_call_target="tpu_custom_call", output_to_operand_aliasing={{0}: (3, {})} | custom-call | flops 6442450944 | bytes 14680064 | tf_op jit(solution)/shard_map/nodes_grad/pallas_call | solution.py:358
  192.8 2.7 %collective-permute-done.18 = bf16[64,2176]{1,0:T(8,128)(2,1)S(1)} collective-permute-done((bf16[64,2176]{1,0:T(8,128)(2,1)S(1)}, bf16[64,2176]{1,0:T(8,128)(2,1)S(1)}, u32[]{:S(2)}, u32[]{:S(2)}) %collective-permute-start.18) | collective-permute-done | bytes 278560 | tf_op jit(solution)/shard_map/ppermute | solution.py:372
  (79 shorter events, 21.4 us)
Async XLA Ops:
  2.5 21.6 %collective-permute-start.1 = (bf16[64,2176]{1,0:T(8,128)(2,1)S(1)}, bf16[64,2176]{1,0:T(8,128)(2,1)S(1)}, u32[]{:S(2)}, u32[]{:S(2)}) collective-permute-start(bf16[64,2176]{1,0:T(8,128)(2,1)S(1)} %pad_maximum_fusion.2), channel_id=1, source_target_pairs={{0,1},{1,0},{2,3},{3,2},{4,5},{5,4},{6,7},{7,6},{8,9},{9,8},{10,11... | collective-permute-start | bytes 835592 | tf_op jit(solution)/shard_map/ppermute | solution.py:372
  5.6 18.0 %collective-permute-start = (bf16[64,2176]{1,0:T(8,128)(2,1)S(1)}, bf16[64,2176]{1,0:T(8,128)(2,1)S(1)}, u32[]{:S(2)}, u32[]{:S(2)}) collective-permute-start(bf16[64,2176]{1,0:T(8,128)(2,1)S(1)} %pad_maximum_fusion.2), channel_id=1, source_target_pairs={{0,2},{1,3},{2,0},{3,1},{4,6},{5,7},{6,4},{7,5},{8,10},{9,11},{10,... | collective-permute-start | bytes 835592 | tf_op jit(solution)/shard_map/ppermute | solution.py:372
  10.5 13.0 %copy-start.5 = (bf16[64,2048]{1,0:T(8,128)(2,1)S(1)}, bf16[64,2048]{1,0:T(8,128)(2,1)}, u32[]{:S(2)}) copy-start(bf16[64,2048]{1,0:T(8,128)(2,1)} %param.8) | copy-start | bytes 786436
  23.6 7.9 %collective-permute-start.2 = (bf16[64,2176]{1,0:T(8,128)(2,1)S(1)}, bf16[64,2176]{1,0:T(8,128)(2,1)S(1)}, u32[]{:S(2)}, u32[]{:S(2)}) collective-permute-start(bf16[64,2176]{1,0:T(8,128)(2,1)S(1)} %collective-permute-done), channel_id=1, source_target_pairs={{0,1},{1,0},{2,3},{3,2},{4,5},{5,4},{6,7},{7,6},{8,9},{9,8},{10,11... | collective-permute-start | bytes 835592 | tf_op jit(solution)/shard_map/ppermute | solution.py:372
  31.6 15.1 %collective-permute-start.3 = (bf16[256,1024]{1,0:T(8,128)(2,1)S(1)}, bf16[256,1024]{1,0:T(8,128)(2,1)S(1)}, u32[]{:S(2)}, u32[]{:S(2)}) collective-permute-start(bf16[256,1024]{1,0:T(8,128)(2,1)S(1)} %pad_maximum_fusion.1), channel_id=1, source_target_pairs={{0,8},{1,9},{2,10},{3,11},{4,12},{5,13},{6,14},{7,15},{8,0},{9,1},... | collective-permute-start | bytes 1572872 | tf_op jit(solution)/shard_map/ppermute | solution.py:372
  33.2 13.4 %collective-permute-start.4 = (bf16[256,1152]{1,0:T(8,128)(2,1)S(1)}, bf16[256,1152]{1,0:T(8,128)(2,1)S(1)}, u32[]{:S(2)}, u32[]{:S(2)}) collective-permute-start(bf16[256,1152]{1,0:T(8,128)(2,1)S(1)} %pad_maximum_fusion), channel_id=1, source_target_pairs={{0,16},{1,17},{2,18},{3,19},{4,20},{5,21},{6,22},{7,23},{8,24},{9,... | collective-permute-start | bytes 1769480 | tf_op jit(solution)/shard_map/ppermute | solution.py:372
  46.7 17.4 %collective-permute-start.6 = (bf16[512,1152]{1,0:T(8,128)(2,1)S(1)}, bf16[512,1152]{1,0:T(8,128)(2,1)S(1)}, u32[]{:S(2)}, u32[]{:S(2)}) collective-permute-start(bf16[512,1152]{1,0:T(8,128)(2,1)S(1)} %constant_dynamic-update-slice_fusion.5.refs_1_), channel_id=1, source_target_pairs={{0,4},{1,5},{2,6},{3,7},{4,0},{5,1},{6,2},{7,3},{8,12},{9,13},{10,... | collective-permute-start | bytes 3538952 | tf_op jit(solution)/shard_map/ppermute | solution.py:372
  46.8 17.2 %collective-permute-start.5 = (bf16[512,1024]{1,0:T(8,128)(2,1)S(1)}, bf16[512,1024]{1,0:T(8,128)(2,1)S(1)}, u32[]{:S(2)}, u32[]{:S(2)}) collective-permute-start(bf16[512,1024]{1,0:T(8,128)(2,1)S(1)} %constant_dynamic-update-slice_fusion.refs_0_), channel_id=1, source_target_pairs={{0,4},{1,5},{2,6},{3,7},{4,0},{5,1},{6,2},{7,3},{8,12},{9,13},{10,... | collective-permute-start | bytes 3145736 | tf_op jit(solution)/shard_map/ppermute | solution.py:372
  47.4 33.1 %collective-permute-start.7 = (bf16[512,1024]{1,0:T(8,128)(2,1)S(1)}, bf16[512,1024]{1,0:T(8,128)(2,1)S(1)}, u32[]{:S(2)}, u32[]{:S(2)}) collective-permute-start(bf16[512,1024]{1,0:T(8,128)(2,1)S(1)} %constant_dynamic-update-slice_fusion.refs_0_), channel_id=1, source_target_pairs={{0,16},{1,17},{2,18},{3,19},{4,20},{5,21},{6,22},{7,23},{8,24},{9,... | collective-permute-start | bytes 3145736 | tf_op jit(solution)/shard_map/ppermute | solution.py:372
  48.9 31.6 %collective-permute-start.8 = (bf16[512,1152]{1,0:T(8,128)(2,1)S(1)}, bf16[512,1152]{1,0:T(8,128)(2,1)S(1)}, u32[]{:S(2)}, u32[]{:S(2)}) collective-permute-start(bf16[512,1152]{1,0:T(8,128)(2,1)S(1)} %constant_dynamic-update-slice_fusion.5.refs_1_), channel_id=1, source_target_pairs={{0,8},{1,9},{2,10},{3,11},{4,12},{5,13},{6,14},{7,15},{8,0},{9,1},... | collective-permute-start | bytes 3538952 | tf_op jit(solution)/shard_map/ppermute | solution.py:372
  64.0 23.4 %slice-start.2 = ((s8[8388608]{0:T(1024)(128)(4,1)}), s8[4194304]{0:T(1024)(128)(4,1)S(1)}, s32[]{:S(2)}) async-start(s8[8388608]{0:T(1024)(128)(4,1)} %bitcast.77), calls=%async_computation.2 | async-start | bytes 8388608
  66.6 20.8 %slice-start.3 = ((s8[8388608]{0:T(1024)(128)(4,1)}), s8[4194304]{0:T(1024)(128)(4,1)S(1)}, s32[]{:S(2)}) async-start(s8[8388608]{0:T(1024)(128)(4,1)} %bitcast.77), calls=%async_computation.3 | async-start | bytes 8388608
  80.5 4.4 %collective-permute-start.10 = (bf16[512,1152]{1,0:T(8,128)(2,1)S(1)}, bf16[512,1152]{1,0:T(8,128)(2,1)S(1)}, u32[]{:S(2)}, u32[]{:S(2)}) collective-permute-start(bf16[512,1152]{1,0:T(8,128)(2,1)S(1)} %collective-permute-done.8.refs_1_), channel_id=1, source_target_pairs={{0,4},{1,5},{2,6},{3,7},{4,0},{5,1},{6,2},{7,3},{8,12},{9,13},{10,... | collective-permute-start | bytes 3538952 | tf_op jit(solution)/shard_map/ppermute | solution.py:372
  80.5 4.3 %collective-permute-start.9 = (bf16[512,1024]{1,0:T(8,128)(2,1)S(1)}, bf16[512,1024]{1,0:T(8,128)(2,1)S(1)}, u32[]{:S(2)}, u32[]{:S(2)}) collective-permute-start(bf16[512,1024]{1,0:T(8,128)(2,1)S(1)} %collective-permute-done.7.refs_0_), channel_id=1, source_target_pairs={{0,4},{1,5},{2,6},{3,7},{4,0},{5,1},{6,2},{7,3},{8,12},{9,13},{10,... | collective-permute-start | bytes 3145736 | tf_op jit(solution)/shard_map/ppermute | solution.py:372
  118.2 11.8 %collective-permute-start.11 = (bf16[4,256,2176]{2,1,0:T(8,128)(2,1)S(1)}, bf16[4,256,2176]{2,1,0:T(8,128)(2,1)S(1)}, u32[]{:S(2)}, u32[]{:S(2)}) collective-permute-start(bf16[4,256,2176]{2,1,0:T(8,128)(2,1)S(1)} %get-tuple-element.102), channel_id=1, source_target_pairs={{0,4},{1,5},{2,6},{3,7},{4,0},{5,1},{6,2},{7,3},{8,12},{9,13},{10,... | collective-permute-start | bytes 13369352 | tf_op jit(solution)/shard_map/ppermute | solution.py:372
  130.3 31.5 %slice-start = ((s8[8388608]{0:T(1024)(128)(4,1)}), s8[4194304]{0:T(1024)(128)(4,1)S(1)}, s32[]{:S(2)}) async-start(s8[8388608]{0:T(1024)(128)(4,1)} %bitcast.62), calls=%async_computation | async-start | bytes 8388608
  130.6 31.2 %slice-start.1 = ((s8[8388608]{0:T(1024)(128)(4,1)}), s8[4194304]{0:T(1024)(128)(4,1)S(1)}, s32[]{:S(2)}) async-start(s8[8388608]{0:T(1024)(128)(4,1)} %bitcast.62), calls=%async_computation.1 | async-start | bytes 8388608
  130.6 25.5 %collective-permute-start.12 = (bf16[2,256,1024]{2,1,0:T(8,128)(2,1)S(1)}, bf16[2,256,1024]{2,1,0:T(8,128)(2,1)S(1)}, u32[]{:S(2)}, u32[]{:S(2)}) collective-permute-start(bf16[2,256,1024]{2,1,0:T(8,128)(2,1)S(1)} %fusion.2), channel_id=1, source_target_pairs={{0,16},{1,17},{2,18},{3,19},{4,20},{5,21},{6,22},{7,23},{8,24},{9,... | collective-permute-start | bytes 3145736 | tf_op jit(solution)/shard_map/ppermute | solution.py:372
  131.2 28.6 %collective-permute-start.13 = (bf16[2,256,1152]{2,1,0:T(8,128)(2,1)S(1)}, bf16[2,256,1152]{2,1,0:T(8,128)(2,1)S(1)}, u32[]{:S(2)}, u32[]{:S(2)}) collective-permute-start(bf16[2,256,1152]{2,1,0:T(8,128)(2,1)S(1)} %fusion), channel_id=1, source_target_pairs={{0,8},{1,9},{2,10},{3,11},{4,12},{5,13},{6,14},{7,15},{8,0},{9,1},... | collective-permute-start | bytes 3538952 | tf_op jit(solution)/shard_map/ppermute | solution.py:372
  156.3 14.3 %collective-permute-start.14 = (bf16[256,1024]{1,0:T(8,128)(2,1)S(1)}, bf16[256,1024]{1,0:T(8,128)(2,1)S(1)}, u32[]{:S(2)}, u32[]{:S(2)}) collective-permute-start(bf16[256,1024]{1,0:T(8,128)(2,1)S(1)} %fusion.3), channel_id=1, source_target_pairs={{0,8},{1,9},{2,10},{3,11},{4,12},{5,13},{6,14},{7,15},{8,0},{9,1},... | collective-permute-start | bytes 1572872 | tf_op jit(solution)/shard_map/ppermute | solution.py:372
  160.0 13.9 %collective-permute-start.15 = (bf16[256,1152]{1,0:T(8,128)(2,1)S(1)}, bf16[256,1152]{1,0:T(8,128)(2,1)S(1)}, u32[]{:S(2)}, u32[]{:S(2)}) collective-permute-start(bf16[256,1152]{1,0:T(8,128)(2,1)S(1)} %fusion.1), channel_id=1, source_target_pairs={{0,16},{1,17},{2,18},{3,19},{4,20},{5,21},{6,22},{7,23},{8,24},{9,... | collective-permute-start | bytes 1769480 | tf_op jit(solution)/shard_map/ppermute | solution.py:372
  174.2 9.3 %collective-permute-start.16 = (bf16[64,2176]{1,0:T(8,128)(2,1)S(1)}, bf16[64,2176]{1,0:T(8,128)(2,1)S(1)}, u32[]{:S(2)}, u32[]{:S(2)}) collective-permute-start(bf16[64,2176]{1,0:T(8,128)(2,1)S(1)} %pad_maximum_fusion.3), channel_id=1, source_target_pairs={{0,1},{1,0},{2,3},{3,2},{4,5},{5,4},{6,7},{7,6},{8,9},{9,8},{10,11... | collective-permute-start | bytes 835592 | tf_op jit(solution)/shard_map/ppermute | solution.py:372
  174.9 17.9 %collective-permute-start.17 = (bf16[64,2176]{1,0:T(8,128)(2,1)S(1)}, bf16[64,2176]{1,0:T(8,128)(2,1)S(1)}, u32[]{:S(2)}, u32[]{:S(2)}) collective-permute-start(bf16[64,2176]{1,0:T(8,128)(2,1)S(1)} %pad_maximum_fusion.4), channel_id=1, source_target_pairs={{0,1},{1,0},{2,3},{3,2},{4,5},{5,4},{6,7},{7,6},{8,9},{9,8},{10,11... | collective-permute-start | bytes 835592 | tf_op jit(solution)/shard_map/ppermute | solution.py:372
  183.6 11.8 %collective-permute-start.18 = (bf16[64,2176]{1,0:T(8,128)(2,1)S(1)}, bf16[64,2176]{1,0:T(8,128)(2,1)S(1)}, u32[]{:S(2)}, u32[]{:S(2)}) collective-permute-start(bf16[64,2176]{1,0:T(8,128)(2,1)S(1)} %fusion.4), channel_id=1, source_target_pairs={{0,2},{1,3},{2,0},{3,1},{4,6},{5,7},{6,4},{7,5},{8,10},{9,11},{10,... | collective-permute-start | bytes 835592 | tf_op jit(solution)/shard_map/ppermute | solution.py:372
  (5 other events, 13.8 us)

commit v4 on v3

--- a/solution.py
+++ b/solution.py
@@ -40,57 +40,50 @@
     return live / (degree.astype(F32) + 1.0)
 
 
-def table_kernel(first, ctl, nb, deg, *rest):
-    table, ctl_out = rest[-2:]
-    hand_on(ctl, ctl_out)
-    n = table.shape[0]
+def table_kernel(ctl, nb, deg, table, ctl_out):
+    hand_on(ctl, ctl_out)
+    quarter = table.shape[0] // 4
     fan, tile = nb.shape
-    start = (pl.program_id(0) + first) * tile
-    chunk = 256
+    chunk = min(quarter, 128)
     used = lax.broadcasted_iota(jnp.int32, (fan, tile), 0) < deg[...]
-    slots = jnp.where(used, nb[...], -1)
-    targets = lax.broadcasted_iota(jnp.int32, (chunk, tile), 0).astype(F32).astype(BF16)
-    own = start + lax.broadcasted_iota(jnp.int32, (1, tile), 1)
-    one = jnp.ones((), BF16)
-    zero = jnp.zeros((), BF16)
-
-    def local(rows, base):
-        off = rows - base
-        off = jnp.where(jnp.logical_and(off >= 0, off < chunk), off, -1)
-        return off.astype(F32).astype(BF16)
+    slots = nb[...]
+    word = jnp.where(used, slots % quarter, -1)
+    value = jnp.left_shift(1, slots // quarter * 8)
+    own = pl.program_id(0) * tile + lax.broadcasted_iota(jnp.int32, (1, tile), 1)
+    own_word, own_value = own % quarter, jnp.left_shift(2, own // quarter * 8)
+    words = lax.broadcasted_iota(jnp.int32, (chunk, tile), 0)
 
     def build(c, carry):
         base = c * chunk
-        here = local(slots, base)
-        acc = jnp.where(targets == local(own, base), one + one, zero)
+        at = words + base
+        acc = jnp.where(at == own_word, own_value, 0)
         for k in range(fan):
-            acc = acc + jnp.where(targets == here[k : k + 1, :], one, zero)
-        table[pl.ds(pl.multiple_of(base, chunk), chunk), :] = acc
+            acc = acc + jnp.where(at == word[k : k + 1, :], value[k : k + 1, :], 0)
+        for part in range(4):
+            counts = jnp.bitwise_and(jnp.right_shift(acc, 8 * part), 255)
+            rows = pl.ds(pl.multiple_of(part * quarter + base, chunk), chunk)
+            table[rows, :] = counts.astype(F32).astype(BF16)
         return carry
 
-    lax.fori_loop(0, n // chunk, build, 0)
-
-
-def neighbour_table(ctl, nb, deg, first, steps, into=None):
+    lax.fori_loop(0, quarter // chunk, build, 0)
+
+
+def neighbour_table(ctl, nb, deg):
     fan, n = nb.shape
-    tile = n // 4
-    extra = [] if into is None else [into]
-    return pl.pallas_call(
-        functools.partial(table_kernel, first),
-        grid=(steps,),
+    return pl.pallas_call(
+        table_kernel,
+        grid=(n // TILE,),
         in_specs=[
             SMEM,
-            pl.BlockSpec((fan, tile), lambda t: (0, t + first)),
-            pl.BlockSpec((1, tile), lambda t: (0, t + first)),
-        ]
-        + [ANY] * len(extra),
-        out_specs=[pl.BlockSpec((n, tile), lambda t: (0, t + first)), SMEM],
+            pl.BlockSpec((fan, TILE), lambda t: (0, t)),
+            pl.BlockSpec((1, TILE), lambda t: (0, t)),
+        ],
+        out_specs=[pl.BlockSpec((n, TILE), lambda t: (0, t)), SMEM],
         out_shape=[pltpu.HBM((n, n), BF16), CTL],
-        input_output_aliases={3: 0} if extra else {},
         compiler_params=params(6),
-        cost_estimate=cost(n * n * tile * steps, n * tile * steps * 2),
+        cost_estimate=cost(n * n * n, n * n * 2),
         name="table",
-    )(ctl, nb, deg, *extra)
+    )(ctl, nb, deg)
 
 
 TILE = 256
@@ -295,32 +288,32 @@
         out[pl.ds(at, 16), m:] = jnp.where(head, pair, 0.0).astype(BF16)
 
 
-def wgrad_kernel(other, ctl, agg, grad, bias_sum, out, ctl_out, _):
-    hand_on(ctl, ctl_out)
-    tile = lax.bitwise_xor(ctl[0] // 4, 2 * pl.program_id(0) + other)
+def wgrad_kernel(code, ctl, agg, grad, bias_sum, out, ctl_out, _):
+    hand_on(ctl, ctl_out)
+    tile = lax.bitwise_xor(ctl[0] // 4, 2 * pl.program_id(0) + code)
     value = lax.dot_general(agg[...], grad[...], TN, preferred_element_type=F32)
     terms_of(ctl[0], tile, value, bias_sum, out.at[0])
 
 
-def wgrad(ctl, agg, grad, bias_sum, other):
+def wgrad(ctl, agg, grad, bias_sum, code, steps):
     n, d = agg.shape
     m = grad.shape[1]
     return pl.pallas_call(
-        functools.partial(wgrad_kernel, other),
+        functools.partial(wgrad_kernel, code),
         grid_spec=pltpu.PrefetchScalarGridSpec(
             num_scalar_prefetch=1,
-            grid=(4,),
+            grid=(steps,),
             in_specs=[
-                pl.BlockSpec((n, TILE), lambda t, ctl: (0, (ctl[0] // 4) ^ (2 * t + other))),
+                pl.BlockSpec((n, TILE), lambda t, ctl: (0, (ctl[0] // 4) ^ (2 * t + code))),
                 VMEM,
                 VMEM,
             ],
             out_specs=[pl.BlockSpec((1, TILE, m + EXTRA), lambda t, ctl: (t, 0, 0)), SMEM, ANY],
         ),
-        out_shape=[jax.ShapeDtypeStruct((4, TILE, m + EXTRA), BF16), CTL, pltpu.HBM((n, d), BF16)],
+        out_shape=[jax.ShapeDtypeStruct((steps, TILE, m + EXTRA), BF16), CTL, pltpu.HBM((n, d), BF16)],
         input_output_aliases={1: 2},
         compiler_params=params(8),
-        cost_estimate=cost(n * d * m, 2 * n * m * 2),
+        cost_estimate=cost(2 * n * TILE * steps * m, 2 * n * m * 2),
         name="wgrad",
     )(ctl, agg, grad, bias_sum)
 
@@ -408,20 +401,20 @@
     odd = me % 2 == 1
     own = with_bias(odd, weight, bias)
     one, two = swap(own, Z1), swap(own, Z2)
-    table, ctl = neighbour_table(after(ctl, own), nb, deg, 0, 3)
+    table, ctl = neighbour_table(after(ctl, own), nb, deg)
     one, two = after(one, ctl), after(two, ctl)
     three = swap(two, Z1)
-    table, ctl = neighbour_table(after(ctl, two), nb, deg, 3, 1, table)
+    agg, ctl, table = aggregate(after(ctl, two), deg, table, nodes, 0, 2)
     three = after(three, ctl)
     p = cat(own[:, :half], one[:, :half], two[:, :half], three[:, :half])
     q = cat(own[:, half:], one[:, half:], two[:, half:], three[:, half:])
     px, qy = swap(p, X), swap(q, Y)
-    agg, ctl, table = aggregate(after(ctl, p, q), deg, table, nodes, 0, 3)
+    agg, ctl, table = aggregate(after(ctl, p, q), deg, table, nodes, 2, 4, agg)
     px, qy = after(px, ctl), after(qy, ctl)
     p, q = cat(p, px), cat(q, qy)
     py, qx = swap(p, Y), swap(q, X)
     p_other, q_other = swap(p, CORE), swap(q, CORE)
-    agg, ctl, table = aggregate(after(ctl, p, q), deg, table, nodes, 3, steps - 3, agg)
+    agg, ctl, table = aggregate(after(ctl, p, q), deg, table, nodes, 6, steps - 6, agg)
     zs = (0, Z1, Z2, Z1 ^ Z2)
     near_p, near_q = codes_of(zs, (0, X)), codes_of(zs, (0, Y))
 
@@ -436,42 +429,44 @@
     full, bias_full, ctl = place(ctl, pieces, ends(Y, X), (32 * rows, m), full)
     act, grad, bias_sum, ctl, agg = forward(ctl, agg, full, bias_full, cotangent, part)
 
-    terms, ctl, agg = wgrad(ctl, agg, grad, bias_sum, 1)
+    terms, ctl, agg = wgrad(ctl, agg, grad, bias_sum, 1, 4)
     got = swap(terms, CORE)
-    mine, ctl, _ = wgrad(ctl, agg, grad, bias_sum, 0)
-    got = after(got, ctl).reshape(2, 2, 4 * rows, m + EXTRA)
-    mine = mine.reshape(2, 2, 4 * rows, m + EXTRA)
+    mine, ctl, agg = wgrad(ctl, agg, grad, bias_sum, 2, 3)
+    got = after(got, ctl)
 
     def total(*parts):
         return functools.reduce(jnp.add, [part.astype(F32) for part in parts])
 
-    send_p = total(mine[1, :, :, :half], got[1, :, :, :half]).astype(BF16)
-    send_q = total(mine[:, 1, :, half:], got[:, 1, :, half:]).astype(BF16)
+    send_p = total(mine[1:, :, :half], got[2:, :, :half]).astype(BF16)
+    send_q = total(mine[::2, :, half:], got[1::2, :, half:]).astype(BF16)
     got_p, got_q = swap(send_p, Y), swap(send_q, X)
-    spread, ctl = agg_grad(after(ctl, send_p, send_q), deg, grad, full)
+    kept, ctl, _ = wgrad(after(ctl, send_p, send_q), agg, grad, bias_sum, 0, 1)
+    spread, ctl = agg_grad(ctl, deg, grad, full)
     got_p, got_q = after(got_p, ctl), after(got_q, ctl)
-    next_p = total(mine[0, 1, :, :half], got[0, 1, :, :half], got_p[1]).astype(BF16)
-    next_q = total(mine[1, 0, :, half:], got[1, 0, :, half:], got_q[1]).astype(BF16)
+    next_p = total(mine[0, :, :half], got[1, :, :half], got_p[1]).astype(BF16)
+    next_q = total(mine[1, :, half:], got[2, :, half:], got_q[1]).astype(BF16)
     got2_p, got2_q = swap(next_p, X), swap(next_q, Y)
     out, ctl = nodes_grad(after(ctl, next_p, next_q), table, spread, 0, 3)
     got2_p, got2_q = after(got2_p, ctl), after(got2_q, ctl)
 
     def piece(i):
         at = slice(i * rows, (i + 1) * rows)
-        p = total(mine[0, 0, at, :half], got[0, 0, at, :half], got_p[0, at], got2_p[at])
-        q = total(mine[0, 0, at, half:], got[0, 0, at, half:], got_q[0, at], got2_q[at])
+        p = total(kept[0, at, :half], got[0, at, :half], got_p[0, at], got2_p[at])
+        q = total(kept[0, at, half:], got[0, at, half:], got_q[0, at], got2_q[at])
         return jnp.concatenate([p, q], axis=1)
 
     third, first = piece(3).astype(BF16), piece(1).astype(BF16)
-    far, near = swap(third, Z1), swap(first, Z1)
+    far = swap(third, Z1)
     out, ctl = nodes_grad(after(ctl, third, first), table, spread, 3, 2, out)
-    second = (piece(2) + after(far, ctl).astype(F32)).astype(BF16)
-    mid = swap(second, Z2)
+    far = after(far, ctl)
+    second = (piece(2) + far.astype(F32)).astype(BF16)
+    mid, near = swap(second, Z2), swap(after(first, far), Z1)
     out, ctl = nodes_grad(after(ctl, second), table, spread, 5, steps - 5, out)
     near, mid = after(near, ctl), after(mid, ctl)
-    last = piece(0) + near.astype(F32) + mid.astype(F32)
-    bias_grad = jnp.where(odd, last[0, m + rows :], last[0, m : m + rows])
-    return act, out, last[:, :m], bias_grad
+    own_rows = piece(0)
+    weight_grad = total(own_rows[:, :m], near[:, :m], mid[:, :m])
+    ends = total(own_rows[0, m:], near[0, m:], mid[0, m:])
+    return act, out, weight_grad, jnp.where(odd, ends[rows:], ends[:rows])
 
 
 def general(nodes, weight, bias, neighbours, degree, counts, cotangent):
@@ -481,7 +476,7 @@
     steps = nodes.shape[0] // TILE
     full = lax.all_gather(weight, AXES, axis=0, tiled=True)
     bias_full = lax.all_gather(bias, AXES, axis=0, tiled=True).astype(F32)[None, :]
-    table, _ = neighbour_table(ctl, nb, deg, 0, 4)
+    table, _ = neighbour_table(ctl, nb, deg)
     agg, _, table = aggregate(ctl, deg, table, nodes, 0, steps)
     act, grad, bias_sum, _, agg = forward(ctl, agg, full, bias_full, cotangent)
     term = lax.dot_general(agg, grad, TN, preferred_element_type=F32)

time: 198 us -> 190 us (0.960)
  waiting for transfers between devices: 19.6 us -> 16 us
  Pallas kernels: 148 us -> 145 us
    pallas_call x4, Pallas kernels: 41.6 us -> 36.9 us  [the longest x3 25.7 us: wgrad(): pl.pallas_call(functools.partial(wgrad_kernel, code), grid_spec=pltpu.Pre...]
    ppermute x19, waiting for transfers between devices: 19.6 us -> 16 us  [swap(): return lax.ppermute(value, AXES, [(i, i ^ bit) for i in range(32)])]
    pallas_call x2 -> x3, Pallas kernels: 24.2 us -> 26 us  [aggregate(): pl.pallas_call(functools.partial(aggregate_kernel, first), grid=(steps,),...]
  transfers between devices with their start and end apart: 19 -> 19, of which waited for: 8 -> 9; matrix products, arithmetic and copies ran while one was open for 1% -> 1% of each run, Pallas kernels for 58% -> 59%
where the time goes in v4:
time: 190 us
  Pallas kernels  145 us (76%)
  starting transfers between devices  20.1 us (11%)
  waiting for transfers between devices  16 us (8%)
  other arithmetic  5.31 us (3%)
  local copies, waits for them, and re-layouts  1.91 us (1%)
    pallas_call x3, Pallas kernels, aggregate(): pl.pallas_call(functools.partial(aggregate_kernel, first), grid=(steps,),...  26 us
    pallas_call x3, Pallas kernels, wgrad(): pl.pallas_call(functools.partial(wgrad_kernel, code), grid_spec=pltpu.Pre...  25.7 us
    pallas_call x3, Pallas kernels, nodes_grad(): pl.pallas_call(nodes_grad_kernel, grid=(steps,), in_specs=[SMEM, rows_spe...  23.8 us
    ppermute x19, starting transfers between devices, swap(): return lax.ppermute(value, AXES, [(i, i ^ bit) for i in range(32)])  20.1 us
    pallas_call x1, Pallas kernels, agg_grad(): pl.pallas_call(agg_grad_kernel, grid=(n // TILE,), in_specs=[SMEM, VMEM,...  19.8 us
    pallas_call x1, Pallas kernels, forward(): pl.pallas_call(functools.partial(forward_kernel, bool(part)), grid=(n //...  19.3 us
    ppermute x19, waiting for transfers between devices, swap(): return lax.ppermute(value, AXES, [(i, i ^ bit) for i in range(32)])  16 us
    pallas_call x1, Pallas kernels, near_product(): pl.pallas_call(near_kernel, grid=(n // TILE,), in_specs=[SMEM, rows_spec(...  13.9 us
  transfers between devices with their start and end apart: 19, of which 9 were waited for; matrix products, arithmetic and copies ran while one was open for 1% of the time, Pallas kernels for 59%

profile of v4, /device:TPU:0, one launch (start us, length us, event | category | flops | bytes accessed | tf_op | source)
XLA Modules:
  0.0 189.6 jit_solution(4339861769853832575)
XLA Ops:
  2.7 3.1 %collective-permute-start.1 = (bf16[64,2176]{1,0:T(8,128)(2,1)S(1)}, bf16[64,2176]{1,0:T(8,128)(2,1)S(1)}, u32[]{:S(2)}, u32[]{:S(2)}) collective-permute-start(bf16[64,2176]{1,0:T(8,128)(2,1)S(1)} %pad_maximum_fusion.3), channel_id=1, source_target_pairs={{0,1},{1,0},{2,3},{3,2},{4,5},{5,4},{6,7},{7,6},{8,9},{9,8},{10,11... | collective-permute-start | bytes 835592 | tf_op jit(solution)/shard_map/ppermute | solution.py:365
  5.8 2.6 %collective-permute-start = (bf16[64,2176]{1,0:T(8,128)(2,1)S(1)}, bf16[64,2176]{1,0:T(8,128)(2,1)S(1)}, u32[]{:S(2)}, u32[]{:S(2)}) collective-permute-start(bf16[64,2176]{1,0:T(8,128)(2,1)S(1)} %pad_maximum_fusion.3), channel_id=1, source_target_pairs={{0,2},{1,3},{2,0},{3,1},{4,6},{5,7},{6,4},{7,5},{8,10},{9,11},{10,... | collective-permute-start | bytes 835592 | tf_op jit(solution)/shard_map/ppermute | solution.py:365
  10.7 11.2 %table.1 = (bf16[2048,2048]{1,0:T(8,128)(2,1)}, s32[2]{0:T(128)S(1)}) custom-call(s32[2]{0:T(128)S(1)} %pad_add_fusion.ctl, s32[16,2048]{1,0:T(8,128)S(1)} %bitcast.45, s32[1,2048]{1,0:T(1,128)S(1)} %bitcast.38), custom_call_target="tpu_custom_call" | custom-call | flops 8589934592 | bytes 8388608 | tf_op jit(solution)/shard_map/table/pallas_call | solution.py:73
  22.6 7.0 %aggregate.3 = (bf16[2048,2048]{1,0:T(8,128)(2,1)}, s32[2]{0:T(128)S(1)}, bf16[2048,2048]{1,0:T(8,128)(2,1)}) custom-call(s32[2]{0:T(128)S(1)} %get-tuple-element.72.ctl, s32[1,2048]{1,0:T(1,128)S(1)} %bitcast.39, bf16[2048,2048]{1,0:T(8,128)(2,1)} %get-tuple-element.73.table, bf16[2048,2048]{1,0:T(8,128)(2,1)S(1)} %bitcast.37), custom_call_target="tpu_custom_call", output_to_operand_aliasing={{2}: (2, {})} | custom-call | flops 4294967296 | bytes 12582912 | tf_op jit(solution)/shard_map/aggregate/pallas_call | solution.py:120
  31.6 1.6 collective-permute-start.4
  33.2 11.9 %aggregate.4 = (bf16[2048,2048]{1,0:T(8,128)(2,1)}, s32[2]{0:T(128)S(1)}, bf16[2048,2048]{1,0:T(8,128)(2,1)}) custom-call(s32[2]{0:T(128)S(1)} %get-tuple-element.77.ctl, s32[1,2048]{1,0:T(1,128)S(1)} %bitcast.40, bf16[2048,2048]{1,0:T(8,128)(2,1)} %get-tuple-element.78.table, ...), custom_call_target="tpu_custom_call", output_to_operand_aliasing={{2}: (2, {}), {0}: (4, {})} | custom-call | flops 8589934592 | bytes 16777216 | tf_op jit(solution)/shard_map/aggregate/pallas_call | solution.py:120
  48.3 7.1 %aggregate.5 = (bf16[2048,2048]{1,0:T(8,128)(2,1)}, s32[2]{0:T(128)S(1)}, bf16[2048,2048]{1,0:T(8,128)(2,1)}) custom-call(s32[2]{0:T(128)S(1)} %get-tuple-element.83.ctl, s32[1,2048]{1,0:T(1,128)S(1)} %bitcast.41, bf16[2048,2048]{1,0:T(8,128)(2,1)} %get-tuple-element.84.table, ...), custom_call_target="tpu_custom_call", output_to_operand_aliasing={{2}: (2, {}), {0}: (4, {})} | custom-call | flops 4294967296 | bytes 12582912 | tf_op jit(solution)/shard_map/aggregate/pallas_call | solution.py:120
  55.4 2.5 %place.2 = (bf16[2048,2048]{1,0:T(8,128)(2,1)S(1)}, f32[1,2048]{1,0:T(1,128)S(1)}, s32[2]{0:T(128)S(1)}) custom-call(s32[2]{0:T(128)S(1)} %get-tuple-element.86.ctl, bf16[512,1024]{1,0:T(8,128)(2,1)S(1)} %constant_dynamic-update-slice_fusion.refs_0_, bf16[512,1152]{1,0:T(8,128)(2,1)S(1)} %constant_dynamic-update-slice_fusion.5.refs_1_, ...), custom_call_target="tpu_custom_call" | custom-call | bytes 8388608 | tf_op jit(solution)/shard_map/place/pallas_call | solution.py:261
  57.9 13.9 %near.1 = (bf16[2048,2048]{1,0:T(8,128)(2,1)}, s32[2]{0:T(128)S(1)}, bf16[2048,2048]{1,0:T(8,128)(2,1)}) custom-call(s32[2]{0:T(128)S(1)} %get-tuple-element.87.ctl, bf16[2048,2048]{1,0:T(8,128)(2,1)} %get-tuple-element.88.agg, bf16[2048,2048]{1,0:T(8,128)(2,1)S(1)} %get-tuple-element.89.weight.refs_4_), custom_call_target="tpu_custom_call", output_to_operand_aliasing={{2}: (1, {})} | custom-call | flops 8589934592 | bytes 33554432 | tf_op jit(solution)/shard_map/near/pallas_call | solution.py:160
  71.8 3.6 %collective-permute-done.8.refs_1_ = bf16[512,1152]{1,0:T(8,128)(2,1)S(1)} collective-permute-done((bf16[512,1152]{1,0:T(8,128)(2,1)S(1)}, bf16[512,1152]{1,0:T(8,128)(2,1)S(1)}, u32[]{:S(2)}, u32[]{:S(2)}) %collective-permute-start.8) | collective-permute-done | bytes 1179680 | tf_op jit(solution)/shard_map/ppermute | solution.py:365
  75.9 3.8 %collective-permute-done.9.refs_2_ = bf16[512,1024]{1,0:T(8,128)(2,1)S(1)} collective-permute-done((bf16[512,1024]{1,0:T(8,128)(2,1)S(1)}, bf16[512,1024]{1,0:T(8,128)(2,1)S(1)}, u32[]{:S(2)}, u32[]{:S(2)}) %collective-permute-start.9) | collective-permute-done | bytes 1048608 | tf_op jit(solution)/shard_map/ppermute | solution.py:365
  79.7 2.5 %place.3 = (bf16[2048,2048]{1,0:T(8,128)(2,1)S(1)}, f32[1,2048]{1,0:T(1,128)S(1)}, s32[2]{0:T(128)S(1)}) custom-call(s32[2]{0:T(128)S(1)} %get-tuple-element.90.ctl, bf16[512,1024]{1,0:T(8,128)(2,1)S(1)} %collective-permute-done.7.refs_0_, bf16[512,1152]{1,0:T(8,128)(2,1)S(1)} %collective-permute-done.8.refs_1_, ...), custom_call_target="tpu_custom_call", output_to_operand_aliasing={{0}: (5, {})} | custom-call | bytes 8388608 | tf_op jit(solution)/shard_map/place/pallas_call | solution.py:261
  82.3 19.3 %forward.1 = (bf16[2048,2048]{1,0:T(8,128)(2,1)}, bf16[2048,2048]{1,0:T(8,128)(2,1)S(1)}, f32[1,2048]{1,0:T(1,128)S(1)}, s32[2]{0:T(128)S(1)}, bf16[2048,2048]{1,0:T(8,128)(2,1)}) custom-call(s32[2]{0:T(128)S(1)} %get-tuple-element.94.ctl, bf16[2048,2048]{1,0:T(8,128)(2,1)} %get-tuple-element.95.agg, ...), custom_call_target="tpu_custom_call", output_to_operand_aliasing={{4}: (1, {}), {0}: (5, {})} | custom-call | flops 17179869184 | bytes 41943040 | tf_op jit(solution)/shard_map/forward/pallas_call | solution.py:203
  101.6 11.5 %wgrad.3 = (bf16[4,256,2176]{2,1,0:T(8,128)(2,1)S(1)}, s32[2]{0:T(128)S(1)}, bf16[2048,2048]{1,0:T(8,128)(2,1)}) custom-call(s32[2]{0:T(128)S(1)} %get-tuple-element.100.ctl, bf16[2048,2048]{1,0:T(8,128)(2,1)} %get-tuple-element.101.agg, bf16[2048,2048]{1,0:T(8,128)(2,1)S(1)} %get-tuple-element.102.grad, ...), custom_call_target="tpu_custom_call", output_to_operand_aliasing={{2}: (1, {})} | custom-call | flops 8589934592 | bytes 16777216 | tf_op jit(solution)/shard_map/wgrad/pallas_call | solution.py:301
  113.3 9.3 %wgrad.4 = (bf16[3,256,2176]{2,1,0:T(8,128)(2,1)S(1)}, s32[2]{0:T(128)S(1)}, bf16[2048,2048]{1,0:T(8,128)(2,1)}) custom-call(s32[2]{0:T(128)S(1)} %get-tuple-element.104.ctl, bf16[2048,2048]{1,0:T(8,128)(2,1)} %get-tuple-element.105.agg, bf16[2048,2048]{1,0:T(8,128)(2,1)S(1)} %get-tuple-element.102.grad, ...), custom_call_target="tpu_custom_call", output_to_operand_aliasing={{2}: (1, {})} | custom-call | flops 6442450944 | bytes 16777216 | tf_op jit(solution)/shard_map/wgrad/pallas_call | solution.py:301
  124.3 4.8 %wgrad.5 = (bf16[1,256,2176]{2,1,0:T(8,128)(2,1)S(1)}, s32[2]{0:T(128)S(1)}, bf16[2048,2048]{1,0:T(8,128)(2,1)}) custom-call(s32[2]{0:T(128)S(1)} %get-tuple-element.110.ctl, bf16[2048,2048]{1,0:T(8,128)(2,1)} %get-tuple-element.111.agg, bf16[2048,2048]{1,0:T(8,128)(2,1)S(1)} %get-tuple-element.102.grad, ...), custom_call_target="tpu_custom_call", output_to_operand_aliasing={{2}: (1, {})} | custom-call | flops 2147483648 | bytes 16777216 | tf_op jit(solution)/shard_map/wgrad/pallas_call | solution.py:301
  129.2 19.8 %agg_grad.1 = (bf16[2048,2048]{1,0:T(8,128)(2,1)S(1)}, s32[2]{0:T(128)S(1)}) custom-call(s32[2]{0:T(128)S(1)} %get-tuple-element.112.ctl, s32[1,2048]{1,0:T(1,128)S(1)} %bitcast.42, bf16[2048,2048]{1,0:T(8,128)(2,1)S(1)} %get-tuple-element.102.grad, bf16[2048,2048]{1,0:T(8,128)(2,1)S(1)} %get-tuple-element.96.weight), custom_call_target="tpu_custom_call" | custom-call | flops 17179869184 | bytes 25165824 | tf_op jit(solution)/shard_map/agg_grad/pallas_call | solution.py:330
  152.0 1.7 collective-permute-start.15
  153.7 8.7 %nodes_grad.3 = (bf16[2048,2048]{1,0:T(8,128)(2,1)}, s32[2]{0:T(128)S(1)}) custom-call(s32[2]{0:T(128)S(1)} %get-tuple-element.116.ctl, bf16[2048,2048]{1,0:T(8,128)(2,1)S(1)} %bitcast.35, bf16[2048,2048]{1,0:T(8,128)(2,1)S(1)} %get-tuple-element.118.spread), custom_call_target="tpu_custom_call" | custom-call | flops 6442450944 | bytes 14680064 | tf_op jit(solution)/shard_map/nodes_grad/pallas_call | solution.py:351
  163.2 3.2 %collective-permute-done.15 = bf16[256,1152]{1,0:T(8,128)(2,1)S(1)} collective-permute-done((bf16[256,1152]{1,0:T(8,128)(2,1)S(1)}, bf16[256,1152]{1,0:T(8,128)(2,1)S(1)}, u32[]{:S(2)}, u32[]{:S(2)}) %collective-permute-start.15) | collective-permute-done | bytes 589856 | tf_op jit(solution)/shard_map/ppermute | solution.py:365
  166.8 1.7 collective-permute-start.16
  168.4 6.3 %nodes_grad.4 = (bf16[2048,2048]{1,0:T(8,128)(2,1)}, s32[2]{0:T(128)S(1)}) custom-call(s32[2]{0:T(128)S(1)} %get-tuple-element.123.ctl, bf16[2048,2048]{1,0:T(8,128)(2,1)S(1)} %bitcast.35, bf16[2048,2048]{1,0:T(8,128)(2,1)S(1)} %get-tuple-element.118.spread, bf16[2048,2048]{1,0:T(8,128)(2,1)} %get-tuple-element.124.rest_0_), custom_call_target="tpu_custom_call", output_to_operand_aliasing={{0}: (3, {})} | custom-call | flops 4294967296 | bytes 12582912 | tf_op jit(solution)/shard_map/nodes_grad/pallas_call | solution.py:351
  176.2 8.7 %nodes_grad.5 = (bf16[2048,2048]{1,0:T(8,128)(2,1)}, s32[2]{0:T(128)}) custom-call(s32[2]{0:T(128)S(1)} %get-tuple-element.127.ctl, bf16[2048,2048]{1,0:T(8,128)(2,1)S(1)} %bitcast.35, bf16[2048,2048]{1,0:T(8,128)(2,1)S(1)} %get-tuple-element.118.spread, bf16[2048,2048]{1,0:T(8,128)(2,1)} %get-tuple-element.128.rest_0_), custom_call_target="tpu_custom_call", output_to_operand_aliasing={{0}: (3, {})} | custom-call | flops 6442450944 | bytes 14680064 | tf_op jit(solution)/shard_map/nodes_grad/pallas_call | solution.py:351
  185.3 2.9 %collective-permute-done.18 = bf16[64,2176]{1,0:T(8,128)(2,1)S(1)} collective-permute-done((bf16[64,2176]{1,0:T(8,128)(2,1)S(1)}, bf16[64,2176]{1,0:T(8,128)(2,1)S(1)}, u32[]{:S(2)}, u32[]{:S(2)}) %collective-permute-start.18) | collective-permute-done | bytes 278560 | tf_op jit(solution)/shard_map/ppermute | solution.py:365
  (81 shorter events, 19.3 us)
Async XLA Ops:
  1.6 21.0 %slice-start.2 = ((s8[8388608]{0:T(1024)(128)(4,1)}), s8[4194304]{0:T(1024)(128)(4,1)S(1)}, s32[]{:S(2)}) async-start(s8[8388608]{0:T(1024)(128)(4,1)} %bitcast.36), calls=%async_computation.2 | async-start | bytes 8388608
  2.7 19.8 %collective-permute-start.1 = (bf16[64,2176]{1,0:T(8,128)(2,1)S(1)}, bf16[64,2176]{1,0:T(8,128)(2,1)S(1)}, u32[]{:S(2)}, u32[]{:S(2)}) collective-permute-start(bf16[64,2176]{1,0:T(8,128)(2,1)S(1)} %pad_maximum_fusion.3), channel_id=1, source_target_pairs={{0,1},{1,0},{2,3},{3,2},{4,5},{5,4},{6,7},{7,6},{8,9},{9,8},{10,11... | collective-permute-start | bytes 835592 | tf_op jit(solution)/shard_map/ppermute | solution.py:365
  5.8 16.2 %collective-permute-start = (bf16[64,2176]{1,0:T(8,128)(2,1)S(1)}, bf16[64,2176]{1,0:T(8,128)(2,1)S(1)}, u32[]{:S(2)}, u32[]{:S(2)}) collective-permute-start(bf16[64,2176]{1,0:T(8,128)(2,1)S(1)} %pad_maximum_fusion.3), channel_id=1, source_target_pairs={{0,2},{1,3},{2,0},{3,1},{4,6},{5,7},{6,4},{7,5},{8,10},{9,11},{10,... | collective-permute-start | bytes 835592 | tf_op jit(solution)/shard_map/ppermute | solution.py:365
  22.0 7.9 %collective-permute-start.2 = (bf16[64,2176]{1,0:T(8,128)(2,1)S(1)}, bf16[64,2176]{1,0:T(8,128)(2,1)S(1)}, u32[]{:S(2)}, u32[]{:S(2)}) collective-permute-start(bf16[64,2176]{1,0:T(8,128)(2,1)S(1)} %collective-permute-done), channel_id=1, source_target_pairs={{0,1},{1,0},{2,3},{3,2},{4,5},{5,4},{6,7},{7,6},{8,9},{9,8},{10,11... | collective-permute-start | bytes 835592 | tf_op jit(solution)/shard_map/ppermute | solution.py:365
  30.0 15.6 %collective-permute-start.3 = (bf16[256,1024]{1,0:T(8,128)(2,1)S(1)}, bf16[256,1024]{1,0:T(8,128)(2,1)S(1)}, u32[]{:S(2)}, u32[]{:S(2)}) collective-permute-start(bf16[256,1024]{1,0:T(8,128)(2,1)S(1)} %pad_maximum_fusion.2), channel_id=1, source_target_pairs={{0,8},{1,9},{2,10},{3,11},{4,12},{5,13},{6,14},{7,15},{8,0},{9,1},... | collective-permute-start | bytes 1572872 | tf_op jit(solution)/shard_map/ppermute | solution.py:365
  31.6 13.8 %collective-permute-start.4 = (bf16[256,1152]{1,0:T(8,128)(2,1)S(1)}, bf16[256,1152]{1,0:T(8,128)(2,1)S(1)}, u32[]{:S(2)}, u32[]{:S(2)}) collective-permute-start(bf16[256,1152]{1,0:T(8,128)(2,1)S(1)} %pad_maximum_fusion), channel_id=1, source_target_pairs={{0,16},{1,17},{2,18},{3,19},{4,20},{5,21},{6,22},{7,23},{8,24},{9,... | collective-permute-start | bytes 1769480 | tf_op jit(solution)/shard_map/ppermute | solution.py:365
  45.5 9.8 %collective-permute-start.6 = (bf16[512,1152]{1,0:T(8,128)(2,1)S(1)}, bf16[512,1152]{1,0:T(8,128)(2,1)S(1)}, u32[]{:S(2)}, u32[]{:S(2)}) collective-permute-start(bf16[512,1152]{1,0:T(8,128)(2,1)S(1)} %constant_dynamic-update-slice_fusion.5.refs_1_), channel_id=1, source_target_pairs={{0,4},{1,5},{2,6},{3,7},{4,0},{5,1},{6,2},{7,3},{8,12},{9,13},{10,... | collective-permute-start | bytes 3538952 | tf_op jit(solution)/shard_map/ppermute | solution.py:365
  45.6 9.7 %collective-permute-start.5 = (bf16[512,1024]{1,0:T(8,128)(2,1)S(1)}, bf16[512,1024]{1,0:T(8,128)(2,1)S(1)}, u32[]{:S(2)}, u32[]{:S(2)}) collective-permute-start(bf16[512,1024]{1,0:T(8,128)(2,1)S(1)} %constant_dynamic-update-slice_fusion.refs_0_), channel_id=1, source_target_pairs={{0,4},{1,5},{2,6},{3,7},{4,0},{5,1},{6,2},{7,3},{8,12},{9,13},{10,... | collective-permute-start | bytes 3145736 | tf_op jit(solution)/shard_map/ppermute | solution.py:365
  46.2 29.2 %collective-permute-start.7 = (bf16[512,1024]{1,0:T(8,128)(2,1)S(1)}, bf16[512,1024]{1,0:T(8,128)(2,1)S(1)}, u32[]{:S(2)}, u32[]{:S(2)}) collective-permute-start(bf16[512,1024]{1,0:T(8,128)(2,1)S(1)} %constant_dynamic-update-slice_fusion.refs_0_), channel_id=1, source_target_pairs={{0,16},{1,17},{2,18},{3,19},{4,20},{5,21},{6,22},{7,23},{8,24},{9,... | collective-permute-start | bytes 3145736 | tf_op jit(solution)/shard_map/ppermute | solution.py:365
  47.7 27.7 %collective-permute-start.8 = (bf16[512,1152]{1,0:T(8,128)(2,1)S(1)}, bf16[512,1152]{1,0:T(8,128)(2,1)S(1)}, u32[]{:S(2)}, u32[]{:S(2)}) collective-permute-start(bf16[512,1152]{1,0:T(8,128)(2,1)S(1)} %constant_dynamic-update-slice_fusion.5.refs_1_), channel_id=1, source_target_pairs={{0,8},{1,9},{2,10},{3,11},{4,12},{5,13},{6,14},{7,15},{8,0},{9,1},... | collective-permute-start | bytes 3538952 | tf_op jit(solution)/shard_map/ppermute | solution.py:365
  55.4 26.9 %slice-start.4 = ((s8[8388608]{0:T(1024)(128)(4,1)}), s8[4194304]{0:T(1024)(128)(4,1)S(1)}, s32[]{:S(2)}) async-start(s8[8388608]{0:T(1024)(128)(4,1)} %bitcast.43), calls=%async_computation.4 | async-start | bytes 8388608
  57.9 24.4 %slice-start.5 = ((s8[8388608]{0:T(1024)(128)(4,1)}), s8[4194304]{0:T(1024)(128)(4,1)S(1)}, s32[]{:S(2)}) async-start(s8[8388608]{0:T(1024)(128)(4,1)} %bitcast.43), calls=%async_computation.5 | async-start | bytes 8388608
  75.4 4.4 %collective-permute-start.10 = (bf16[512,1152]{1,0:T(8,128)(2,1)S(1)}, bf16[512,1152]{1,0:T(8,128)(2,1)S(1)}, u32[]{:S(2)}, u32[]{:S(2)}) collective-permute-start(bf16[512,1152]{1,0:T(8,128)(2,1)S(1)} %collective-permute-done.8.refs_1_), channel_id=1, source_target_pairs={{0,4},{1,5},{2,6},{3,7},{4,0},{5,1},{6,2},{7,3},{8,12},{9,13},{10,... | collective-permute-start | bytes 3538952 | tf_op jit(solution)/shard_map/ppermute | solution.py:365
  75.4 4.3 %collective-permute-start.9 = (bf16[512,1024]{1,0:T(8,128)(2,1)S(1)}, bf16[512,1024]{1,0:T(8,128)(2,1)S(1)}, u32[]{:S(2)}, u32[]{:S(2)}) collective-permute-start(bf16[512,1024]{1,0:T(8,128)(2,1)S(1)} %collective-permute-done.7.refs_0_), channel_id=1, source_target_pairs={{0,4},{1,5},{2,6},{3,7},{4,0},{5,1},{6,2},{7,3},{8,12},{9,13},{10,... | collective-permute-start | bytes 3145736 | tf_op jit(solution)/shard_map/ppermute | solution.py:365
  113.1 9.6 %collective-permute-start.11 = (bf16[4,256,2176]{2,1,0:T(8,128)(2,1)S(1)}, bf16[4,256,2176]{2,1,0:T(8,128)(2,1)S(1)}, u32[]{:S(2)}, u32[]{:S(2)}) collective-permute-start(bf16[4,256,2176]{2,1,0:T(8,128)(2,1)S(1)} %get-tuple-element.108), channel_id=1, source_target_pairs={{0,4},{1,5},{2,6},{3,7},{4,0},{5,1},{6,2},{7,3},{8,12},{9,13},{10,... | collective-permute-start | bytes 13369352 | tf_op jit(solution)/shard_map/ppermute | solution.py:365
  123.2 25.7 %collective-permute-start.12 = (bf16[2,256,1024]{2,1,0:T(8,128)(2,1)S(1)}, bf16[2,256,1024]{2,1,0:T(8,128)(2,1)S(1)}, u32[]{:S(2)}, u32[]{:S(2)}) collective-permute-start(bf16[2,256,1024]{2,1,0:T(8,128)(2,1)S(1)} %add_convert_fusion.1), channel_id=1, source_target_pairs={{0,16},{1,17},{2,18},{3,19},{4,20},{5,21},{6,22},{7,23},{8,24},{9,... | collective-permute-start | bytes 3145736 | tf_op jit(solution)/shard_map/ppermute | solution.py:365
  123.8 27.9 %collective-permute-start.13 = (bf16[2,256,1152]{2,1,0:T(8,128)(2,1)S(1)}, bf16[2,256,1152]{2,1,0:T(8,128)(2,1)S(1)}, u32[]{:S(2)}, u32[]{:S(2)}) collective-permute-start(bf16[2,256,1152]{2,1,0:T(8,128)(2,1)S(1)} %add_convert_fusion), channel_id=1, source_target_pairs={{0,8},{1,9},{2,10},{3,11},{4,12},{5,13},{6,14},{7,15},{8,0},{9,1},... | collective-permute-start | bytes 3538952 | tf_op jit(solution)/shard_map/ppermute | solution.py:365
  124.3 29.3 %slice-start = ((s8[8388608]{0:T(1024)(128)(4,1)}), s8[4194304]{0:T(1024)(128)(4,1)S(1)}, s32[]{:S(2)}) async-start(s8[8388608]{0:T(1024)(128)(4,1)} %bitcast.34), calls=%async_computation | async-start | bytes 8388608
  129.2 24.5 %slice-start.1 = ((s8[8388608]{0:T(1024)(128)(4,1)}), s8[4194304]{0:T(1024)(128)(4,1)S(1)}, s32[]{:S(2)}) async-start(s8[8388608]{0:T(1024)(128)(4,1)} %bitcast.34), calls=%async_computation.1 | async-start | bytes 8388608
  149.2 13.8 %collective-permute-start.14 = (bf16[256,1024]{1,0:T(8,128)(2,1)S(1)}, bf16[256,1024]{1,0:T(8,128)(2,1)S(1)}, u32[]{:S(2)}, u32[]{:S(2)}) collective-permute-start(bf16[256,1024]{1,0:T(8,128)(2,1)S(1)} %fusion.2), channel_id=1, source_target_pairs={{0,8},{1,9},{2,10},{3,11},{4,12},{5,13},{6,14},{7,15},{8,0},{9,1},... | collective-permute-start | bytes 1572872 | tf_op jit(solution)/shard_map/ppermute | solution.py:365
  152.0 14.5 %collective-permute-start.15 = (bf16[256,1152]{1,0:T(8,128)(2,1)S(1)}, bf16[256,1152]{1,0:T(8,128)(2,1)S(1)}, u32[]{:S(2)}, u32[]{:S(2)}) collective-permute-start(bf16[256,1152]{1,0:T(8,128)(2,1)S(1)} %fusion), channel_id=1, source_target_pairs={{0,16},{1,17},{2,18},{3,19},{4,20},{5,21},{6,22},{7,23},{8,24},{9,... | collective-permute-start | bytes 1769480 | tf_op jit(solution)/shard_map/ppermute | solution.py:365
  166.8 8.0 %collective-permute-start.16 = (bf16[64,2176]{1,0:T(8,128)(2,1)S(1)}, bf16[64,2176]{1,0:T(8,128)(2,1)S(1)}, u32[]{:S(2)}, u32[]{:S(2)}) collective-permute-start(bf16[64,2176]{1,0:T(8,128)(2,1)S(1)} %pad_maximum_fusion.4), channel_id=1, source_target_pairs={{0,1},{1,0},{2,3},{3,2},{4,5},{5,4},{6,7},{7,6},{8,9},{9,8},{10,11... | collective-permute-start | bytes 835592 | tf_op jit(solution)/shard_map/ppermute | solution.py:365
  174.8 13.3 %collective-permute-start.18 = (bf16[64,2176]{1,0:T(8,128)(2,1)S(1)}, bf16[64,2176]{1,0:T(8,128)(2,1)S(1)}, u32[]{:S(2)}, u32[]{:S(2)}) collective-permute-start(bf16[64,2176]{1,0:T(8,128)(2,1)S(1)} %fusion.1), channel_id=1, source_target_pairs={{0,2},{1,3},{2,0},{3,1},{4,6},{5,7},{6,4},{7,5},{8,10},{9,11},{10,... | collective-permute-start | bytes 835592 | tf_op jit(solution)/shard_map/ppermute | solution.py:365
  175.2 10.1 %collective-permute-start.17 = (bf16[64,2176]{1,0:T(8,128)(2,1)S(1)}, bf16[64,2176]{1,0:T(8,128)(2,1)S(1)}, u32[]{:S(2)}, u32[]{:S(2)}) collective-permute-start(bf16[64,2176]{1,0:T(8,128)(2,1)S(1)} %pad_maximum_fusion.5), channel_id=1, source_target_pairs={{0,1},{1,0},{2,3},{3,2},{4,5},{5,4},{6,7},{7,6},{8,9},{9,8},{10,11... | collective-permute-start | bytes 835592 | tf_op jit(solution)/shard_map/ppermute | solution.py:365
  (5 other events, 36.6 us)

commit v5 on v4

--- a/solution.py
+++ b/solution.py
@@ -20,6 +20,7 @@
 VMEM = pl.BlockSpec(memory_space=pltpu.VMEM)
 HBM = pl.BlockSpec(memory_space=pltpu.HBM)
 EXTRA = 128
+HEAD = 16
 
 
 def params(mib=12):
@@ -40,15 +41,14 @@
     return live / (degree.astype(F32) + 1.0)
 
 
-def table_kernel(ctl, nb, deg, table, ctl_out):
+def table_kernel(ctl, used, table, ctl_out):
     hand_on(ctl, ctl_out)
     quarter = table.shape[0] // 4
-    fan, tile = nb.shape
+    fan, tile = used.shape
     chunk = min(quarter, 128)
-    used = lax.broadcasted_iota(jnp.int32, (fan, tile), 0) < deg[...]
-    slots = nb[...]
-    word = jnp.where(used, slots % quarter, -1)
-    value = jnp.left_shift(1, slots // quarter * 8)
+    slots = used[...]
+    word = jnp.where(slots >= 0, slots % quarter, -1)
+    value = jnp.left_shift(1, jnp.maximum(slots, 0) // quarter * 8)
     own = pl.program_id(0) * tile + lax.broadcasted_iota(jnp.int32, (1, tile), 1)
     own_word, own_value = own % quarter, jnp.left_shift(2, own // quarter * 8)
     words = lax.broadcasted_iota(jnp.int32, (chunk, tile), 0)
@@ -70,20 +70,20 @@
 
 def neighbour_table(ctl, nb, deg):
     fan, n = nb.shape
+    used = jnp.where(jnp.arange(fan, dtype=jnp.int32)[:, None] < deg, nb, -1)
     return pl.pallas_call(
         table_kernel,
         grid=(n // TILE,),
         in_specs=[
             SMEM,
             pl.BlockSpec((fan, TILE), lambda t: (0, t)),
-            pl.BlockSpec((1, TILE), lambda t: (0, t)),
         ],
         out_specs=[pl.BlockSpec((n, TILE), lambda t: (0, t)), SMEM],
         out_shape=[pltpu.HBM((n, n), BF16), CTL],
         compiler_params=params(6),
         cost_estimate=cost(n * n * n, n * n * 2),
         name="table",
-    )(ctl, nb, deg)
+    )(ctl, used)
 
 
 TILE = 256
@@ -223,40 +223,42 @@
     pieces, refs = refs[: len(codes)], refs[len(codes) :]
     weight, bias, ctl_out, heads, weight_sem, head_sem = refs[-6:]
     hand_on(ctl, ctl_out)
-    m = weight.shape[1]
+    half = weight.shape[1] // 2
+    rows = weight.shape[0] // 32
     copies, head_copies, pairs = [], [], []
-    for (order, col), piece in zip(codes, pieces):
-        rows = piece.shape[0] // len(order)
-        wide = min(piece.shape[1], m - col)
+    for (order, col, headed), piece in zip(codes, pieces):
+        group = 4 * rows + HEAD * headed
         for i, code in enumerate(order):
             owner = lax.bitwise_xor(ctl[0], code)
+            start = i // 4 * group + i % 4 * rows
             copies.append(
                 pltpu.make_async_copy(
-                    piece.at[pl.ds(i * rows, rows), pl.ds(0, wide)],
-                    weight.at[pl.ds(pl.multiple_of(owner * rows, rows), rows), pl.ds(col, wide)],
+                    piece.at[pl.ds(start, rows), :],
+                    weight.at[pl.ds(pl.multiple_of(owner * rows, rows), rows), pl.ds(col, half)],
                     weight_sem.at[len(copies)],
                 )
             )
-            if wide < piece.shape[1]:
-                head = piece.at[pl.ds(i * rows, 16), pl.ds(wide, EXTRA)]
+            if headed and i % 4 == 0:
                 k = len(head_copies)
+                head = piece.at[pl.ds(start + 4 * rows, HEAD), pl.ds(0, 4 * EXTRA)]
                 head_copies.append(pltpu.make_async_copy(head, heads.at[k], head_sem.at[k]))
-                if code & 1 == 0:
-                    pairs.append((k, order.index(code ^ 1) - i + k, owner // 2))
+            if headed and i % 2 == 0:
+                pairs.append((i % 4 * EXTRA, len(head_copies) - 1, owner // 2))
     for c in copies + head_copies:
         c.start()
     bias[...] = refs[1][...] if len(refs) == 8 else jnp.zeros_like(bias)
     for c in head_copies:
         c.wait()
-    for one, two, pair in pairs:
-        both = heads[one, :1, :].astype(F32) + heads[two, :1, :].astype(F32)
-        bias[:, pl.ds(pl.multiple_of(pair * EXTRA, EXTRA), EXTRA)] = both
+    for lane, k, pair in pairs:
+        one = heads[k, :1, lane : lane + EXTRA].astype(F32)
+        two = heads[k, :1, lane + EXTRA : lane + 2 * EXTRA].astype(F32)
+        bias[:, pl.ds(pl.multiple_of(pair * EXTRA, EXTRA), EXTRA)] = one + two
     for c in copies:
         c.wait()
 
 
 def place(ctl, pieces, codes, shape, into=()):
-    total = sum(len(order) for order, _ in codes)
+    total = sum(len(order) for order, _, _ in codes)
     first = 1 + len(pieces)
     return pl.pallas_call(
         functools.partial(place_kernel, codes),
@@ -265,9 +267,9 @@
         out_shape=[jax.ShapeDtypeStruct(shape, BF16), jax.ShapeDtypeStruct((1, shape[1]), F32), CTL],
         input_output_aliases={first: 0} if into else {},
         scratch_shapes=[
-            pltpu.VMEM((total // 2, 16, EXTRA), BF16),
+            pltpu.VMEM((total // 8, HEAD, 4 * EXTRA), BF16),
             pltpu.SemaphoreType.DMA((total,)),
-            pltpu.SemaphoreType.DMA((total // 2,)),
+            pltpu.SemaphoreType.DMA((total // 8,)),
         ],
         compiler_params=params(2),
         cost_estimate=cost(0, 2 * shape[0] * shape[1]),
@@ -276,16 +278,16 @@
 
 
 def terms_of(me, tile, value, bias_sum, out):
-    m = value.shape[1]
-    rows = value.shape[0] // 4
+    count, m = value.shape
+    rows = count // 4
     z = lax.rem(me, 4)
-    out[:, m:] = jnp.zeros((value.shape[0], EXTRA), BF16)
-    head = lax.broadcasted_iota(jnp.int32, (16, EXTRA), 0) == 0
+    out[count:, :] = jnp.zeros((HEAD, m), BF16)
+    top = lax.broadcasted_iota(jnp.int32, (HEAD, EXTRA), 0) == 0
     for q in range(4):
-        at = pl.multiple_of(lax.bitwise_xor(z, q) * rows, rows)
-        out[pl.ds(at, rows), :m] = value[q * rows : (q + 1) * rows, :].astype(BF16)
+        place = lax.bitwise_xor(z, q)
+        out[pl.ds(pl.multiple_of(place * rows, rows), rows), :] = value[q * rows : (q + 1) * rows, :].astype(BF16)
         pair = bias_sum[:, pl.ds(pl.multiple_of(tile * TILE + q // 2 * EXTRA, EXTRA), EXTRA)]
-        out[pl.ds(at, 16), m:] = jnp.where(head, pair, 0.0).astype(BF16)
+        out[count:, pl.ds(pl.multiple_of(place * EXTRA, EXTRA), EXTRA)] = jnp.where(top, pair, 0.0).astype(BF16)
 
 
 def wgrad_kernel(code, ctl, agg, grad, bias_sum, out, ctl_out, _):
@@ -308,9 +310,9 @@
                 VMEM,
                 VMEM,
             ],
-            out_specs=[pl.BlockSpec((1, TILE, m + EXTRA), lambda t, ctl: (t, 0, 0)), SMEM, ANY],
+            out_specs=[pl.BlockSpec((1, TILE + HEAD, m), lambda t, ctl: (t, 0, 0)), SMEM, ANY],
         ),
-        out_shape=[jax.ShapeDtypeStruct((steps, TILE, m + EXTRA), BF16), CTL, pltpu.HBM((n, d), BF16)],
+        out_shape=[jax.ShapeDtypeStruct((steps, TILE + HEAD, m), BF16), CTL, pltpu.HBM((n, d), BF16)],
         input_output_aliases={1: 2},
         compiler_params=params(8),
         cost_estimate=cost(2 * n * TILE * steps * m, 2 * n * m * 2),
@@ -345,20 +347,20 @@
     out[...] = jnp.dot(table[...], spread[...], preferred_element_type=F32).astype(BF16)
 
 
-def nodes_grad(ctl, table, spread, first, steps, into=None):
+def nodes_grad(ctl, table, spread, first, steps, into=None, behind=()):
     n, d = spread.shape
     extra = [] if into is None else [into]
     return pl.pallas_call(
         nodes_grad_kernel,
         grid=(steps,),
-        in_specs=[SMEM, rows_spec(n, first), VMEM] + [ANY] * len(extra),
+        in_specs=[SMEM, rows_spec(n, first), VMEM] + [ANY] * len((*extra, *behind)),
         out_specs=[rows_spec(d, first), SMEM],
         out_shape=[jax.ShapeDtypeStruct((n, d), BF16), CTL],
         input_output_aliases={3: 0} if extra else {},
         compiler_params=params(5),
         cost_estimate=cost(2 * steps * TILE * d * n, (n + 2 * steps * TILE) * d * 2),
         name="nodes_grad",
-    )(ctl, table, spread, *extra)
+    )(ctl, table, spread, *extra, *behind)
 
 
 def swap(value, bit):
@@ -406,8 +408,10 @@
     three = swap(two, Z1)
     agg, ctl, table = aggregate(after(ctl, two), deg, table, nodes, 0, 2)
     three = after(three, ctl)
-    p = cat(own[:, :half], one[:, :half], two[:, :half], three[:, :half])
-    q = cat(own[:, half:], one[:, half:], two[:, half:], three[:, half:])
+    heads = jnp.concatenate([own[:1, m:], one[:1, m:], two[:1, m:], three[:1, m:]], axis=1)
+    heads = jnp.pad(heads, ((0, HEAD - 1), (0, half - 4 * EXTRA)))
+    p = cat(own[:, :half], one[:, :half], two[:, :half], three[:, :half], heads)
+    q = cat(own[:, half:m], one[:, half:m], two[:, half:m], three[:, half:m])
     px, qy = swap(p, X), swap(q, Y)
     agg, ctl, table = aggregate(after(ctl, p, q), deg, table, nodes, 2, 4, agg)
     px, qy = after(px, ctl), after(qy, ctl)
@@ -420,13 +424,17 @@
 
     def ends(flip_p, flip_q):
         order_p, order_q = [c ^ flip_p for c in near_p], [c ^ flip_q for c in near_q]
-        return (order_p, 0), (order_q, half), ([c ^ CORE for c in order_p], 0), ([c ^ CORE for c in order_q], half)
+        mine = (order_p, 0, True), (order_q, half, False)
+        return *mine, *[([c ^ CORE for c in order], col, headed) for order, col, headed in mine]
 
     *full, ctl = place(ctl, (p, q, p_other, q_other), ends(0, 0), (32 * rows, m))
     part, ctl, agg = near_product(ctl, agg, full[0])
     py, qx = after(py, ctl), after(qx, ctl)
-    pieces = (py, qx, swap(py, CORE), swap(qx, CORE))
-    full, bias_full, ctl = place(ctl, pieces, ends(Y, X), (32 * rows, m), full)
+    py_other, qx_other = swap(py, CORE), swap(qx, CORE)
+    far = ends(Y, X)
+    *full, ctl = place(ctl, (py, qx), far[:2], (32 * rows, m), full)
+    py_other, qx_other = after(py_other, ctl), after(qx_other, ctl)
+    full, bias_full, ctl = place(ctl, (py_other, qx_other), far[2:], (32 * rows, m), full)
     act, grad, bias_sum, ctl, agg = forward(ctl, agg, full, bias_full, cotangent, part)
 
     terms, ctl, agg = wgrad(ctl, agg, grad, bias_sum, 1, 4)
@@ -438,30 +446,34 @@
         return functools.reduce(jnp.add, [part.astype(F32) for part in parts])
 
     send_p = total(mine[1:, :, :half], got[2:, :, :half]).astype(BF16)
-    send_q = total(mine[::2, :, half:], got[1::2, :, half:]).astype(BF16)
+    send_q = total(mine[::2, :TILE, half:], got[1::2, :TILE, half:]).astype(BF16)
     got_p, got_q = swap(send_p, Y), swap(send_q, X)
     kept, ctl, _ = wgrad(after(ctl, send_p, send_q), agg, grad, bias_sum, 0, 1)
     spread, ctl = agg_grad(ctl, deg, grad, full)
     got_p, got_q = after(got_p, ctl), after(got_q, ctl)
+    last = 3 * rows
     next_p = total(mine[0, :, :half], got[1, :, :half], got_p[1]).astype(BF16)
-    next_q = total(mine[1, :, half:], got[2, :, half:], got_q[1]).astype(BF16)
-    got2_p, got2_q = swap(next_p, X), swap(next_q, Y)
-    out, ctl = nodes_grad(after(ctl, next_p, next_q), table, spread, 0, 3)
-    got2_p, got2_q = after(got2_p, ctl), after(got2_q, ctl)
+    next_q = total(mine[1, :TILE, half:], got[2, :TILE, half:], got_q[1]).astype(BF16)
+    sends = next_p[last:], next_q[last:], next_p[:last], next_q[:last]
+    early_p, early_q, late_p, late_q = [swap(part, bit) for part, bit in zip(sends, (X, Y, X, Y))]
+    out, ctl = nodes_grad(ctl, table, spread, 0, 2, behind=sends)
+    early_p, early_q = after(early_p, ctl), after(early_q, ctl)
 
     def piece(i):
-        at = slice(i * rows, (i + 1) * rows)
-        p = total(kept[0, at, :half], got[0, at, :half], got_p[0, at], got2_p[at])
-        q = total(kept[0, at, half:], got[0, at, half:], got_q[0, at], got2_q[at])
-        return jnp.concatenate([p, q], axis=1)
-
-    third, first = piece(3).astype(BF16), piece(1).astype(BF16)
+        at, head, lanes = slice(i * rows, (i + 1) * rows), slice(TILE, TILE + 1), slice(i * EXTRA, (i + 1) * EXTRA)
+        more_p, more_q = (early_p[:rows], early_q) if i == 3 else (late_p[at], late_q[at])
+        p = total(kept[0, at, :half], got[0, at, :half], got_p[0, at], more_p)
+        q = total(kept[0, at, half:], got[0, at, half:], got_q[0, at], more_q)
+        ends = total(kept[0, head, lanes], got[0, head, lanes], got_p[0, head, lanes], early_p[rows : rows + 1, lanes])
+        return jnp.concatenate([p, q, jnp.pad(ends, ((0, rows - 1), (0, 0)))], axis=1)
+
+    third = piece(3).astype(BF16)
     far = swap(third, Z1)
-    out, ctl = nodes_grad(after(ctl, third, first), table, spread, 3, 2, out)
-    far = after(far, ctl)
-    second = (piece(2) + far.astype(F32)).astype(BF16)
-    mid, near = swap(second, Z2), swap(after(first, far), Z1)
-    out, ctl = nodes_grad(after(ctl, second), table, spread, 5, steps - 5, out)
+    out, ctl = nodes_grad(ctl, table, spread, 2, 2, out, behind=(third,))
+    far, late_p, late_q = after(far, ctl), after(late_p, ctl), after(late_q, ctl)
+    second, first = (piece(2) + far.astype(F32)).astype(BF16), piece(1).astype(BF16)
+    mid, near = swap(second, Z2), swap(first, Z1)
+    out, ctl = nodes_grad(ctl, table, spread, 4, steps - 4, out, behind=(second, first))
     near, mid = after(near, ctl), after(mid, ctl)
     own_rows = piece(0)
     weight_grad = total(own_rows[:, :m], near[:, :m], mid[:, :m])

time: 190 us -> 182 us (0.958)
  waiting for transfers between devices: 16 us -> 5.65 us
    ppermute x19 -> x21, waiting for transfers between devices: 16 us -> 5.65 us  [swap(): return lax.ppermute(value, AXES, [(i, i ^ bit) for i in range(32)])]
    ppermute x19 -> x21, starting transfers between devices: 20.1 us -> 21.9 us  [swap(): return lax.ppermute(value, AXES, [(i, i ^ bit) for i in range(32)])]
    pallas_call x2 -> x3, Pallas kernels: 5.08 us -> 5.95 us  [place(): pl.pallas_call(functools.partial(place_kernel, codes), in_specs=[SMEM] +...]
  transfers between devices with their start and end apart: 19 -> 21, of which waited for: 9 -> 4; matrix products, arithmetic and copies ran while one was open for 1% -> 1% of each run, Pallas kernels for 59% -> 62%
where the time goes in v5:
time: 182 us; the launch traced here: 181 us
  Pallas kernels  144 us (79%)
  starting transfers between devices  21.9 us (12%)
  other arithmetic  6.76 us (4%)
  waiting for transfers between devices  5.65 us (3%)
    pallas_call x3, Pallas kernels, aggregate(): pl.pallas_call(functools.partial(aggregate_kernel, first), grid=(steps,),...  26 us
    pallas_call x3, Pallas kernels, wgrad(): pl.pallas_call(functools.partial(wgrad_kernel, code), grid_spec=pltpu.Pre...  25 us
    pallas_call x3, Pallas kernels, nodes_grad(): pl.pallas_call(nodes_grad_kernel, grid=(steps,), in_specs=[SMEM, rows_spe...  23.4 us
    ppermute x21, starting transfers between devices, swap(): return lax.ppermute(value, AXES, [(i, i ^ bit) for i in range(32)])  21.9 us
    pallas_call x1, Pallas kernels, agg_grad(): pl.pallas_call(agg_grad_kernel, grid=(n // TILE,), in_specs=[SMEM, VMEM,...  19.7 us
    pallas_call x1, Pallas kernels, forward(): pl.pallas_call(functools.partial(forward_kernel, bool(part)), grid=(n //...  19.2 us
    pallas_call x1, Pallas kernels, near_product(): pl.pallas_call(near_kernel, grid=(n // TILE,), in_specs=[SMEM, rows_spec(...  13.7 us
    pallas_call x1, Pallas kernels, neighbour_table(): pl.pallas_call(table_kernel, grid=(n // TILE,), in_specs=[SMEM, pl.BlockS...  11.3 us
  transfers between devices with their start and end apart: 21, of which 4 were waited for; matrix products, arithmetic and copies ran while one was open for 1% of the time, Pallas kernels for 62%

profile of v5, /device:TPU:0, one launch (start us, length us, event | category | flops | bytes accessed | tf_op | source)
XLA Modules:
  0.0 181.0 jit_solution(14400686281188246085)
XLA Ops:
  2.7 3.1 %collective-permute-start.1 = (bf16[64,2176]{1,0:T(8,128)(2,1)S(1)}, bf16[64,2176]{1,0:T(8,128)(2,1)S(1)}, u32[]{:S(2)}, u32[]{:S(2)}) collective-permute-start(bf16[64,2176]{1,0:T(8,128)(2,1)S(1)} %pad_maximum_fusion.1), channel_id=1, source_target_pairs={{0,1},{1,0},{2,3},{3,2},{4,5},{5,4},{6,7},{7,6},{8,9},{9,8},{10,11... | collective-permute-start | bytes 835592 | tf_op jit(solution)/shard_map/ppermute | solution.py:367
  5.8 2.6 %collective-permute-start = (bf16[64,2176]{1,0:T(8,128)(2,1)S(1)}, bf16[64,2176]{1,0:T(8,128)(2,1)S(1)}, u32[]{:S(2)}, u32[]{:S(2)}) collective-permute-start(bf16[64,2176]{1,0:T(8,128)(2,1)S(1)} %pad_maximum_fusion.1), channel_id=1, source_target_pairs={{0,2},{1,3},{2,0},{3,1},{4,6},{5,7},{6,4},{7,5},{8,10},{9,11},{10,... | collective-permute-start | bytes 835592 | tf_op jit(solution)/shard_map/ppermute | solution.py:367
  10.1 11.3 %table.1 = (bf16[2048,2048]{1,0:T(8,128)(2,1)}, s32[2]{0:T(128)S(1)}) custom-call(s32[2]{0:T(128)S(1)} %pad_add_fusion.ctl, s32[16,2048]{1,0:T(8,128)S(1)} %bitcast_select_fusion.used), custom_call_target="tpu_custom_call" | custom-call | flops 8589934592 | bytes 8388608 | tf_op jit(solution)/shard_map/table/pallas_call | solution.py:74
  22.0 7.0 %aggregate.3 = (bf16[2048,2048]{1,0:T(8,128)(2,1)}, s32[2]{0:T(128)S(1)}, bf16[2048,2048]{1,0:T(8,128)(2,1)}) custom-call(s32[2]{0:T(128)S(1)} %get-tuple-element.75.ctl, s32[1,2048]{1,0:T(1,128)S(1)} %bitcast.59, bf16[2048,2048]{1,0:T(8,128)(2,1)} %get-tuple-element.76.table, bf16[2048,2048]{1,0:T(8,128)(2,1)S(1)} %bitcast.58), custom_call_target="tpu_custom_call", output_to_operand_aliasing={{2}: (2, {})} | custom-call | flops 4294967296 | bytes 12582912 | tf_op jit(solution)/shard_map/aggregate/pallas_call | solution.py:120
  29.4 1.6 collective-permute-start.4
  32.6 11.9 %aggregate.4 = (bf16[2048,2048]{1,0:T(8,128)(2,1)}, s32[2]{0:T(128)S(1)}, bf16[2048,2048]{1,0:T(8,128)(2,1)}) custom-call(s32[2]{0:T(128)S(1)} %get-tuple-element.80.ctl, s32[1,2048]{1,0:T(1,128)S(1)} %bitcast.60, bf16[2048,2048]{1,0:T(8,128)(2,1)} %get-tuple-element.81.table, ...), custom_call_target="tpu_custom_call", output_to_operand_aliasing={{2}: (2, {}), {0}: (4, {})} | custom-call | flops 8589934592 | bytes 16777216 | tf_op jit(solution)/shard_map/aggregate/pallas_call | solution.py:120
  46.9 7.1 %aggregate.5 = (bf16[2048,2048]{1,0:T(8,128)(2,1)}, s32[2]{0:T(128)S(1)}, bf16[2048,2048]{1,0:T(8,128)(2,1)}) custom-call(s32[2]{0:T(128)S(1)} %get-tuple-element.86.ctl, s32[1,2048]{1,0:T(1,128)S(1)} %bitcast.61, bf16[2048,2048]{1,0:T(8,128)(2,1)} %get-tuple-element.87.table, ...), custom_call_target="tpu_custom_call", output_to_operand_aliasing={{2}: (2, {}), {0}: (4, {})} | custom-call | flops 4294967296 | bytes 12582912 | tf_op jit(solution)/shard_map/aggregate/pallas_call | solution.py:120
  54.0 2.5 %place.3 = (bf16[2048,2048]{1,0:T(8,128)(2,1)S(1)}, f32[1,2048]{1,0:T(1,128)S(1)}, s32[2]{0:T(128)S(1)}) custom-call(s32[2]{0:T(128)S(1)} %get-tuple-element.89.ctl, bf16[544,1024]{1,0:T(8,128)(2,1)S(1)} %constant_dynamic-update-slice_fusion.1.refs_0_, bf16[512,1024]{1,0:T(8,128)(2,1)S(1)} %constant_dynamic-update-slice_fusion.3.refs_1_, ...), custom_call_target="tpu_custom_call" | custom-call | bytes 8388608 | tf_op jit(solution)/shard_map/place/pallas_call | solution.py:263
  56.5 13.7 %near.1 = (bf16[2048,2048]{1,0:T(8,128)(2,1)}, s32[2]{0:T(128)S(1)}, bf16[2048,2048]{1,0:T(8,128)(2,1)}) custom-call(s32[2]{0:T(128)S(1)} %get-tuple-element.90.ctl, bf16[2048,2048]{1,0:T(8,128)(2,1)} %get-tuple-element.91.agg, bf16[2048,2048]{1,0:T(8,128)(2,1)S(1)} %get-tuple-element.92.weight.refs_2_), custom_call_target="tpu_custom_call", output_to_operand_aliasing={{2}: (1, {})} | custom-call | flops 8589934592 | bytes 33554432 | tf_op jit(solution)/shard_map/near/pallas_call | solution.py:160
  70.1 2.5 %collective-permute-done.7.refs_0_ = bf16[544,1024]{1,0:T(8,128)(2,1)S(1)} collective-permute-done((bf16[544,1024]{1,0:T(8,128)(2,1)S(1)}, bf16[544,1024]{1,0:T(8,128)(2,1)S(1)}, u32[]{:S(2)}, u32[]{:S(2)}) %collective-permute-start.7) | collective-permute-done | bytes 1114144 | tf_op jit(solution)/shard_map/ppermute | solution.py:367
  73.2 1.7 place.4
  74.9 2.0 %collective-permute-done.10.refs_1_ = bf16[512,1024]{1,0:T(8,128)(2,1)S(1)} collective-permute-done((bf16[512,1024]{1,0:T(8,128)(2,1)S(1)}, bf16[512,1024]{1,0:T(8,128)(2,1)S(1)}, u32[]{:S(2)}, u32[]{:S(2)}) %collective-permute-start.10) | collective-permute-done | bytes 1048608 | tf_op jit(solution)/shard_map/ppermute | solution.py:367
  76.9 1.7 place.5
  79.1 19.2 %forward.1 = (bf16[2048,2048]{1,0:T(8,128)(2,1)}, bf16[2048,2048]{1,0:T(8,128)(2,1)S(1)}, f32[1,2048]{1,0:T(1,128)S(1)}, s32[2]{0:T(128)S(1)}, bf16[2048,2048]{1,0:T(8,128)(2,1)}) custom-call(s32[2]{0:T(128)S(1)} %get-tuple-element.102.ctl, bf16[2048,2048]{1,0:T(8,128)(2,1)} %get-tuple-element.103.agg, ...), custom_call_target="tpu_custom_call", output_to_operand_aliasing={{4}: (1, {}), {0}: (5, {})} | custom-call | flops 17179869184 | bytes 41943040 | tf_op jit(solution)/shard_map/forward/pallas_call | solution.py:203
  98.3 11.4 %wgrad.3 = (bf16[4,272,2048]{2,1,0:T(8,128)(2,1)S(1)}, s32[2]{0:T(128)S(1)}, bf16[2048,2048]{1,0:T(8,128)(2,1)}) custom-call(s32[2]{0:T(128)S(1)} %get-tuple-element.108.ctl, bf16[2048,2048]{1,0:T(8,128)(2,1)} %get-tuple-element.109.agg, bf16[2048,2048]{1,0:T(8,128)(2,1)S(1)} %get-tuple-element.110.grad, ...), custom_call_target="tpu_custom_call", output_to_operand_aliasing={{2}: (1, {})} | custom-call | flops 8589934592 | bytes 16777216 | tf_op jit(solution)/shard_map/wgrad/pallas_call | solution.py:303
  109.9 9.2 %wgrad.4 = (bf16[3,272,2048]{2,1,0:T(8,128)(2,1)S(1)}, s32[2]{0:T(128)S(1)}, bf16[2048,2048]{1,0:T(8,128)(2,1)}) custom-call(s32[2]{0:T(128)S(1)} %get-tuple-element.112.ctl, bf16[2048,2048]{1,0:T(8,128)(2,1)} %get-tuple-element.113.agg, bf16[2048,2048]{1,0:T(8,128)(2,1)S(1)} %get-tuple-element.110.grad, ...), custom_call_target="tpu_custom_call", output_to_operand_aliasing={{2}: (1, {})} | custom-call | flops 6442450944 | bytes 16777216 | tf_op jit(solution)/shard_map/wgrad/pallas_call | solution.py:303
  121.3 4.5 %wgrad.5 = (bf16[1,272,2048]{2,1,0:T(8,128)(2,1)S(1)}, s32[2]{0:T(128)S(1)}, bf16[2048,2048]{1,0:T(8,128)(2,1)}) custom-call(s32[2]{0:T(128)S(1)} %get-tuple-element.118.ctl, bf16[2048,2048]{1,0:T(8,128)(2,1)} %get-tuple-element.119.agg, bf16[2048,2048]{1,0:T(8,128)(2,1)S(1)} %get-tuple-element.110.grad, ...), custom_call_target="tpu_custom_call", output_to_operand_aliasing={{2}: (1, {})} | custom-call | flops 2147483648 | bytes 16777216 | tf_op jit(solution)/shard_map/wgrad/pallas_call | solution.py:303
  125.8 19.7 %agg_grad.1 = (bf16[2048,2048]{1,0:T(8,128)(2,1)S(1)}, s32[2]{0:T(128)S(1)}) custom-call(s32[2]{0:T(128)S(1)} %get-tuple-element.120.ctl, s32[1,2048]{1,0:T(1,128)S(1)} %bitcast.62, bf16[2048,2048]{1,0:T(8,128)(2,1)S(1)} %get-tuple-element.110.grad, bf16[2048,2048]{1,0:T(8,128)(2,1)S(1)} %get-tuple-element.104.weight), custom_call_target="tpu_custom_call" | custom-call | flops 17179869184 | bytes 25165824 | tf_op jit(solution)/shard_map/agg_grad/pallas_call | solution.py:332
  145.8 1.6 collective-permute-start.15
  150.4 6.2 %nodes_grad.3 = (bf16[2048,2048]{1,0:T(8,128)(2,1)}, s32[2]{0:T(128)S(1)}) custom-call(s32[2]{0:T(128)S(1)} %get-tuple-element.121.ctl, bf16[2048,2048]{1,0:T(8,128)(2,1)S(1)} %bitcast.56, bf16[2048,2048]{1,0:T(8,128)(2,1)S(1)} %get-tuple-element.123.spread, bf16[80,1024]{1,0:T(8,128)(2,1)S(1)} %slice_bitcast_fusion.2.rest_0_, ...), custom_call_target="tpu_custom_call" | custom-call | flops 4294967296 | bytes 12582912 | tf_op jit(solution)/shard_map/nodes_grad/pallas_call | solution.py:353
  156.9 1.6 collective-permute-start.18
  158.5 6.2 %nodes_grad.4 = (bf16[2048,2048]{1,0:T(8,128)(2,1)}, s32[2]{0:T(128)S(1)}) custom-call(s32[2]{0:T(128)S(1)} %get-tuple-element.126.ctl, bf16[2048,2048]{1,0:T(8,128)(2,1)S(1)} %bitcast.56, bf16[2048,2048]{1,0:T(8,128)(2,1)S(1)} %get-tuple-element.123.spread, bf16[2048,2048]{1,0:T(8,128)(2,1)} %get-tuple-element.127.rest_0_, ...), custom_call_target="tpu_custom_call", output_to_operand_aliasing={{0}: (3, {})} | custom-call | flops 4294967296 | bytes 12582912 | tf_op jit(solution)/shard_map/nodes_grad/pallas_call | solution.py:353
  165.9 1.8 %collective-permute-start.20 = (bf16[64,2176]{1,0:T(8,128)(2,1)S(1)}, bf16[64,2176]{1,0:T(8,128)(2,1)S(1)}, u32[]{:S(2)}, u32[]{:S(2)}) collective-permute-start(bf16[64,2176]{1,0:T(8,128)(2,1)S(1)} %fusion.1.rest_1_), channel_id=1, source_target_pairs={{0,2},{1,3},{2,0},{3,1},{4,6},{5,7},{6,4},{7,5},{8,10},{9,11},{10,... | collective-permute-start | bytes 835592 | tf_op jit(solution)/shard_map/ppermute | solution.py:367
  167.7 10.9 %nodes_grad.5 = (bf16[2048,2048]{1,0:T(8,128)(2,1)}, s32[2]{0:T(128)}) custom-call(s32[2]{0:T(128)S(1)} %get-tuple-element.131.ctl, bf16[2048,2048]{1,0:T(8,128)(2,1)S(1)} %bitcast.56, bf16[2048,2048]{1,0:T(8,128)(2,1)S(1)} %get-tuple-element.123.spread, bf16[2048,2048]{1,0:T(8,128)(2,1)} %get-tuple-element.132.rest_0_, ...), custom_call_target="tpu_custom_call", output_to_operand_aliasing={{0}: (3, {})} | custom-call | flops 8589934592 | bytes 16777216 | tf_op jit(solution)/shard_map/nodes_grad/pallas_call | solution.py:353
  (89 shorter events, 18.4 us)
Async XLA Ops:
  1.6 20.4 %slice-start.2 = ((s8[8388608]{0:T(1024)(128)(4,1)}), s8[4194304]{0:T(1024)(128)(4,1)S(1)}, s32[]{:S(2)}) async-start(s8[8388608]{0:T(1024)(128)(4,1)} %bitcast.57), calls=%async_computation.2 | async-start | bytes 8388608
  2.7 19.2 %collective-permute-start.1 = (bf16[64,2176]{1,0:T(8,128)(2,1)S(1)}, bf16[64,2176]{1,0:T(8,128)(2,1)S(1)}, u32[]{:S(2)}, u32[]{:S(2)}) collective-permute-start(bf16[64,2176]{1,0:T(8,128)(2,1)S(1)} %pad_maximum_fusion.1), channel_id=1, source_target_pairs={{0,1},{1,0},{2,3},{3,2},{4,5},{5,4},{6,7},{7,6},{8,9},{9,8},{10,11... | collective-permute-start | bytes 835592 | tf_op jit(solution)/shard_map/ppermute | solution.py:367
  5.8 15.6 %collective-permute-start = (bf16[64,2176]{1,0:T(8,128)(2,1)S(1)}, bf16[64,2176]{1,0:T(8,128)(2,1)S(1)}, u32[]{:S(2)}, u32[]{:S(2)}) collective-permute-start(bf16[64,2176]{1,0:T(8,128)(2,1)S(1)} %pad_maximum_fusion.1), channel_id=1, source_target_pairs={{0,2},{1,3},{2,0},{3,1},{4,6},{5,7},{6,4},{7,5},{8,10},{9,11},{10,... | collective-permute-start | bytes 835592 | tf_op jit(solution)/shard_map/ppermute | solution.py:367
  21.4 7.9 %collective-permute-start.2 = (bf16[64,2176]{1,0:T(8,128)(2,1)S(1)}, bf16[64,2176]{1,0:T(8,128)(2,1)S(1)}, u32[]{:S(2)}, u32[]{:S(2)}) collective-permute-start(bf16[64,2176]{1,0:T(8,128)(2,1)S(1)} %collective-permute-done), channel_id=1, source_target_pairs={{0,1},{1,0},{2,3},{3,2},{4,5},{5,4},{6,7},{7,6},{8,9},{9,8},{10,11... | collective-permute-start | bytes 835592 | tf_op jit(solution)/shard_map/ppermute | solution.py:367
  29.4 15.0 %collective-permute-start.4 = (bf16[256,1024]{1,0:T(8,128)(2,1)S(1)}, bf16[256,1024]{1,0:T(8,128)(2,1)S(1)}, u32[]{:S(2)}, u32[]{:S(2)}) collective-permute-start(bf16[256,1024]{1,0:T(8,128)(2,1)S(1)} %pad_maximum_fusion), channel_id=1, source_target_pairs={{0,16},{1,17},{2,18},{3,19},{4,20},{5,21},{6,22},{7,23},{8,24},{9,... | collective-permute-start | bytes 1572872 | tf_op jit(solution)/shard_map/ppermute | solution.py:367
  31.0 13.4 %collective-permute-start.3 = (bf16[272,1024]{1,0:T(8,128)(2,1)S(1)}, bf16[272,1024]{1,0:T(8,128)(2,1)S(1)}, u32[]{:S(2)}, u32[]{:S(2)}) collective-permute-start(bf16[272,1024]{1,0:T(8,128)(2,1)S(1)} %get-tuple-element.168), channel_id=1, source_target_pairs={{0,8},{1,9},{2,10},{3,11},{4,12},{5,13},{6,14},{7,15},{8,0},{9,1},... | collective-permute-start | bytes 1671176 | tf_op jit(solution)/shard_map/ppermute | solution.py:367
  44.5 9.5 %collective-permute-start.5 = (bf16[544,1024]{1,0:T(8,128)(2,1)S(1)}, bf16[544,1024]{1,0:T(8,128)(2,1)S(1)}, u32[]{:S(2)}, u32[]{:S(2)}) collective-permute-start(bf16[544,1024]{1,0:T(8,128)(2,1)S(1)} %constant_dynamic-update-slice_fusion.1.refs_0_), channel_id=1, source_target_pairs={{0,4},{1,5},{2,6},{3,7},{4,0},{5,1},{6,2},{7,3},{8,12},{9,13},{10,... | collective-permute-start | bytes 3342344 | tf_op jit(solution)/shard_map/ppermute | solution.py:367
  44.6 9.4 %collective-permute-start.6 = (bf16[512,1024]{1,0:T(8,128)(2,1)S(1)}, bf16[512,1024]{1,0:T(8,128)(2,1)S(1)}, u32[]{:S(2)}, u32[]{:S(2)}) collective-permute-start(bf16[512,1024]{1,0:T(8,128)(2,1)S(1)} %constant_dynamic-update-slice_fusion.3.refs_1_), channel_id=1, source_target_pairs={{0,4},{1,5},{2,6},{3,7},{4,0},{5,1},{6,2},{7,3},{8,12},{9,13},{10,... | collective-permute-start | bytes 3145736 | tf_op jit(solution)/shard_map/ppermute | solution.py:367
  45.2 27.5 %collective-permute-start.8 = (bf16[512,1024]{1,0:T(8,128)(2,1)S(1)}, bf16[512,1024]{1,0:T(8,128)(2,1)S(1)}, u32[]{:S(2)}, u32[]{:S(2)}) collective-permute-start(bf16[512,1024]{1,0:T(8,128)(2,1)S(1)} %constant_dynamic-update-slice_fusion.3.refs_1_), channel_id=1, source_target_pairs={{0,8},{1,9},{2,10},{3,11},{4,12},{5,13},{6,14},{7,15},{8,0},{9,1},... | collective-permute-start | bytes 3145736 | tf_op jit(solution)/shard_map/ppermute | solution.py:367
  46.4 26.3 %collective-permute-start.7 = (bf16[544,1024]{1,0:T(8,128)(2,1)S(1)}, bf16[544,1024]{1,0:T(8,128)(2,1)S(1)}, u32[]{:S(2)}, u32[]{:S(2)}) collective-permute-start(bf16[544,1024]{1,0:T(8,128)(2,1)S(1)} %constant_dynamic-update-slice_fusion.1.refs_0_), channel_id=1, source_target_pairs={{0,16},{1,17},{2,18},{3,19},{4,20},{5,21},{6,22},{7,23},{8,24},{9,... | collective-permute-start | bytes 3342344 | tf_op jit(solution)/shard_map/ppermute | solution.py:367
  72.6 4.3 %collective-permute-start.9 = (bf16[544,1024]{1,0:T(8,128)(2,1)S(1)}, bf16[544,1024]{1,0:T(8,128)(2,1)S(1)}, u32[]{:S(2)}, u32[]{:S(2)}) collective-permute-start(bf16[544,1024]{1,0:T(8,128)(2,1)S(1)} %collective-permute-done.7.refs_0_), channel_id=1, source_target_pairs={{0,4},{1,5},{2,6},{3,7},{4,0},{5,1},{6,2},{7,3},{8,12},{9,13},{10,... | collective-permute-start | bytes 3342344 | tf_op jit(solution)/shard_map/ppermute | solution.py:367
  72.7 4.2 %collective-permute-start.10 = (bf16[512,1024]{1,0:T(8,128)(2,1)S(1)}, bf16[512,1024]{1,0:T(8,128)(2,1)S(1)}, u32[]{:S(2)}, u32[]{:S(2)}) collective-permute-start(bf16[512,1024]{1,0:T(8,128)(2,1)S(1)} %collective-permute-done.8.refs_1_), channel_id=1, source_target_pairs={{0,4},{1,5},{2,6},{3,7},{4,0},{5,1},{6,2},{7,3},{8,12},{9,13},{10,... | collective-permute-start | bytes 3145736 | tf_op jit(solution)/shard_map/ppermute | solution.py:367
  109.7 9.4 %collective-permute-start.11 = (bf16[4,272,2048]{2,1,0:T(8,128)(2,1)S(1)}, bf16[4,272,2048]{2,1,0:T(8,128)(2,1)S(1)}, u32[]{:S(2)}, u32[]{:S(2)}) collective-permute-start(bf16[4,272,2048]{2,1,0:T(8,128)(2,1)S(1)} %get-tuple-element.116), channel_id=1, source_target_pairs={{0,4},{1,5},{2,6},{3,7},{4,0},{5,1},{6,2},{7,3},{8,12},{9,13},{10,... | collective-permute-start | bytes 13369352 | tf_op jit(solution)/shard_map/ppermute | solution.py:367
  120.0 25.5 %collective-permute-start.13 = (bf16[2,256,1024]{2,1,0:T(8,128)(2,1)S(1)}, bf16[2,256,1024]{2,1,0:T(8,128)(2,1)S(1)}, u32[]{:S(2)}, u32[]{:S(2)}) collective-permute-start(bf16[2,256,1024]{2,1,0:T(8,128)(2,1)S(1)} %add_convert_fusion.1), channel_id=1, source_target_pairs={{0,8},{1,9},{2,10},{3,11},{4,12},{5,13},{6,14},{7,15},{8,0},{9,1},... | collective-permute-start | bytes 3145736 | tf_op jit(solution)/shard_map/ppermute | solution.py:367
  120.8 27.2 %collective-permute-start.12 = (bf16[2,272,1024]{2,1,0:T(8,128)(2,1)S(1)}, bf16[2,272,1024]{2,1,0:T(8,128)(2,1)S(1)}, u32[]{:S(2)}, u32[]{:S(2)}) collective-permute-start(bf16[2,272,1024]{2,1,0:T(8,128)(2,1)S(1)} %add_convert_fusion), channel_id=1, source_target_pairs={{0,16},{1,17},{2,18},{3,19},{4,20},{5,21},{6,22},{7,23},{8,24},{9,... | collective-permute-start | bytes 3342344 | tf_op jit(solution)/shard_map/ppermute | solution.py:367
  125.8 24.7 %slice-start = ((s8[8388608]{0:T(1024)(128)(4,1)}), s8[4194304]{0:T(1024)(128)(4,1)S(1)}, s32[]{:S(2)}) async-start(s8[8388608]{0:T(1024)(128)(4,1)} %bitcast.55), calls=%async_computation | async-start | bytes 8388608
  125.8 24.6 %slice-start.1 = ((s8[8388608]{0:T(1024)(128)(4,1)}), s8[4194304]{0:T(1024)(128)(4,1)S(1)}, s32[]{:S(2)}) async-start(s8[8388608]{0:T(1024)(128)(4,1)} %bitcast.55), calls=%async_computation.1 | async-start | bytes 8388608
  145.8 10.9 %collective-permute-start.15 = (bf16[64,1024]{1,0:T(8,128)(2,1)S(1)}, bf16[64,1024]{1,0:T(8,128)(2,1)S(1)}, u32[]{:S(2)}, u32[]{:S(2)}) collective-permute-start(bf16[64,1024]{1,0:T(8,128)(2,1)S(1)} %slice_bitcast_fusion.3.rest_1_), channel_id=1, source_target_pairs={{0,16},{1,17},{2,18},{3,19},{4,20},{5,21},{6,22},{7,23},{8,24},{9,... | collective-permute-start | bytes 393224 | tf_op jit(solution)/shard_map/ppermute | solution.py:367
  147.4 17.3 %collective-permute-start.17 = (bf16[192,1024]{1,0:T(8,128)(2,1)S(1)}, bf16[192,1024]{1,0:T(8,128)(2,1)S(1)}, u32[]{:S(2)}, u32[]{:S(2)}) collective-permute-start(bf16[192,1024]{1,0:T(8,128)(2,1)S(1)} %slice_bitcast_fusion.rest_3_), channel_id=1, source_target_pairs={{0,16},{1,17},{2,18},{3,19},{4,20},{5,21},{6,22},{7,23},{8,24},{9,... | collective-permute-start | bytes 1179656 | tf_op jit(solution)/shard_map/ppermute | solution.py:367
  148.3 8.3 %collective-permute-start.14 = (bf16[80,1024]{1,0:T(8,128)(2,1)S(1)}, bf16[80,1024]{1,0:T(8,128)(2,1)S(1)}, u32[]{:S(2)}, u32[]{:S(2)}) collective-permute-start(bf16[80,1024]{1,0:T(8,128)(2,1)S(1)} %slice_bitcast_fusion.2.rest_0_), channel_id=1, source_target_pairs={{0,8},{1,9},{2,10},{3,11},{4,12},{5,13},{6,14},{7,15},{8,0},{9,1},... | collective-permute-start | bytes 491528 | tf_op jit(solution)/shard_map/ppermute | solution.py:367
  149.7 15.3 %collective-permute-start.16 = (bf16[192,1024]{1,0:T(8,128)(2,1)S(1)}, bf16[192,1024]{1,0:T(8,128)(2,1)S(1)}, u32[]{:S(2)}, u32[]{:S(2)}) collective-permute-start(bf16[192,1024]{1,0:T(8,128)(2,1)S(1)} %slice_bitcast_fusion.1.rest_2_), channel_id=1, source_target_pairs={{0,8},{1,9},{2,10},{3,11},{4,12},{5,13},{6,14},{7,15},{8,0},{9,1},... | collective-permute-start | bytes 1179656 | tf_op jit(solution)/shard_map/ppermute | solution.py:367
  156.9 8.9 %collective-permute-start.18 = (bf16[64,2176]{1,0:T(8,128)(2,1)S(1)}, bf16[64,2176]{1,0:T(8,128)(2,1)S(1)}, u32[]{:S(2)}, u32[]{:S(2)}) collective-permute-start(bf16[64,2176]{1,0:T(8,128)(2,1)S(1)} %fusion.5.rest_1_), channel_id=1, source_target_pairs={{0,1},{1,0},{2,3},{3,2},{4,5},{5,4},{6,7},{7,6},{8,9},{9,8},{10,11... | collective-permute-start | bytes 835592 | tf_op jit(solution)/shard_map/ppermute | solution.py:367
  165.2 13.4 %collective-permute-start.19 = (bf16[64,2176]{1,0:T(8,128)(2,1)S(1)}, bf16[64,2176]{1,0:T(8,128)(2,1)S(1)}, u32[]{:S(2)}, u32[]{:S(2)}) collective-permute-start(bf16[64,2176]{1,0:T(8,128)(2,1)S(1)} %fusion.6.rest_2_), channel_id=1, source_target_pairs={{0,1},{1,0},{2,3},{3,2},{4,5},{5,4},{6,7},{7,6},{8,9},{9,8},{10,11... | collective-permute-start | bytes 835592 | tf_op jit(solution)/shard_map/ppermute | solution.py:367
  165.9 13.7 %collective-permute-start.20 = (bf16[64,2176]{1,0:T(8,128)(2,1)S(1)}, bf16[64,2176]{1,0:T(8,128)(2,1)S(1)}, u32[]{:S(2)}, u32[]{:S(2)}) collective-permute-start(bf16[64,2176]{1,0:T(8,128)(2,1)S(1)} %fusion.1.rest_1_), channel_id=1, source_target_pairs={{0,2},{1,3},{2,0},{3,1},{4,6},{5,7},{6,4},{7,5},{8,10},{9,11},{10,... | collective-permute-start | bytes 835592 | tf_op jit(solution)/shard_map/ppermute | solution.py:367
  (5 other events, 42.8 us)

commit v6 on v5

--- a/solution.py
+++ b/solution.py
@@ -181,8 +181,9 @@
     def _():
         bias_sum[...] = jnp.zeros_like(bias_sum)
 
-    slots = t * TILE + lax.broadcasted_iota(jnp.int32, (TILE, half), 0)
+    slots = t * TILE + lax.broadcasted_iota(jnp.int32, (TILE, EXTRA), 0)
     live = (slots < ctl[1]).astype(F32).astype(BF16)
+    live = jnp.concatenate([live] * (half // EXTRA), axis=1)
     for side, where in enumerate(halves(ctl, d, True)):
         at = slice(side * half, (side + 1) * half)
         if split:

time: 182 us -> 182 us (level)
  no operation moved by 1% of the time
where the time goes in v6:
time: 182 us; the launch traced here: 181 us
  Pallas kernels  144 us (79%)
  starting transfers between devices  21.9 us (12%)
  other arithmetic  6.76 us (4%)
  waiting for transfers between devices  5.64 us (3%)
    pallas_call x3, Pallas kernels, aggregate(): pl.pallas_call(functools.partial(aggregate_kernel, first), grid=(steps,),...  26 us
    pallas_call x3, Pallas kernels, wgrad(): pl.pallas_call(functools.partial(wgrad_kernel, code), grid_spec=pltpu.Pre...  25 us
    pallas_call x3, Pallas kernels, nodes_grad(): pl.pallas_call(nodes_grad_kernel, grid=(steps,), in_specs=[SMEM, rows_spe...  23.4 us
    ppermute x21, starting transfers between devices, swap(): return lax.ppermute(value, AXES, [(i, i ^ bit) for i in range(32)])  21.9 us
    pallas_call x1, Pallas kernels, agg_grad(): pl.pallas_call(agg_grad_kernel, grid=(n // TILE,), in_specs=[SMEM, VMEM,...  19.7 us
    pallas_call x1, Pallas kernels, forward(): pl.pallas_call(functools.partial(forward_kernel, bool(part)), grid=(n //...  19.3 us
    pallas_call x1, Pallas kernels, near_product(): pl.pallas_call(near_kernel, grid=(n // TILE,), in_specs=[SMEM, rows_spec(...  13.7 us
    pallas_call x1, Pallas kernels, neighbour_table(): pl.pallas_call(table_kernel, grid=(n // TILE,), in_specs=[SMEM, pl.BlockS...  11.3 us
  transfers between devices with their start and end apart: 21, of which 4 were waited for; matrix products, arithmetic and copies ran while one was open for 1% of the time, Pallas kernels for 62%

profile of v6, /device:TPU:0, one launch (start us, length us, event | category | flops | bytes accessed | tf_op | source)
XLA Modules:
  0.0 181.0 jit_solution(2221666548371998131)
XLA Ops:
  2.7 3.1 %collective-permute-start.1 = (bf16[64,2176]{1,0:T(8,128)(2,1)S(1)}, bf16[64,2176]{1,0:T(8,128)(2,1)S(1)}, u32[]{:S(2)}, u32[]{:S(2)}) collective-permute-start(bf16[64,2176]{1,0:T(8,128)(2,1)S(1)} %pad_maximum_fusion.1), channel_id=1, source_target_pairs={{0,1},{1,0},{2,3},{3,2},{4,5},{5,4},{6,7},{7,6},{8,9},{9,8},{10,11... | collective-permute-start | bytes 835592 | tf_op jit(solution)/shard_map/ppermute | solution.py:368
  5.8 2.6 %collective-permute-start = (bf16[64,2176]{1,0:T(8,128)(2,1)S(1)}, bf16[64,2176]{1,0:T(8,128)(2,1)S(1)}, u32[]{:S(2)}, u32[]{:S(2)}) collective-permute-start(bf16[64,2176]{1,0:T(8,128)(2,1)S(1)} %pad_maximum_fusion.1), channel_id=1, source_target_pairs={{0,2},{1,3},{2,0},{3,1},{4,6},{5,7},{6,4},{7,5},{8,10},{9,11},{10,... | collective-permute-start | bytes 835592 | tf_op jit(solution)/shard_map/ppermute | solution.py:368
  10.1 11.3 %table.1 = (bf16[2048,2048]{1,0:T(8,128)(2,1)}, s32[2]{0:T(128)S(1)}) custom-call(s32[2]{0:T(128)S(1)} %pad_add_fusion.ctl, s32[16,2048]{1,0:T(8,128)S(1)} %bitcast_select_fusion.used), custom_call_target="tpu_custom_call" | custom-call | flops 8589934592 | bytes 8388608 | tf_op jit(solution)/shard_map/table/pallas_call | solution.py:74
  22.0 7.0 %aggregate.3 = (bf16[2048,2048]{1,0:T(8,128)(2,1)}, s32[2]{0:T(128)S(1)}, bf16[2048,2048]{1,0:T(8,128)(2,1)}) custom-call(s32[2]{0:T(128)S(1)} %get-tuple-element.75.ctl, s32[1,2048]{1,0:T(1,128)S(1)} %bitcast.59, bf16[2048,2048]{1,0:T(8,128)(2,1)} %get-tuple-element.76.table, bf16[2048,2048]{1,0:T(8,128)(2,1)S(1)} %bitcast.58), custom_call_target="tpu_custom_call", output_to_operand_aliasing={{2}: (2, {})} | custom-call | flops 4294967296 | bytes 12582912 | tf_op jit(solution)/shard_map/aggregate/pallas_call | solution.py:120
  29.4 1.6 collective-permute-start.4
  31.0 1.6 collective-permute-start.3
  32.6 11.9 %aggregate.4 = (bf16[2048,2048]{1,0:T(8,128)(2,1)}, s32[2]{0:T(128)S(1)}, bf16[2048,2048]{1,0:T(8,128)(2,1)}) custom-call(s32[2]{0:T(128)S(1)} %get-tuple-element.80.ctl, s32[1,2048]{1,0:T(1,128)S(1)} %bitcast.60, bf16[2048,2048]{1,0:T(8,128)(2,1)} %get-tuple-element.81.table, ...), custom_call_target="tpu_custom_call", output_to_operand_aliasing={{2}: (2, {}), {0}: (4, {})} | custom-call | flops 8589934592 | bytes 16777216 | tf_op jit(solution)/shard_map/aggregate/pallas_call | solution.py:120
  46.9 7.1 %aggregate.5 = (bf16[2048,2048]{1,0:T(8,128)(2,1)}, s32[2]{0:T(128)S(1)}, bf16[2048,2048]{1,0:T(8,128)(2,1)}) custom-call(s32[2]{0:T(128)S(1)} %get-tuple-element.86.ctl, s32[1,2048]{1,0:T(1,128)S(1)} %bitcast.61, bf16[2048,2048]{1,0:T(8,128)(2,1)} %get-tuple-element.87.table, ...), custom_call_target="tpu_custom_call", output_to_operand_aliasing={{2}: (2, {}), {0}: (4, {})} | custom-call | flops 4294967296 | bytes 12582912 | tf_op jit(solution)/shard_map/aggregate/pallas_call | solution.py:120
  54.0 2.5 %place.3 = (bf16[2048,2048]{1,0:T(8,128)(2,1)S(1)}, f32[1,2048]{1,0:T(1,128)S(1)}, s32[2]{0:T(128)S(1)}) custom-call(s32[2]{0:T(128)S(1)} %get-tuple-element.89.ctl, bf16[544,1024]{1,0:T(8,128)(2,1)S(1)} %constant_dynamic-update-slice_fusion.1.refs_0_, bf16[512,1024]{1,0:T(8,128)(2,1)S(1)} %constant_dynamic-update-slice_fusion.3.refs_1_, ...), custom_call_target="tpu_custom_call" | custom-call | bytes 8388608 | tf_op jit(solution)/shard_map/place/pallas_call | solution.py:264
  56.5 13.7 %near.1 = (bf16[2048,2048]{1,0:T(8,128)(2,1)}, s32[2]{0:T(128)S(1)}, bf16[2048,2048]{1,0:T(8,128)(2,1)}) custom-call(s32[2]{0:T(128)S(1)} %get-tuple-element.90.ctl, bf16[2048,2048]{1,0:T(8,128)(2,1)} %get-tuple-element.91.agg, bf16[2048,2048]{1,0:T(8,128)(2,1)S(1)} %get-tuple-element.92.weight.refs_2_), custom_call_target="tpu_custom_call", output_to_operand_aliasing={{2}: (1, {})} | custom-call | flops 8589934592 | bytes 33554432 | tf_op jit(solution)/shard_map/near/pallas_call | solution.py:160
  70.1 2.5 %collective-permute-done.7.refs_0_ = bf16[544,1024]{1,0:T(8,128)(2,1)S(1)} collective-permute-done((bf16[544,1024]{1,0:T(8,128)(2,1)S(1)}, bf16[544,1024]{1,0:T(8,128)(2,1)S(1)}, u32[]{:S(2)}, u32[]{:S(2)}) %collective-permute-start.7) | collective-permute-done | bytes 1114144 | tf_op jit(solution)/shard_map/ppermute | solution.py:368
  73.2 1.7 place.4
  74.9 2.0 %collective-permute-done.10.refs_1_ = bf16[512,1024]{1,0:T(8,128)(2,1)S(1)} collective-permute-done((bf16[512,1024]{1,0:T(8,128)(2,1)S(1)}, bf16[512,1024]{1,0:T(8,128)(2,1)S(1)}, u32[]{:S(2)}, u32[]{:S(2)}) %collective-permute-start.10) | collective-permute-done | bytes 1048608 | tf_op jit(solution)/shard_map/ppermute | solution.py:368
  76.9 1.7 place.5
  79.1 19.3 %forward.1 = (bf16[2048,2048]{1,0:T(8,128)(2,1)}, bf16[2048,2048]{1,0:T(8,128)(2,1)S(1)}, f32[1,2048]{1,0:T(1,128)S(1)}, s32[2]{0:T(128)S(1)}, bf16[2048,2048]{1,0:T(8,128)(2,1)}) custom-call(s32[2]{0:T(128)S(1)} %get-tuple-element.102.ctl, bf16[2048,2048]{1,0:T(8,128)(2,1)} %get-tuple-element.103.agg, ...), custom_call_target="tpu_custom_call", output_to_operand_aliasing={{4}: (1, {}), {0}: (5, {})} | custom-call | flops 17179869184 | bytes 41943040 | tf_op jit(solution)/shard_map/forward/pallas_call | solution.py:204
  98.4 11.4 %wgrad.3 = (bf16[4,272,2048]{2,1,0:T(8,128)(2,1)S(1)}, s32[2]{0:T(128)S(1)}, bf16[2048,2048]{1,0:T(8,128)(2,1)}) custom-call(s32[2]{0:T(128)S(1)} %get-tuple-element.108.ctl, bf16[2048,2048]{1,0:T(8,128)(2,1)} %get-tuple-element.109.agg, bf16[2048,2048]{1,0:T(8,128)(2,1)S(1)} %get-tuple-element.110.grad, ...), custom_call_target="tpu_custom_call", output_to_operand_aliasing={{2}: (1, {})} | custom-call | flops 8589934592 | bytes 16777216 | tf_op jit(solution)/shard_map/wgrad/pallas_call | solution.py:304
  109.8 9.2 %wgrad.4 = (bf16[3,272,2048]{2,1,0:T(8,128)(2,1)S(1)}, s32[2]{0:T(128)S(1)}, bf16[2048,2048]{1,0:T(8,128)(2,1)}) custom-call(s32[2]{0:T(128)S(1)} %get-tuple-element.112.ctl, bf16[2048,2048]{1,0:T(8,128)(2,1)} %get-tuple-element.113.agg, bf16[2048,2048]{1,0:T(8,128)(2,1)S(1)} %get-tuple-element.110.grad, ...), custom_call_target="tpu_custom_call", output_to_operand_aliasing={{2}: (1, {})} | custom-call | flops 6442450944 | bytes 16777216 | tf_op jit(solution)/shard_map/wgrad/pallas_call | solution.py:304
  121.3 4.5 %wgrad.5 = (bf16[1,272,2048]{2,1,0:T(8,128)(2,1)S(1)}, s32[2]{0:T(128)S(1)}, bf16[2048,2048]{1,0:T(8,128)(2,1)}) custom-call(s32[2]{0:T(128)S(1)} %get-tuple-element.118.ctl, bf16[2048,2048]{1,0:T(8,128)(2,1)} %get-tuple-element.119.agg, bf16[2048,2048]{1,0:T(8,128)(2,1)S(1)} %get-tuple-element.110.grad, ...), custom_call_target="tpu_custom_call", output_to_operand_aliasing={{2}: (1, {})} | custom-call | flops 2147483648 | bytes 16777216 | tf_op jit(solution)/shard_map/wgrad/pallas_call | solution.py:304
  125.8 19.7 %agg_grad.1 = (bf16[2048,2048]{1,0:T(8,128)(2,1)S(1)}, s32[2]{0:T(128)S(1)}) custom-call(s32[2]{0:T(128)S(1)} %get-tuple-element.120.ctl, s32[1,2048]{1,0:T(1,128)S(1)} %bitcast.62, bf16[2048,2048]{1,0:T(8,128)(2,1)S(1)} %get-tuple-element.110.grad, bf16[2048,2048]{1,0:T(8,128)(2,1)S(1)} %get-tuple-element.104.weight), custom_call_target="tpu_custom_call" | custom-call | flops 17179869184 | bytes 25165824 | tf_op jit(solution)/shard_map/agg_grad/pallas_call | solution.py:333
  145.8 1.6 collective-permute-start.15
  150.5 6.2 %nodes_grad.3 = (bf16[2048,2048]{1,0:T(8,128)(2,1)}, s32[2]{0:T(128)S(1)}) custom-call(s32[2]{0:T(128)S(1)} %get-tuple-element.121.ctl, bf16[2048,2048]{1,0:T(8,128)(2,1)S(1)} %bitcast.56, bf16[2048,2048]{1,0:T(8,128)(2,1)S(1)} %get-tuple-element.123.spread, bf16[80,1024]{1,0:T(8,128)(2,1)S(1)} %slice_bitcast_fusion.2.rest_0_, ...), custom_call_target="tpu_custom_call" | custom-call | flops 4294967296 | bytes 12582912 | tf_op jit(solution)/shard_map/nodes_grad/pallas_call | solution.py:354
  158.5 6.2 %nodes_grad.4 = (bf16[2048,2048]{1,0:T(8,128)(2,1)}, s32[2]{0:T(128)S(1)}) custom-call(s32[2]{0:T(128)S(1)} %get-tuple-element.126.ctl, bf16[2048,2048]{1,0:T(8,128)(2,1)S(1)} %bitcast.56, bf16[2048,2048]{1,0:T(8,128)(2,1)S(1)} %get-tuple-element.123.spread, bf16[2048,2048]{1,0:T(8,128)(2,1)} %get-tuple-element.127.rest_0_, ...), custom_call_target="tpu_custom_call", output_to_operand_aliasing={{0}: (3, {})} | custom-call | flops 4294967296 | bytes 12582912 | tf_op jit(solution)/shard_map/nodes_grad/pallas_call | solution.py:354
  165.9 1.8 %collective-permute-start.20 = (bf16[64,2176]{1,0:T(8,128)(2,1)S(1)}, bf16[64,2176]{1,0:T(8,128)(2,1)S(1)}, u32[]{:S(2)}, u32[]{:S(2)}) collective-permute-start(bf16[64,2176]{1,0:T(8,128)(2,1)S(1)} %fusion.1.rest_1_), channel_id=1, source_target_pairs={{0,2},{1,3},{2,0},{3,1},{4,6},{5,7},{6,4},{7,5},{8,10},{9,11},{10,... | collective-permute-start | bytes 835592 | tf_op jit(solution)/shard_map/ppermute | solution.py:368
  167.7 10.9 %nodes_grad.5 = (bf16[2048,2048]{1,0:T(8,128)(2,1)}, s32[2]{0:T(128)}) custom-call(s32[2]{0:T(128)S(1)} %get-tuple-element.131.ctl, bf16[2048,2048]{1,0:T(8,128)(2,1)S(1)} %bitcast.56, bf16[2048,2048]{1,0:T(8,128)(2,1)S(1)} %get-tuple-element.123.spread, bf16[2048,2048]{1,0:T(8,128)(2,1)} %get-tuple-element.132.rest_0_, ...), custom_call_target="tpu_custom_call", output_to_operand_aliasing={{0}: (3, {})} | custom-call | flops 8589934592 | bytes 16777216 | tf_op jit(solution)/shard_map/nodes_grad/pallas_call | solution.py:354
  (89 shorter events, 18.4 us)
Async XLA Ops:
  1.6 20.4 %slice-start.2 = ((s8[8388608]{0:T(1024)(128)(4,1)}), s8[4194304]{0:T(1024)(128)(4,1)S(1)}, s32[]{:S(2)}) async-start(s8[8388608]{0:T(1024)(128)(4,1)} %bitcast.57), calls=%async_computation.2 | async-start | bytes 8388608
  2.7 19.2 %collective-permute-start.1 = (bf16[64,2176]{1,0:T(8,128)(2,1)S(1)}, bf16[64,2176]{1,0:T(8,128)(2,1)S(1)}, u32[]{:S(2)}, u32[]{:S(2)}) collective-permute-start(bf16[64,2176]{1,0:T(8,128)(2,1)S(1)} %pad_maximum_fusion.1), channel_id=1, source_target_pairs={{0,1},{1,0},{2,3},{3,2},{4,5},{5,4},{6,7},{7,6},{8,9},{9,8},{10,11... | collective-permute-start | bytes 835592 | tf_op jit(solution)/shard_map/ppermute | solution.py:368
  5.8 15.6 %collective-permute-start = (bf16[64,2176]{1,0:T(8,128)(2,1)S(1)}, bf16[64,2176]{1,0:T(8,128)(2,1)S(1)}, u32[]{:S(2)}, u32[]{:S(2)}) collective-permute-start(bf16[64,2176]{1,0:T(8,128)(2,1)S(1)} %pad_maximum_fusion.1), channel_id=1, source_target_pairs={{0,2},{1,3},{2,0},{3,1},{4,6},{5,7},{6,4},{7,5},{8,10},{9,11},{10,... | collective-permute-start | bytes 835592 | tf_op jit(solution)/shard_map/ppermute | solution.py:368
  21.4 7.9 %collective-permute-start.2 = (bf16[64,2176]{1,0:T(8,128)(2,1)S(1)}, bf16[64,2176]{1,0:T(8,128)(2,1)S(1)}, u32[]{:S(2)}, u32[]{:S(2)}) collective-permute-start(bf16[64,2176]{1,0:T(8,128)(2,1)S(1)} %collective-permute-done), channel_id=1, source_target_pairs={{0,1},{1,0},{2,3},{3,2},{4,5},{5,4},{6,7},{7,6},{8,9},{9,8},{10,11... | collective-permute-start | bytes 835592 | tf_op jit(solution)/shard_map/ppermute | solution.py:368
  29.4 15.0 %collective-permute-start.4 = (bf16[256,1024]{1,0:T(8,128)(2,1)S(1)}, bf16[256,1024]{1,0:T(8,128)(2,1)S(1)}, u32[]{:S(2)}, u32[]{:S(2)}) collective-permute-start(bf16[256,1024]{1,0:T(8,128)(2,1)S(1)} %pad_maximum_fusion), channel_id=1, source_target_pairs={{0,16},{1,17},{2,18},{3,19},{4,20},{5,21},{6,22},{7,23},{8,24},{9,... | collective-permute-start | bytes 1572872 | tf_op jit(solution)/shard_map/ppermute | solution.py:368
  31.0 13.4 %collective-permute-start.3 = (bf16[272,1024]{1,0:T(8,128)(2,1)S(1)}, bf16[272,1024]{1,0:T(8,128)(2,1)S(1)}, u32[]{:S(2)}, u32[]{:S(2)}) collective-permute-start(bf16[272,1024]{1,0:T(8,128)(2,1)S(1)} %get-tuple-element.168), channel_id=1, source_target_pairs={{0,8},{1,9},{2,10},{3,11},{4,12},{5,13},{6,14},{7,15},{8,0},{9,1},... | collective-permute-start | bytes 1671176 | tf_op jit(solution)/shard_map/ppermute | solution.py:368
  44.5 9.5 %collective-permute-start.5 = (bf16[544,1024]{1,0:T(8,128)(2,1)S(1)}, bf16[544,1024]{1,0:T(8,128)(2,1)S(1)}, u32[]{:S(2)}, u32[]{:S(2)}) collective-permute-start(bf16[544,1024]{1,0:T(8,128)(2,1)S(1)} %constant_dynamic-update-slice_fusion.1.refs_0_), channel_id=1, source_target_pairs={{0,4},{1,5},{2,6},{3,7},{4,0},{5,1},{6,2},{7,3},{8,12},{9,13},{10,... | collective-permute-start | bytes 3342344 | tf_op jit(solution)/shard_map/ppermute | solution.py:368
  44.6 9.4 %collective-permute-start.6 = (bf16[512,1024]{1,0:T(8,128)(2,1)S(1)}, bf16[512,1024]{1,0:T(8,128)(2,1)S(1)}, u32[]{:S(2)}, u32[]{:S(2)}) collective-permute-start(bf16[512,1024]{1,0:T(8,128)(2,1)S(1)} %constant_dynamic-update-slice_fusion.3.refs_1_), channel_id=1, source_target_pairs={{0,4},{1,5},{2,6},{3,7},{4,0},{5,1},{6,2},{7,3},{8,12},{9,13},{10,... | collective-permute-start | bytes 3145736 | tf_op jit(solution)/shard_map/ppermute | solution.py:368
  45.2 27.5 %collective-permute-start.8 = (bf16[512,1024]{1,0:T(8,128)(2,1)S(1)}, bf16[512,1024]{1,0:T(8,128)(2,1)S(1)}, u32[]{:S(2)}, u32[]{:S(2)}) collective-permute-start(bf16[512,1024]{1,0:T(8,128)(2,1)S(1)} %constant_dynamic-update-slice_fusion.3.refs_1_), channel_id=1, source_target_pairs={{0,8},{1,9},{2,10},{3,11},{4,12},{5,13},{6,14},{7,15},{8,0},{9,1},... | collective-permute-start | bytes 3145736 | tf_op jit(solution)/shard_map/ppermute | solution.py:368
  46.4 26.3 %collective-permute-start.7 = (bf16[544,1024]{1,0:T(8,128)(2,1)S(1)}, bf16[544,1024]{1,0:T(8,128)(2,1)S(1)}, u32[]{:S(2)}, u32[]{:S(2)}) collective-permute-start(bf16[544,1024]{1,0:T(8,128)(2,1)S(1)} %constant_dynamic-update-slice_fusion.1.refs_0_), channel_id=1, source_target_pairs={{0,16},{1,17},{2,18},{3,19},{4,20},{5,21},{6,22},{7,23},{8,24},{9,... | collective-permute-start | bytes 3342344 | tf_op jit(solution)/shard_map/ppermute | solution.py:368
  72.6 4.3 %collective-permute-start.9 = (bf16[544,1024]{1,0:T(8,128)(2,1)S(1)}, bf16[544,1024]{1,0:T(8,128)(2,1)S(1)}, u32[]{:S(2)}, u32[]{:S(2)}) collective-permute-start(bf16[544,1024]{1,0:T(8,128)(2,1)S(1)} %collective-permute-done.7.refs_0_), channel_id=1, source_target_pairs={{0,4},{1,5},{2,6},{3,7},{4,0},{5,1},{6,2},{7,3},{8,12},{9,13},{10,... | collective-permute-start | bytes 3342344 | tf_op jit(solution)/shard_map/ppermute | solution.py:368
  72.7 4.2 %collective-permute-start.10 = (bf16[512,1024]{1,0:T(8,128)(2,1)S(1)}, bf16[512,1024]{1,0:T(8,128)(2,1)S(1)}, u32[]{:S(2)}, u32[]{:S(2)}) collective-permute-start(bf16[512,1024]{1,0:T(8,128)(2,1)S(1)} %collective-permute-done.8.refs_1_), channel_id=1, source_target_pairs={{0,4},{1,5},{2,6},{3,7},{4,0},{5,1},{6,2},{7,3},{8,12},{9,13},{10,... | collective-permute-start | bytes 3145736 | tf_op jit(solution)/shard_map/ppermute | solution.py:368
  109.7 9.3 %collective-permute-start.11 = (bf16[4,272,2048]{2,1,0:T(8,128)(2,1)S(1)}, bf16[4,272,2048]{2,1,0:T(8,128)(2,1)S(1)}, u32[]{:S(2)}, u32[]{:S(2)}) collective-permute-start(bf16[4,272,2048]{2,1,0:T(8,128)(2,1)S(1)} %get-tuple-element.116), channel_id=1, source_target_pairs={{0,4},{1,5},{2,6},{3,7},{4,0},{5,1},{6,2},{7,3},{8,12},{9,13},{10,... | collective-permute-start | bytes 13369352 | tf_op jit(solution)/shard_map/ppermute | solution.py:368
  119.9 25.6 %collective-permute-start.13 = (bf16[2,256,1024]{2,1,0:T(8,128)(2,1)S(1)}, bf16[2,256,1024]{2,1,0:T(8,128)(2,1)S(1)}, u32[]{:S(2)}, u32[]{:S(2)}) collective-permute-start(bf16[2,256,1024]{2,1,0:T(8,128)(2,1)S(1)} %add_convert_fusion.1), channel_id=1, source_target_pairs={{0,8},{1,9},{2,10},{3,11},{4,12},{5,13},{6,14},{7,15},{8,0},{9,1},... | collective-permute-start | bytes 3145736 | tf_op jit(solution)/shard_map/ppermute | solution.py:368
  120.8 27.2 %collective-permute-start.12 = (bf16[2,272,1024]{2,1,0:T(8,128)(2,1)S(1)}, bf16[2,272,1024]{2,1,0:T(8,128)(2,1)S(1)}, u32[]{:S(2)}, u32[]{:S(2)}) collective-permute-start(bf16[2,272,1024]{2,1,0:T(8,128)(2,1)S(1)} %add_convert_fusion), channel_id=1, source_target_pairs={{0,16},{1,17},{2,18},{3,19},{4,20},{5,21},{6,22},{7,23},{8,24},{9,... | collective-permute-start | bytes 3342344 | tf_op jit(solution)/shard_map/ppermute | solution.py:368
  125.8 24.6 %slice-start = ((s8[8388608]{0:T(1024)(128)(4,1)}), s8[4194304]{0:T(1024)(128)(4,1)S(1)}, s32[]{:S(2)}) async-start(s8[8388608]{0:T(1024)(128)(4,1)} %bitcast.55), calls=%async_computation | async-start | bytes 8388608
  125.8 24.6 %slice-start.1 = ((s8[8388608]{0:T(1024)(128)(4,1)}), s8[4194304]{0:T(1024)(128)(4,1)S(1)}, s32[]{:S(2)}) async-start(s8[8388608]{0:T(1024)(128)(4,1)} %bitcast.55), calls=%async_computation.1 | async-start | bytes 8388608
  145.8 10.9 %collective-permute-start.15 = (bf16[64,1024]{1,0:T(8,128)(2,1)S(1)}, bf16[64,1024]{1,0:T(8,128)(2,1)S(1)}, u32[]{:S(2)}, u32[]{:S(2)}) collective-permute-start(bf16[64,1024]{1,0:T(8,128)(2,1)S(1)} %slice_bitcast_fusion.3.rest_1_), channel_id=1, source_target_pairs={{0,16},{1,17},{2,18},{3,19},{4,20},{5,21},{6,22},{7,23},{8,24},{9,... | collective-permute-start | bytes 393224 | tf_op jit(solution)/shard_map/ppermute | solution.py:368
  147.4 17.2 %collective-permute-start.17 = (bf16[192,1024]{1,0:T(8,128)(2,1)S(1)}, bf16[192,1024]{1,0:T(8,128)(2,1)S(1)}, u32[]{:S(2)}, u32[]{:S(2)}) collective-permute-start(bf16[192,1024]{1,0:T(8,128)(2,1)S(1)} %slice_bitcast_fusion.rest_3_), channel_id=1, source_target_pairs={{0,16},{1,17},{2,18},{3,19},{4,20},{5,21},{6,22},{7,23},{8,24},{9,... | collective-permute-start | bytes 1179656 | tf_op jit(solution)/shard_map/ppermute | solution.py:368
  148.4 8.3 %collective-permute-start.14 = (bf16[80,1024]{1,0:T(8,128)(2,1)S(1)}, bf16[80,1024]{1,0:T(8,128)(2,1)S(1)}, u32[]{:S(2)}, u32[]{:S(2)}) collective-permute-start(bf16[80,1024]{1,0:T(8,128)(2,1)S(1)} %slice_bitcast_fusion.2.rest_0_), channel_id=1, source_target_pairs={{0,8},{1,9},{2,10},{3,11},{4,12},{5,13},{6,14},{7,15},{8,0},{9,1},... | collective-permute-start | bytes 491528 | tf_op jit(solution)/shard_map/ppermute | solution.py:368
  149.7 15.2 %collective-permute-start.16 = (bf16[192,1024]{1,0:T(8,128)(2,1)S(1)}, bf16[192,1024]{1,0:T(8,128)(2,1)S(1)}, u32[]{:S(2)}, u32[]{:S(2)}) collective-permute-start(bf16[192,1024]{1,0:T(8,128)(2,1)S(1)} %slice_bitcast_fusion.1.rest_2_), channel_id=1, source_target_pairs={{0,8},{1,9},{2,10},{3,11},{4,12},{5,13},{6,14},{7,15},{8,0},{9,1},... | collective-permute-start | bytes 1179656 | tf_op jit(solution)/shard_map/ppermute | solution.py:368
  156.9 8.9 %collective-permute-start.18 = (bf16[64,2176]{1,0:T(8,128)(2,1)S(1)}, bf16[64,2176]{1,0:T(8,128)(2,1)S(1)}, u32[]{:S(2)}, u32[]{:S(2)}) collective-permute-start(bf16[64,2176]{1,0:T(8,128)(2,1)S(1)} %fusion.5.rest_1_), channel_id=1, source_target_pairs={{0,1},{1,0},{2,3},{3,2},{4,5},{5,4},{6,7},{7,6},{8,9},{9,8},{10,11... | collective-permute-start | bytes 835592 | tf_op jit(solution)/shard_map/ppermute | solution.py:368
  165.2 13.4 %collective-permute-start.19 = (bf16[64,2176]{1,0:T(8,128)(2,1)S(1)}, bf16[64,2176]{1,0:T(8,128)(2,1)S(1)}, u32[]{:S(2)}, u32[]{:S(2)}) collective-permute-start(bf16[64,2176]{1,0:T(8,128)(2,1)S(1)} %fusion.6.rest_2_), channel_id=1, source_target_pairs={{0,1},{1,0},{2,3},{3,2},{4,5},{5,4},{6,7},{7,6},{8,9},{9,8},{10,11... | collective-permute-start | bytes 835592 | tf_op jit(solution)/shard_map/ppermute | solution.py:368
  165.9 13.7 %collective-permute-start.20 = (bf16[64,2176]{1,0:T(8,128)(2,1)S(1)}, bf16[64,2176]{1,0:T(8,128)(2,1)S(1)}, u32[]{:S(2)}, u32[]{:S(2)}) collective-permute-start(bf16[64,2176]{1,0:T(8,128)(2,1)S(1)} %fusion.1.rest_1_), channel_id=1, source_target_pairs={{0,2},{1,3},{2,0},{3,1},{4,6},{5,7},{6,4},{7,5},{8,10},{9,11},{10,... | collective-permute-start | bytes 835592 | tf_op jit(solution)/shard_map/ppermute | solution.py:368
  (5 other events, 42.8 us)

commit v7 on v6

--- a/solution.py
+++ b/solution.py
@@ -414,12 +414,12 @@
     p = cat(own[:, :half], one[:, :half], two[:, :half], three[:, :half], heads)
     q = cat(own[:, half:m], one[:, half:m], two[:, half:m], three[:, half:m])
     px, qy = swap(p, X), swap(q, Y)
-    agg, ctl, table = aggregate(after(ctl, p, q), deg, table, nodes, 2, 4, agg)
+    agg, ctl, table = aggregate(after(ctl, p, q), deg, table, nodes, 2, 3, agg)
     px, qy = after(px, ctl), after(qy, ctl)
     p, q = cat(p, px), cat(q, qy)
     py, qx = swap(p, Y), swap(q, X)
     p_other, q_other = swap(p, CORE), swap(q, CORE)
-    agg, ctl, table = aggregate(after(ctl, p, q), deg, table, nodes, 6, steps - 6, agg)
+    agg, ctl, table = aggregate(after(ctl, p, q), deg, table, nodes, 5, steps - 5, agg)
     zs = (0, Z1, Z2, Z1 ^ Z2)
     near_p, near_q = codes_of(zs, (0, X)), codes_of(zs, (0, Y))
 

time: 182 us -> 182 us (level)
  transfers between devices with their start and end apart: 21 -> 21, of which waited for: 4 -> 6; matrix products, arithmetic and copies ran while one was open for 1% -> 1% of each run, Pallas kernels for 62% -> 62%
where the time goes in v7:
time: 182 us
  Pallas kernels  144 us (79%)
  starting transfers between devices  21.5 us (12%)
  waiting for transfers between devices  6.78 us (4%)
  other arithmetic  6.76 us (4%)
    pallas_call x3, Pallas kernels, aggregate(): pl.pallas_call(functools.partial(aggregate_kernel, first), grid=(steps,),...  26 us
    pallas_call x3, Pallas kernels, wgrad(): pl.pallas_call(functools.partial(wgrad_kernel, code), grid_spec=pltpu.Pre...  25 us
    pallas_call x3, Pallas kernels, nodes_grad(): pl.pallas_call(nodes_grad_kernel, grid=(steps,), in_specs=[SMEM, rows_spe...  23.4 us
    ppermute x21, starting transfers between devices, swap(): return lax.ppermute(value, AXES, [(i, i ^ bit) for i in range(32)])  21.5 us
    pallas_call x1, Pallas kernels, agg_grad(): pl.pallas_call(agg_grad_kernel, grid=(n // TILE,), in_specs=[SMEM, VMEM,...  19.7 us
    pallas_call x1, Pallas kernels, forward(): pl.pallas_call(functools.partial(forward_kernel, bool(part)), grid=(n //...  19.2 us
    pallas_call x1, Pallas kernels, near_product(): pl.pallas_call(near_kernel, grid=(n // TILE,), in_specs=[SMEM, rows_spec(...  13.7 us
    pallas_call x1, Pallas kernels, neighbour_table(): pl.pallas_call(table_kernel, grid=(n // TILE,), in_specs=[SMEM, pl.BlockS...  11.3 us
  transfers between devices with their start and end apart: 21, of which 6 were waited for; matrix products, arithmetic and copies ran while one was open for 1% of the time, Pallas kernels for 62%

profile of v7, /device:TPU:0, one launch (start us, length us, event | category | flops | bytes accessed | tf_op | source)
XLA Modules:
  0.0 181.7 jit_solution(16071937040264039853)
XLA Ops:
  2.7 3.1 %collective-permute-start.1 = (bf16[64,2176]{1,0:T(8,128)(2,1)S(1)}, bf16[64,2176]{1,0:T(8,128)(2,1)S(1)}, u32[]{:S(2)}, u32[]{:S(2)}) collective-permute-start(bf16[64,2176]{1,0:T(8,128)(2,1)S(1)} %pad_maximum_fusion.1), channel_id=1, source_target_pairs={{0,1},{1,0},{2,3},{3,2},{4,5},{5,4},{6,7},{7,6},{8,9},{9,8},{10,11... | collective-permute-start | bytes 835592 | tf_op jit(solution)/shard_map/ppermute | solution.py:368
  5.8 2.6 %collective-permute-start = (bf16[64,2176]{1,0:T(8,128)(2,1)S(1)}, bf16[64,2176]{1,0:T(8,128)(2,1)S(1)}, u32[]{:S(2)}, u32[]{:S(2)}) collective-permute-start(bf16[64,2176]{1,0:T(8,128)(2,1)S(1)} %pad_maximum_fusion.1), channel_id=1, source_target_pairs={{0,2},{1,3},{2,0},{3,1},{4,6},{5,7},{6,4},{7,5},{8,10},{9,11},{10,... | collective-permute-start | bytes 835592 | tf_op jit(solution)/shard_map/ppermute | solution.py:368
  10.1 11.3 %table.1 = (bf16[2048,2048]{1,0:T(8,128)(2,1)}, s32[2]{0:T(128)S(1)}) custom-call(s32[2]{0:T(128)S(1)} %pad_add_fusion.ctl, s32[16,2048]{1,0:T(8,128)S(1)} %bitcast_select_fusion.used), custom_call_target="tpu_custom_call" | custom-call | flops 8589934592 | bytes 8388608 | tf_op jit(solution)/shard_map/table/pallas_call | solution.py:74
  22.0 7.0 %aggregate.3 = (bf16[2048,2048]{1,0:T(8,128)(2,1)}, s32[2]{0:T(128)S(1)}, bf16[2048,2048]{1,0:T(8,128)(2,1)}) custom-call(s32[2]{0:T(128)S(1)} %get-tuple-element.75.ctl, s32[1,2048]{1,0:T(1,128)S(1)} %bitcast.59, bf16[2048,2048]{1,0:T(8,128)(2,1)} %get-tuple-element.76.table, bf16[2048,2048]{1,0:T(8,128)(2,1)S(1)} %bitcast.58), custom_call_target="tpu_custom_call", output_to_operand_aliasing={{2}: (2, {})} | custom-call | flops 4294967296 | bytes 12582912 | tf_op jit(solution)/shard_map/aggregate/pallas_call | solution.py:120
  29.4 1.6 collective-permute-start.4
  32.6 9.4 %aggregate.4 = (bf16[2048,2048]{1,0:T(8,128)(2,1)}, s32[2]{0:T(128)S(1)}, bf16[2048,2048]{1,0:T(8,128)(2,1)}) custom-call(s32[2]{0:T(128)S(1)} %get-tuple-element.80.ctl, s32[1,2048]{1,0:T(1,128)S(1)} %bitcast.60, bf16[2048,2048]{1,0:T(8,128)(2,1)} %get-tuple-element.81.table, ...), custom_call_target="tpu_custom_call", output_to_operand_aliasing={{2}: (2, {}), {0}: (4, {})} | custom-call | flops 6442450944 | bytes 14680064 | tf_op jit(solution)/shard_map/aggregate/pallas_call | solution.py:120
  42.2 2.0 %collective-permute-done.3 = bf16[272,1024]{1,0:T(8,128)(2,1)S(1)} collective-permute-done((bf16[272,1024]{1,0:T(8,128)(2,1)S(1)}, bf16[272,1024]{1,0:T(8,128)(2,1)S(1)}, u32[]{:S(2)}, u32[]{:S(2)}) %collective-permute-start.3) | collective-permute-done | bytes 557088 | tf_op jit(solution)/shard_map/ppermute | solution.py:368
  46.9 9.5 %aggregate.5 = (bf16[2048,2048]{1,0:T(8,128)(2,1)}, s32[2]{0:T(128)S(1)}, bf16[2048,2048]{1,0:T(8,128)(2,1)}) custom-call(s32[2]{0:T(128)S(1)} %get-tuple-element.86.ctl, s32[1,2048]{1,0:T(1,128)S(1)} %bitcast.61, bf16[2048,2048]{1,0:T(8,128)(2,1)} %get-tuple-element.87.table, ...), custom_call_target="tpu_custom_call", output_to_operand_aliasing={{2}: (2, {}), {0}: (4, {})} | custom-call | flops 6442450944 | bytes 14680064 | tf_op jit(solution)/shard_map/aggregate/pallas_call | solution.py:120
  56.4 2.5 %place.3 = (bf16[2048,2048]{1,0:T(8,128)(2,1)S(1)}, f32[1,2048]{1,0:T(1,128)S(1)}, s32[2]{0:T(128)S(1)}) custom-call(s32[2]{0:T(128)S(1)} %get-tuple-element.89.ctl, bf16[544,1024]{1,0:T(8,128)(2,1)S(1)} %constant_dynamic-update-slice_fusion.1.refs_0_, bf16[512,1024]{1,0:T(8,128)(2,1)S(1)} %constant_dynamic-update-slice_fusion.3.refs_1_, ...), custom_call_target="tpu_custom_call" | custom-call | bytes 8388608 | tf_op jit(solution)/shard_map/place/pallas_call | solution.py:264
  58.9 13.7 %near.1 = (bf16[2048,2048]{1,0:T(8,128)(2,1)}, s32[2]{0:T(128)S(1)}, bf16[2048,2048]{1,0:T(8,128)(2,1)}) custom-call(s32[2]{0:T(128)S(1)} %get-tuple-element.90.ctl, bf16[2048,2048]{1,0:T(8,128)(2,1)} %get-tuple-element.91.agg, bf16[2048,2048]{1,0:T(8,128)(2,1)S(1)} %get-tuple-element.92.weight.refs_2_), custom_call_target="tpu_custom_call", output_to_operand_aliasing={{2}: (1, {})} | custom-call | flops 8589934592 | bytes 33554432 | tf_op jit(solution)/shard_map/near/pallas_call | solution.py:160
  73.2 1.7 place.4
  74.9 2.0 %collective-permute-done.10.refs_1_ = bf16[512,1024]{1,0:T(8,128)(2,1)S(1)} collective-permute-done((bf16[512,1024]{1,0:T(8,128)(2,1)S(1)}, bf16[512,1024]{1,0:T(8,128)(2,1)S(1)}, u32[]{:S(2)}, u32[]{:S(2)}) %collective-permute-start.10) | collective-permute-done | bytes 1048608 | tf_op jit(solution)/shard_map/ppermute | solution.py:368
  76.9 1.7 place.5
  79.1 19.2 %forward.1 = (bf16[2048,2048]{1,0:T(8,128)(2,1)}, bf16[2048,2048]{1,0:T(8,128)(2,1)S(1)}, f32[1,2048]{1,0:T(1,128)S(1)}, s32[2]{0:T(128)S(1)}, bf16[2048,2048]{1,0:T(8,128)(2,1)}) custom-call(s32[2]{0:T(128)S(1)} %get-tuple-element.102.ctl, bf16[2048,2048]{1,0:T(8,128)(2,1)} %get-tuple-element.103.agg, ...), custom_call_target="tpu_custom_call", output_to_operand_aliasing={{4}: (1, {}), {0}: (5, {})} | custom-call | flops 17179869184 | bytes 41943040 | tf_op jit(solution)/shard_map/forward/pallas_call | solution.py:204
  98.3 11.4 %wgrad.3 = (bf16[4,272,2048]{2,1,0:T(8,128)(2,1)S(1)}, s32[2]{0:T(128)S(1)}, bf16[2048,2048]{1,0:T(8,128)(2,1)}) custom-call(s32[2]{0:T(128)S(1)} %get-tuple-element.108.ctl, bf16[2048,2048]{1,0:T(8,128)(2,1)} %get-tuple-element.109.agg, bf16[2048,2048]{1,0:T(8,128)(2,1)S(1)} %get-tuple-element.110.grad, ...), custom_call_target="tpu_custom_call", output_to_operand_aliasing={{2}: (1, {})} | custom-call | flops 8589934592 | bytes 16777216 | tf_op jit(solution)/shard_map/wgrad/pallas_call | solution.py:304
  109.9 9.2 %wgrad.4 = (bf16[3,272,2048]{2,1,0:T(8,128)(2,1)S(1)}, s32[2]{0:T(128)S(1)}, bf16[2048,2048]{1,0:T(8,128)(2,1)}) custom-call(s32[2]{0:T(128)S(1)} %get-tuple-element.112.ctl, bf16[2048,2048]{1,0:T(8,128)(2,1)} %get-tuple-element.113.agg, bf16[2048,2048]{1,0:T(8,128)(2,1)S(1)} %get-tuple-element.110.grad, ...), custom_call_target="tpu_custom_call", output_to_operand_aliasing={{2}: (1, {})} | custom-call | flops 6442450944 | bytes 16777216 | tf_op jit(solution)/shard_map/wgrad/pallas_call | solution.py:304
  122.0 4.5 %wgrad.5 = (bf16[1,272,2048]{2,1,0:T(8,128)(2,1)S(1)}, s32[2]{0:T(128)S(1)}, bf16[2048,2048]{1,0:T(8,128)(2,1)}) custom-call(s32[2]{0:T(128)S(1)} %get-tuple-element.118.ctl, bf16[2048,2048]{1,0:T(8,128)(2,1)} %get-tuple-element.119.agg, bf16[2048,2048]{1,0:T(8,128)(2,1)S(1)} %get-tuple-element.110.grad, ...), custom_call_target="tpu_custom_call", output_to_operand_aliasing={{2}: (1, {})} | custom-call | flops 2147483648 | bytes 16777216 | tf_op jit(solution)/shard_map/wgrad/pallas_call | solution.py:304
  126.5 19.7 %agg_grad.1 = (bf16[2048,2048]{1,0:T(8,128)(2,1)S(1)}, s32[2]{0:T(128)S(1)}) custom-call(s32[2]{0:T(128)S(1)} %get-tuple-element.120.ctl, s32[1,2048]{1,0:T(1,128)S(1)} %bitcast.62, bf16[2048,2048]{1,0:T(8,128)(2,1)S(1)} %get-tuple-element.110.grad, bf16[2048,2048]{1,0:T(8,128)(2,1)S(1)} %get-tuple-element.104.weight), custom_call_target="tpu_custom_call" | custom-call | flops 17179869184 | bytes 25165824 | tf_op jit(solution)/shard_map/agg_grad/pallas_call | solution.py:333
  149.0 1.6 collective-permute-start.14
  151.1 6.2 %nodes_grad.3 = (bf16[2048,2048]{1,0:T(8,128)(2,1)}, s32[2]{0:T(128)S(1)}) custom-call(s32[2]{0:T(128)S(1)} %get-tuple-element.121.ctl, bf16[2048,2048]{1,0:T(8,128)(2,1)S(1)} %bitcast.56, bf16[2048,2048]{1,0:T(8,128)(2,1)S(1)} %get-tuple-element.123.spread, bf16[80,1024]{1,0:T(8,128)(2,1)S(1)} %slice_bitcast_fusion.2.rest_0_, ...), custom_call_target="tpu_custom_call" | custom-call | flops 4294967296 | bytes 12582912 | tf_op jit(solution)/shard_map/nodes_grad/pallas_call | solution.py:354
  157.6 1.7 collective-permute-start.18
  159.2 6.2 %nodes_grad.4 = (bf16[2048,2048]{1,0:T(8,128)(2,1)}, s32[2]{0:T(128)S(1)}) custom-call(s32[2]{0:T(128)S(1)} %get-tuple-element.126.ctl, bf16[2048,2048]{1,0:T(8,128)(2,1)S(1)} %bitcast.56, bf16[2048,2048]{1,0:T(8,128)(2,1)S(1)} %get-tuple-element.123.spread, bf16[2048,2048]{1,0:T(8,128)(2,1)} %get-tuple-element.127.rest_0_, ...), custom_call_target="tpu_custom_call", output_to_operand_aliasing={{0}: (3, {})} | custom-call | flops 4294967296 | bytes 12582912 | tf_op jit(solution)/shard_map/nodes_grad/pallas_call | solution.py:354
  167.0 10.9 %nodes_grad.5 = (bf16[2048,2048]{1,0:T(8,128)(2,1)}, s32[2]{0:T(128)}) custom-call(s32[2]{0:T(128)S(1)} %get-tuple-element.131.ctl, bf16[2048,2048]{1,0:T(8,128)(2,1)S(1)} %bitcast.56, bf16[2048,2048]{1,0:T(8,128)(2,1)S(1)} %get-tuple-element.123.spread, bf16[2048,2048]{1,0:T(8,128)(2,1)} %get-tuple-element.132.rest_0_, ...), custom_call_target="tpu_custom_call", output_to_operand_aliasing={{0}: (3, {})} | custom-call | flops 8589934592 | bytes 16777216 | tf_op jit(solution)/shard_map/nodes_grad/pallas_call | solution.py:354
  177.9 2.3 %collective-permute-done.20 = bf16[64,2176]{1,0:T(8,128)(2,1)S(1)} collective-permute-done((bf16[64,2176]{1,0:T(8,128)(2,1)S(1)}, bf16[64,2176]{1,0:T(8,128)(2,1)S(1)}, u32[]{:S(2)}, u32[]{:S(2)}) %collective-permute-start.20) | collective-permute-done | bytes 278560 | tf_op jit(solution)/shard_map/ppermute | solution.py:368
  (89 shorter events, 19.1 us)
Async XLA Ops:
  1.6 20.4 %slice-start.2 = ((s8[8388608]{0:T(1024)(128)(4,1)}), s8[4194304]{0:T(1024)(128)(4,1)S(1)}, s32[]{:S(2)}) async-start(s8[8388608]{0:T(1024)(128)(4,1)} %bitcast.57), calls=%async_computation.2 | async-start | bytes 8388608
  2.7 19.2 %collective-permute-start.1 = (bf16[64,2176]{1,0:T(8,128)(2,1)S(1)}, bf16[64,2176]{1,0:T(8,128)(2,1)S(1)}, u32[]{:S(2)}, u32[]{:S(2)}) collective-permute-start(bf16[64,2176]{1,0:T(8,128)(2,1)S(1)} %pad_maximum_fusion.1), channel_id=1, source_target_pairs={{0,1},{1,0},{2,3},{3,2},{4,5},{5,4},{6,7},{7,6},{8,9},{9,8},{10,11... | collective-permute-start | bytes 835592 | tf_op jit(solution)/shard_map/ppermute | solution.py:368
  5.8 15.6 %collective-permute-start = (bf16[64,2176]{1,0:T(8,128)(2,1)S(1)}, bf16[64,2176]{1,0:T(8,128)(2,1)S(1)}, u32[]{:S(2)}, u32[]{:S(2)}) collective-permute-start(bf16[64,2176]{1,0:T(8,128)(2,1)S(1)} %pad_maximum_fusion.1), channel_id=1, source_target_pairs={{0,2},{1,3},{2,0},{3,1},{4,6},{5,7},{6,4},{7,5},{8,10},{9,11},{10,... | collective-permute-start | bytes 835592 | tf_op jit(solution)/shard_map/ppermute | solution.py:368
  21.4 7.9 %collective-permute-start.2 = (bf16[64,2176]{1,0:T(8,128)(2,1)S(1)}, bf16[64,2176]{1,0:T(8,128)(2,1)S(1)}, u32[]{:S(2)}, u32[]{:S(2)}) collective-permute-start(bf16[64,2176]{1,0:T(8,128)(2,1)S(1)} %collective-permute-done), channel_id=1, source_target_pairs={{0,1},{1,0},{2,3},{3,2},{4,5},{5,4},{6,7},{7,6},{8,9},{9,8},{10,11... | collective-permute-start | bytes 835592 | tf_op jit(solution)/shard_map/ppermute | solution.py:368
  29.4 12.7 %collective-permute-start.4 = (bf16[256,1024]{1,0:T(8,128)(2,1)S(1)}, bf16[256,1024]{1,0:T(8,128)(2,1)S(1)}, u32[]{:S(2)}, u32[]{:S(2)}) collective-permute-start(bf16[256,1024]{1,0:T(8,128)(2,1)S(1)} %pad_maximum_fusion), channel_id=1, source_target_pairs={{0,16},{1,17},{2,18},{3,19},{4,20},{5,21},{6,22},{7,23},{8,24},{9,... | collective-permute-start | bytes 1572872 | tf_op jit(solution)/shard_map/ppermute | solution.py:368
  31.0 13.1 %collective-permute-start.3 = (bf16[272,1024]{1,0:T(8,128)(2,1)S(1)}, bf16[272,1024]{1,0:T(8,128)(2,1)S(1)}, u32[]{:S(2)}, u32[]{:S(2)}) collective-permute-start(bf16[272,1024]{1,0:T(8,128)(2,1)S(1)} %get-tuple-element.168), channel_id=1, source_target_pairs={{0,8},{1,9},{2,10},{3,11},{4,12},{5,13},{6,14},{7,15},{8,0},{9,1},... | collective-permute-start | bytes 1671176 | tf_op jit(solution)/shard_map/ppermute | solution.py:368
  44.2 12.2 %collective-permute-start.5 = (bf16[544,1024]{1,0:T(8,128)(2,1)S(1)}, bf16[544,1024]{1,0:T(8,128)(2,1)S(1)}, u32[]{:S(2)}, u32[]{:S(2)}) collective-permute-start(bf16[544,1024]{1,0:T(8,128)(2,1)S(1)} %constant_dynamic-update-slice_fusion.1.refs_0_), channel_id=1, source_target_pairs={{0,4},{1,5},{2,6},{3,7},{4,0},{5,1},{6,2},{7,3},{8,12},{9,13},{10,... | collective-permute-start | bytes 3342344 | tf_op jit(solution)/shard_map/ppermute | solution.py:368
  44.3 12.1 %collective-permute-start.6 = (bf16[512,1024]{1,0:T(8,128)(2,1)S(1)}, bf16[512,1024]{1,0:T(8,128)(2,1)S(1)}, u32[]{:S(2)}, u32[]{:S(2)}) collective-permute-start(bf16[512,1024]{1,0:T(8,128)(2,1)S(1)} %constant_dynamic-update-slice_fusion.3.refs_1_), channel_id=1, source_target_pairs={{0,4},{1,5},{2,6},{3,7},{4,0},{5,1},{6,2},{7,3},{8,12},{9,13},{10,... | collective-permute-start | bytes 3145736 | tf_op jit(solution)/shard_map/ppermute | solution.py:368
  44.9 27.8 %collective-permute-start.8 = (bf16[512,1024]{1,0:T(8,128)(2,1)S(1)}, bf16[512,1024]{1,0:T(8,128)(2,1)S(1)}, u32[]{:S(2)}, u32[]{:S(2)}) collective-permute-start(bf16[512,1024]{1,0:T(8,128)(2,1)S(1)} %constant_dynamic-update-slice_fusion.3.refs_1_), channel_id=1, source_target_pairs={{0,8},{1,9},{2,10},{3,11},{4,12},{5,13},{6,14},{7,15},{8,0},{9,1},... | collective-permute-start | bytes 3145736 | tf_op jit(solution)/shard_map/ppermute | solution.py:368
  46.4 26.3 %collective-permute-start.7 = (bf16[544,1024]{1,0:T(8,128)(2,1)S(1)}, bf16[544,1024]{1,0:T(8,128)(2,1)S(1)}, u32[]{:S(2)}, u32[]{:S(2)}) collective-permute-start(bf16[544,1024]{1,0:T(8,128)(2,1)S(1)} %constant_dynamic-update-slice_fusion.1.refs_0_), channel_id=1, source_target_pairs={{0,16},{1,17},{2,18},{3,19},{4,20},{5,21},{6,22},{7,23},{8,24},{9,... | collective-permute-start | bytes 3342344 | tf_op jit(solution)/shard_map/ppermute | solution.py:368
  72.7 4.3 %collective-permute-start.9 = (bf16[544,1024]{1,0:T(8,128)(2,1)S(1)}, bf16[544,1024]{1,0:T(8,128)(2,1)S(1)}, u32[]{:S(2)}, u32[]{:S(2)}) collective-permute-start(bf16[544,1024]{1,0:T(8,128)(2,1)S(1)} %collective-permute-done.7.refs_0_), channel_id=1, source_target_pairs={{0,4},{1,5},{2,6},{3,7},{4,0},{5,1},{6,2},{7,3},{8,12},{9,13},{10,... | collective-permute-start | bytes 3342344 | tf_op jit(solution)/shard_map/ppermute | solution.py:368
  72.7 4.2 %collective-permute-start.10 = (bf16[512,1024]{1,0:T(8,128)(2,1)S(1)}, bf16[512,1024]{1,0:T(8,128)(2,1)S(1)}, u32[]{:S(2)}, u32[]{:S(2)}) collective-permute-start(bf16[512,1024]{1,0:T(8,128)(2,1)S(1)} %collective-permute-done.8.refs_1_), channel_id=1, source_target_pairs={{0,4},{1,5},{2,6},{3,7},{4,0},{5,1},{6,2},{7,3},{8,12},{9,13},{10,... | collective-permute-start | bytes 3145736 | tf_op jit(solution)/shard_map/ppermute | solution.py:368
  109.7 9.4 %collective-permute-start.11 = (bf16[4,272,2048]{2,1,0:T(8,128)(2,1)S(1)}, bf16[4,272,2048]{2,1,0:T(8,128)(2,1)S(1)}, u32[]{:S(2)}, u32[]{:S(2)}) collective-permute-start(bf16[4,272,2048]{2,1,0:T(8,128)(2,1)S(1)} %get-tuple-element.116), channel_id=1, source_target_pairs={{0,4},{1,5},{2,6},{3,7},{4,0},{5,1},{6,2},{7,3},{8,12},{9,13},{10,... | collective-permute-start | bytes 13369352 | tf_op jit(solution)/shard_map/ppermute | solution.py:368
  120.0 26.2 %collective-permute-start.13 = (bf16[2,256,1024]{2,1,0:T(8,128)(2,1)S(1)}, bf16[2,256,1024]{2,1,0:T(8,128)(2,1)S(1)}, u32[]{:S(2)}, u32[]{:S(2)}) collective-permute-start(bf16[2,256,1024]{2,1,0:T(8,128)(2,1)S(1)} %add_convert_fusion.1), channel_id=1, source_target_pairs={{0,8},{1,9},{2,10},{3,11},{4,12},{5,13},{6,14},{7,15},{8,0},{9,1},... | collective-permute-start | bytes 3145736 | tf_op jit(solution)/shard_map/ppermute | solution.py:368
  120.5 28.1 %collective-permute-start.12 = (bf16[2,272,1024]{2,1,0:T(8,128)(2,1)S(1)}, bf16[2,272,1024]{2,1,0:T(8,128)(2,1)S(1)}, u32[]{:S(2)}, u32[]{:S(2)}) collective-permute-start(bf16[2,272,1024]{2,1,0:T(8,128)(2,1)S(1)} %add_convert_fusion), channel_id=1, source_target_pairs={{0,16},{1,17},{2,18},{3,19},{4,20},{5,21},{6,22},{7,23},{8,24},{9,... | collective-permute-start | bytes 3342344 | tf_op jit(solution)/shard_map/ppermute | solution.py:368
  126.5 24.7 %slice-start = ((s8[8388608]{0:T(1024)(128)(4,1)}), s8[4194304]{0:T(1024)(128)(4,1)S(1)}, s32[]{:S(2)}) async-start(s8[8388608]{0:T(1024)(128)(4,1)} %bitcast.55), calls=%async_computation | async-start | bytes 8388608
  126.5 24.6 %slice-start.1 = ((s8[8388608]{0:T(1024)(128)(4,1)}), s8[4194304]{0:T(1024)(128)(4,1)S(1)}, s32[]{:S(2)}) async-start(s8[8388608]{0:T(1024)(128)(4,1)} %bitcast.55), calls=%async_computation.1 | async-start | bytes 8388608
  146.5 10.9 %collective-permute-start.15 = (bf16[64,1024]{1,0:T(8,128)(2,1)S(1)}, bf16[64,1024]{1,0:T(8,128)(2,1)S(1)}, u32[]{:S(2)}, u32[]{:S(2)}) collective-permute-start(bf16[64,1024]{1,0:T(8,128)(2,1)S(1)} %slice_bitcast_fusion.3.rest_1_), channel_id=1, source_target_pairs={{0,16},{1,17},{2,18},{3,19},{4,20},{5,21},{6,22},{7,23},{8,24},{9,... | collective-permute-start | bytes 393224 | tf_op jit(solution)/shard_map/ppermute | solution.py:368
  147.3 18.1 %collective-permute-start.17 = (bf16[192,1024]{1,0:T(8,128)(2,1)S(1)}, bf16[192,1024]{1,0:T(8,128)(2,1)S(1)}, u32[]{:S(2)}, u32[]{:S(2)}) collective-permute-start(bf16[192,1024]{1,0:T(8,128)(2,1)S(1)} %slice_bitcast_fusion.rest_3_), channel_id=1, source_target_pairs={{0,16},{1,17},{2,18},{3,19},{4,20},{5,21},{6,22},{7,23},{8,24},{9,... | collective-permute-start | bytes 1179656 | tf_op jit(solution)/shard_map/ppermute | solution.py:368
  149.0 8.3 %collective-permute-start.14 = (bf16[80,1024]{1,0:T(8,128)(2,1)S(1)}, bf16[80,1024]{1,0:T(8,128)(2,1)S(1)}, u32[]{:S(2)}, u32[]{:S(2)}) collective-permute-start(bf16[80,1024]{1,0:T(8,128)(2,1)S(1)} %slice_bitcast_fusion.2.rest_0_), channel_id=1, source_target_pairs={{0,8},{1,9},{2,10},{3,11},{4,12},{5,13},{6,14},{7,15},{8,0},{9,1},... | collective-permute-start | bytes 491528 | tf_op jit(solution)/shard_map/ppermute | solution.py:368
  150.6 15.1 %collective-permute-start.16 = (bf16[192,1024]{1,0:T(8,128)(2,1)S(1)}, bf16[192,1024]{1,0:T(8,128)(2,1)S(1)}, u32[]{:S(2)}, u32[]{:S(2)}) collective-permute-start(bf16[192,1024]{1,0:T(8,128)(2,1)S(1)} %slice_bitcast_fusion.1.rest_2_), channel_id=1, source_target_pairs={{0,8},{1,9},{2,10},{3,11},{4,12},{5,13},{6,14},{7,15},{8,0},{9,1},... | collective-permute-start | bytes 1179656 | tf_op jit(solution)/shard_map/ppermute | solution.py:368
  157.6 8.9 %collective-permute-start.18 = (bf16[64,2176]{1,0:T(8,128)(2,1)S(1)}, bf16[64,2176]{1,0:T(8,128)(2,1)S(1)}, u32[]{:S(2)}, u32[]{:S(2)}) collective-permute-start(bf16[64,2176]{1,0:T(8,128)(2,1)S(1)} %fusion.5.rest_1_), channel_id=1, source_target_pairs={{0,1},{1,0},{2,3},{3,2},{4,5},{5,4},{6,7},{7,6},{8,9},{9,8},{10,11... | collective-permute-start | bytes 835592 | tf_op jit(solution)/shard_map/ppermute | solution.py:368
  166.0 11.9 %collective-permute-start.19 = (bf16[64,2176]{1,0:T(8,128)(2,1)S(1)}, bf16[64,2176]{1,0:T(8,128)(2,1)S(1)}, u32[]{:S(2)}, u32[]{:S(2)}) collective-permute-start(bf16[64,2176]{1,0:T(8,128)(2,1)S(1)} %fusion.6.rest_2_), channel_id=1, source_target_pairs={{0,1},{1,0},{2,3},{3,2},{4,5},{5,4},{6,7},{7,6},{8,9},{9,8},{10,11... | collective-permute-start | bytes 835592 | tf_op jit(solution)/shard_map/ppermute | solution.py:368
  166.5 13.7 %collective-permute-start.20 = (bf16[64,2176]{1,0:T(8,128)(2,1)S(1)}, bf16[64,2176]{1,0:T(8,128)(2,1)S(1)}, u32[]{:S(2)}, u32[]{:S(2)}) collective-permute-start(bf16[64,2176]{1,0:T(8,128)(2,1)S(1)} %fusion.1.rest_1_), channel_id=1, source_target_pairs={{0,2},{1,3},{2,0},{3,1},{4,6},{5,7},{6,4},{7,5},{8,10},{9,11},{10,... | collective-permute-start | bytes 835592 | tf_op jit(solution)/shard_map/ppermute | solution.py:368
  (5 other events, 42.8 us)
